TPU v7x, 256 devices: a whole 4x4x8 slice. The times are simulated.
256 devices in a mesh: dp: 16 (over x_hi, z), seq: 16 (over y, x_lo, core).
Axes of the slice: x: 4 (x_hi: 2, x_lo: 2; x = x_hi * 2 + x_lo), y: 4, z: 8, core: 2. Of those that a mesh axis runs over, the one named last changes fastest.
Arguments:
- inputs: bfloat16 [16, 2048, 1536], P('dp', 'seq'), may hold values from -6 to 6
- dilations: int32 [2], replicated, may hold values from 1 to 16, as said below
- taps: float32 [2, 3, 1536], replicated, may hold values from -3 to 3
- gains: float32 [3, 1536], replicated, may hold values from 0.5 to 1.5
- bias_table: float32 [64, 4], replicated
- buckets: int32 [4095], replicated, may hold values from 0 to 63, as said below
- w_query: bfloat16 [1536, 256], replicated, may hold values from -0.15625 to 0.15625
- w_key: bfloat16 [1536, 256], replicated, may hold values from -0.15625 to 0.15625
- w_value: bfloat16 [1536, 768], replicated, may hold values from -0.15625 to 0.15625
- w_out: bfloat16 [768, 1536], replicated, may hold values from -0.875 to 0.875
- cotangent: bfloat16 [16, 2048, 1536], P('dp', 'seq'), may hold values from -6 to 6
Outputs:
- result: bfloat16 [16, 2048, 1536], P('dp', 'seq')
- input_grad: bfloat16 [16, 2048, 1536], P('dp', 'seq')
- weight_grads: float32 [1536, 2048], P(('dp', 'seq'))
Inputs may be any that keep to these rules, and one draw needn't show every extreme that they name: `dilations`: some block has dilation exactly 16. `buckets`: entry i - j + 2047 holds the bucket of query bin i and key bin j.
All inputs are finite; a program needn't handle non-finite values.
Results may differ from a plain program's by a relative error of at most 0.015.
Values may be sent and summed in bfloat16 or wider, within the bound.
No kernel may reach another device: no remote copies, remote signals or barrier semaphores. Data moves between devices by JAX's collectives and lax.ppermute only.
A program may use at most 128 MiB of HBM per device.

v0:
```python
import functools

import jax
import jax.numpy as jnp
import numpy as np
from jax import lax
from jax.experimental import pallas as pl
from jax.experimental.pallas import tpu as pltpu
from jax.sharding import Mesh, PartitionSpec as P

HEADS = 4
KEY = 64
VALUE = 192
WIDE = KEY + VALUE
BLOCKS = 2
DMAX = 16
HALO = BLOCKS * DMAX
EPS = 1e-06
STEP = 16
LARGE = 60
SEQ = ("y", "xl", "core")
EVERY = ("xh", "z", "y", "xl", "core")
F32 = jnp.float32
BF16 = jnp.bfloat16
ROOT_HALF = 0.7071067811865476
ROOT_TWO_PI = 0.3989422804014327


def contract(left, right, left_dim, right_dim):
    return lax.dot_general(
        left, right, (((left_dim,), (right_dim,)), ((), ())), preferred_element_type=F32
    )


def call(body, outs, args, scratch=(), smem=(), hbm=(), us=1.0, limit=24):
    spaces = [
        pltpu.SMEM if i in smem else pltpu.HBM if i in hbm else pltpu.VMEM for i in range(len(args))
    ]
    return pl.pallas_call(
        body,
        out_shape=tuple(jax.ShapeDtypeStruct(s, d) for s, d in outs),
        in_specs=[pl.BlockSpec(memory_space=s) for s in spaces],
        out_specs=tuple(pl.BlockSpec(memory_space=pltpu.VMEM) for _ in outs),
        scratch_shapes=list(scratch),
        compiler_params=pltpu.CompilerParams(vmem_limit_bytes=limit << 20),
        cost_estimate=pl.CostEstimate(
            flops=1000, bytes_accessed=int(us * 3.6e6), transcendentals=0
        ),
        name=body.__name__ if hasattr(body, "__name__") else body.func.__name__,
    )(*args)


def inverse_norm(rows):
    return lax.rsqrt(jnp.mean(rows * rows, axis=1, keepdims=True) + EPS)


def activate(rows, gain):
    field = rows * inverse_norm(rows) * gain
    return 0.5 * field * (1.0 + lax.erf(field * ROOT_HALF))


def rounded(rows):
    return rows.astype(BF16).astype(F32)


def loop(count, body):
    def step(i, carry):
        body(pl.multiple_of(i * STEP, STEP))
        return carry

    lax.fori_loop(0, count // STEP, step, 0, unroll=2)


def inside(start, first, last, edge, count):
    out = (first & (start < edge)) | (last & (start >= count - edge))
    return jnp.where(out, 0.0, 1.0)


def move(moved, source, gap):
    count, total = moved.shape[0] // 2, source.shape[0]
    row = lax.broadcasted_iota(jnp.int32, (count, total), 0)
    col = lax.broadcasted_iota(jnp.int32, (count, total), 1)
    held = source[...]
    for i, at in enumerate((DMAX - gap, DMAX + gap)):
        pick = jnp.where(col == row + at, 1.0, 0.0).astype(BF16)
        moved[i * count : (i + 1) * count, :] = contract(pick, held, 1, 0)


def tapped(taps, first, moved, center, r, low=0, high=2):
    count = moved.shape[0] // 2
    return (
        taps[low, first : first + 1, :] * moved[pl.ds(r, STEP), :]
        + taps[1, first : first + 1, :] * center
        + taps[high, first : first + 1, :] * moved[pl.ds(pl.multiple_of(count + r, STEP), STEP), :]
    )


def shuffle(where, order, normed, upstream, f0, f1, f2, f3, slots):
    unit = order.shape[1]
    chan = normed.shape[1]
    row = lax.broadcasted_iota(jnp.int32, (unit, unit), 0)
    pick = jnp.where(row == order[...], 1.0, 0.0).astype(BF16)
    share = unit // 4
    to = 0
    for source in (normed, upstream):
        for low in range(0, chan, unit):
            mixed = contract(source[:, low : low + unit], pick, 1, 0).astype(BF16)
            for y in range(4):
                slots[lax.rem(y - where[0] + 4, 4), :, to : to + share] = mixed[
                    :, y * share : (y + 1) * share
                ]
            to += share
    for i, out in enumerate((f0, f1, f2, f3)):
        out[...] = slots[i]


def fetch(pairs, sems):
    copies = [pltpu.make_async_copy(a, b, sems.at[i]) for i, (a, b) in enumerate(pairs)]
    for copy in copies:
        copy.start()
    return copies


def expand(where, table, buckets, master, line_ref):
    head = where[0]
    count = buckets.shape[1]
    bucket = lax.broadcasted_iota(jnp.int32, (table.shape[1], count), 0)
    line = lax.dot_general(
        table[...],
        jnp.where(buckets[...] == bucket, 1.0, 0.0),
        (((1,), (0,)), ((), ())),
        precision=lax.Precision.HIGHEST,
        preferred_element_type=F32,
    )
    chosen = lax.broadcasted_iota(jnp.int32, line.shape, 0) == head
    line_ref[...] = jnp.zeros(line_ref.shape, F32)
    line_ref[:, :count] = jnp.sum(jnp.where(chosen, line, 0.0), axis=0, keepdims=True)
    line = line_ref[...]
    span = line.shape[1]
    for r in range(0, 128, 8):
        master[r : r + 8, :] = pltpu.roll(
            jnp.broadcast_to(line, (8, span)), (span - 127 + r) % span, 1, stride=1, stride_axis=0
        )


def prelude(
    rows_far, gains, upstream_far, w_out_far,
    act, d_att, rows, upstream, w_out, sems,
):
    copies = fetch(((rows_far, rows), (upstream_far, upstream), (w_out_far, w_out)), sems)
    gain = gains[0:1, :]
    copies[0].wait()

    def body(r):
        act[pl.ds(r, STEP), :] = activate(rows[pl.ds(r, STEP), :].astype(F32), gain).astype(BF16)

    loop(rows.shape[0], body)
    copies[1].wait()
    copies[2].wait()
    d_att[...] = contract(upstream[...], w_out[...], 1, 1).astype(BF16)


def forward(
    where, dil, left, right, rows, act, d_att, taps, gains, wq_far, wk_far, wv_far,
    m0, m1, m2, m3, normed, z, near,
    x_ext, a_ext, b_ext, slots, moved1, moved2, w_query, w_key, w_value, sems,
):
    copies = fetch(((wq_far, w_query), (wk_far, w_key), (wv_far, w_value)), sems)
    iy, iseq, nseq = where[0], where[1], where[2]
    tok = rows.shape[0]
    x_ext[0:HALO, :] = left[...]
    x_ext[HALO : HALO + tok, :] = rows[...]
    x_ext[HALO + tok :, :] = right[...]
    a_ext[HALO : HALO + tok, :] = act[...]
    gain = gains[0:1, :]
    for r in [*range(0, HALO, STEP), *range(HALO + tok, 2 * HALO + tok, STEP)]:
        a_ext[r : r + STEP, :] = activate(x_ext[r : r + STEP, :].astype(F32), gain).astype(BF16)
    gap, wide = dil[0], dil[1]
    first, last = iseq == 0, iseq == nseq - 1
    count = tok + 2 * DMAX
    gain = gains[1:2, :]
    move(moved1, a_ext, gap)

    def middle(r):
        center = pl.ds(pl.multiple_of(r + DMAX, STEP), STEP)
        mixed = tapped(taps, 0, moved1, a_ext[center, :].astype(F32), r)
        hidden = (x_ext[center, :].astype(F32) + mixed).astype(BF16)
        near[pl.ds(r, STEP), :] = hidden
        keep = inside(r, first, last, DMAX, count)
        b_ext[pl.ds(r, STEP), :] = (activate(hidden.astype(F32), gain) * keep).astype(BF16)

    loop(count, middle)
    last_gain = gains[2:3, :]
    move(moved2, b_ext, wide)

    def top(r):
        center = pl.ds(pl.multiple_of(r + DMAX, STEP), STEP)
        mixed = tapped(taps, 1, moved2, b_ext[center, :].astype(F32), r)
        hidden = (near[center, :].astype(F32) + mixed).astype(BF16)
        z[pl.ds(r, STEP), :] = hidden
        hidden = hidden.astype(F32)
        normed[pl.ds(r, STEP), :] = (hidden * inverse_norm(hidden) * last_gain).astype(BF16)

    loop(tok, top)
    field = normed[...]
    for copy in copies:
        copy.wait()
    queries = (rounded(contract(field, w_query[...], 1, 0)) * KEY**-0.5).astype(BF16)
    keys = contract(field, w_key[...], 1, 0).astype(BF16)
    values = contract(field, w_value[...], 1, 0).astype(BF16)
    for h in range(HEADS):
        k, v = slice(h * KEY, (h + 1) * KEY), slice(h * VALUE, (h + 1) * VALUE)
        slots[lax.rem(h - iy + HEADS, HEADS)] = jnp.concatenate(
            [keys[:, k], values[:, v], queries[:, k], d_att[:, v]], axis=1
        )
    for i, out in enumerate((m0, m1, m2, m3)):
        out[...] = slots[i]


def slopes(rows, near, gains, slope0, slope1):
    def fill(source, gain, out):
        def body(r):
            held = source[pl.ds(r, STEP), :].astype(F32)
            field = held * inverse_norm(held) * gain
            below = 0.5 * (1.0 + lax.erf(field * ROOT_HALF))
            out[pl.ds(r, STEP), :] = (
                below + field * (ROOT_TWO_PI * jnp.exp(-0.5 * field * field))
            ) * gain

        loop(source.shape[0], body)

    fill(near, gains[1:2, :], slope1)
    fill(rows, gains[0:1, :], slope0)


def attend(
    where, m0, m1, m2, m3, kv1, kv2, kv3, master,
    t, own, far, give, ask, kv0, score, pull, soft, d_soft,
):
    iy, c = where[0], where[3]
    tok = m0.shape[0]
    many = HEADS * tok
    for i, m in enumerate((m0, m1, m2, m3)):
        kv0[i * tok : (i + 1) * tok, :] = m[:, :WIDE]
        ask[i * tok : (i + 1) * tok, :] = m[:, WIDE:]
    both = ask[...]
    lane = lax.broadcasted_iota(jnp.int32, (1, WIDE), 1)
    is_key = lane < KEY
    zero = jnp.zeros_like(both)
    queries = jnp.where(is_key, both, zero)
    d_att = jnp.where(is_key, zero, both)
    blocks = (kv0, kv1, kv2, kv3)
    bands = [lax.rem(iy - i + HEADS, HEADS) for i in range(HEADS)]
    top = None
    for j, block in enumerate(blocks):
        other = jnp.bitwise_xor(c, j)
        for i in range(HEADS):
            at = j * many + i * tok
            part = contract(block[i * tok : (i + 1) * tok, :], queries, 1, 1)
            bias = jnp.concatenate(
                [
                    master[:, pl.ds(pl.multiple_of((4 * (q - bands[i]) + c - other + 15) * tok, tok), tok)]
                    for q in bands
                ],
                axis=1,
            )
            part = part + bias
            score[at : at + tok, :] = part
            peak = jnp.max(part, axis=0, keepdims=True)
            top = peak if top is None else jnp.maximum(top, peak)
    total = jnp.zeros_like(top)
    for at in range(0, 4 * many, tok):
        part = jnp.exp(score[at : at + tok, :] - top)
        score[at : at + tok, :] = part
        total = total + jnp.sum(part, axis=0, keepdims=True)
    scale = 1.0 / total
    delta = jnp.zeros_like(top)
    for j, block in enumerate(blocks):
        for i in range(HEADS):
            at = j * many + i * tok
            probs = score[at : at + tok, :] * scale
            score[at : at + tok, :] = probs
            soft[at : at + tok, :] = probs.astype(BF16)
            part = contract(block[i * tok : (i + 1) * tok, :], d_att, 1, 1)
            pull[at : at + tok, :] = part
            delta = delta + jnp.sum(part * probs, axis=0, keepdims=True)
    for at in range(0, 4 * many, tok):
        d_soft[at : at + tok, :] = (
            score[at : at + tok, :] * (pull[at : at + tok, :] - delta)
        ).astype(BF16)
    att = jnp.zeros((WIDE, many), F32)
    d_query = jnp.zeros((WIDE, many), F32)
    for j, block in enumerate(blocks):
        held = block[...]
        span = slice(j * many, (j + 1) * many)
        att = att + contract(held, soft[span, :], 0, 0)
        d_query = d_query + contract(held, d_soft[span, :], 0, 0)
        d_kv = jnp.where(
            is_key, contract(d_soft[span, :], both, 1, 0), contract(soft[span, :], both, 1, 0)
        )
        if j == 0:
            own[...] = d_kv
        elif j == 2:
            far[...] = d_kv
        else:
            give[(j // 2) * many : (j // 2 + 1) * many, :] = d_kv.astype(BF16)
    side = lax.broadcasted_iota(jnp.int32, (WIDE, 1), 0) < KEY
    mixed = jnp.where(side, d_query * KEY**-0.5, att).T.astype(BF16)
    for i, band in enumerate(bands):
        t[pl.ds(pl.multiple_of(band * tok, tok), tok), :] = mixed[i * tok : (i + 1) * tok, :]


def first_sum(own, far, got, near, send):
    many = own.shape[0]
    near[...] = own[...] + got[:many, :].astype(F32)
    send[...] = (far[...] + got[many:, :].astype(F32)).astype(BF16)


def second_sum(where, near, got, total):
    held = (near[...] + got[...].astype(F32)).astype(BF16)
    tok = held.shape[0] // HEADS
    for i in range(HEADS):
        band = lax.rem(where[0] - i + HEADS, HEADS)
        total[pl.ds(pl.multiple_of(band * tok, tok), tok), :] = held[i * tok : (i + 1) * tok, :]


def joined(parts, whole):
    half = parts[2].shape[0]
    whole[:half, :] = parts[2][...]
    whole[half:, :] = parts[3][...]
    return parts[0], parts[1], whole, parts[4]


def gathered(slots, parts, whole, iy):
    tok = slots.shape[1]
    for i, part in enumerate(joined(parts, whole)):
        held = part[pl.ds(pl.multiple_of(iy * tok, tok), tok), :]
        slots[lax.rem(iy - i + HEADS, HEADS)] = held


def heads_of(slots, low, high):
    return jnp.concatenate([slots[h][:, low:high] for h in range(HEADS)], axis=1)


def project(where, t0, t1, t2, t3, t4, z, w_out, w_query, result, g_query, slots, whole):
    gathered(slots, (t0, t1, t2, t3, t4), whole, where[0])
    att = heads_of(slots, KEY, WIDE)
    result[...] = (z[...].astype(F32) + contract(att, w_out[...], 1, 0)).astype(BF16)
    g_query[...] = contract(heads_of(slots, 0, KEY), w_query[...], 1, 1)


def pull_norm(held, scaled):
    s = inverse_norm(held)
    return s * scaled - held * (s * s * s) * jnp.mean(scaled * held, axis=1, keepdims=True)


def grad_top(
    where, d0, d1, d2, d3, d4, g_query, z, upstream, w_key, w_value, gains, out, slots, total, whole
):
    gathered(slots, (d0, d1, d2, d3, d4), whole, where[0])
    total[...] = (
        g_query[...]
        + contract(heads_of(slots, 0, KEY), w_key[...], 1, 1)
        + contract(heads_of(slots, KEY, WIDE), w_value[...], 1, 1)
    )
    gain = gains[2:3, :]

    def body(r):
        at = pl.ds(r, STEP)
        grad = pull_norm(z[at, :].astype(F32), total[at, :] * gain)
        out[at, :] = (upstream[at, :].astype(F32) + grad).astype(BF16)

    loop(z.shape[0], body)


def backward(
    where, dil, left, right, grad, slope0, slope1, rows, near, taps, out, g_ext, p_ext, moved1, moved2
):
    iseq, nseq = where[1], where[2]
    tok = rows.shape[0]
    first, last = iseq == 0, iseq == nseq - 1
    g_ext[0:HALO, :] = left[...]
    g_ext[HALO : HALO + tok, :] = grad[...]
    g_ext[HALO + tok :, :] = right[...]
    gap, wide = dil[0], dil[1]
    count = tok + 2 * DMAX

    move(moved1, g_ext, wide)

    def middle(r):
        center = g_ext[pl.ds(pl.multiple_of(r + DMAX, STEP), STEP), :].astype(F32)
        mixed = tapped(taps, 1, moved1, center, r, 2, 0)
        at = pl.ds(r, STEP)
        held = pull_norm(near[at, :].astype(F32), mixed * slope1[at, :])
        keep = inside(r, first, last, DMAX, count)
        p_ext[at, :] = ((center + held) * keep).astype(BF16)

    loop(count, middle)
    move(moved2, p_ext, gap)

    def bottom(r):
        center = p_ext[pl.ds(pl.multiple_of(r + DMAX, STEP), STEP), :].astype(F32)
        mixed = tapped(taps, 0, moved2, center, r, 2, 0)
        at = pl.ds(r, STEP)
        held = pull_norm(rows[at, :].astype(F32), mixed * slope0[at, :])
        out[at, :] = (center + held).astype(BF16)

    loop(tok, bottom)


def placed(out, cuts, head, held):
    nxh, nz0, size = cuts
    at = 0
    for xh in range(nxh):
        for core in range(2):
            for xl in range(2):
                for z0 in range(nz0):
                    to = ((xl * nxh + xh) * nz0 + z0) * size
                    out[core, head, to : to + size, :] = held[at : at + size, :]
                    at += size


def naturally(parts, out, low, iy):
    tok, width = parts[0].shape[0], out.shape[1]
    for i, part in enumerate(parts):
        band = lax.rem(iy - i + HEADS, HEADS)
        out[pl.ds(pl.multiple_of(band * tok, tok), tok), :] = part[:, low : low + width]


def weigh_first(cuts, where, f0, f1, f2, f3, t0, t1, t2, t3, t4, out, n_all, u_all, whole):
    iy = where[0]
    parts = (f0, f1, f2, f3)
    naturally(parts, n_all, 0, iy)
    naturally(parts, u_all, n_all.shape[1], iy)
    is_key = lax.broadcasted_iota(jnp.int32, (1, WIDE), 1) < KEY
    for i, t in enumerate(joined((t0, t1, t2, t3, t4), whole)):
        held = t[...]
        first = jnp.where(
            is_key, contract(n_all[...], held, 0, 0), contract(u_all[...], held, 0, 0)
        )
        placed(out, cuts, lax.rem(iy - i + HEADS, HEADS), first)


def weigh_second(
    cuts, where, f0, f1, f2, f3, d0, d1, d2, d3, d4, before, keep, give, n_all, out, whole
):
    iy, core = where[0], where[4]
    naturally((f0, f1, f2, f3), n_all, 0, iy)
    for i, d in enumerate(joined((d0, d1, d2, d3, d4), whole)):
        placed(out, cuts, lax.rem(iy - i + HEADS, HEADS), contract(n_all[...], d[...], 0, 0))
    keep[:, :, :WIDE] = before[core]
    keep[:, :, WIDE:] = out[core]
    give[:, :, :WIDE] = before[1 - core].astype(BF16)
    give[:, :, WIDE:] = out[1 - core].astype(BF16)


def fold(count, part_of, where, keep, *refs):
    got, outs, held = refs[:count], refs[count:-1], refs[-1]
    total = keep[...]
    for g in got:
        total = total + g[...].astype(F32)
    held[...] = total
    size = outs[0].shape[1]
    for i, out in enumerate(outs):
        at = part_of(where, i)
        out[...] = held[:, pl.ds(pl.multiple_of(at * size, 8), size), :].astype(out.dtype)


def fold_call(keep, got, where, part_of, count):
    heads, rows, width = keep.shape
    shape = (heads, rows // count, width)
    return call(
        functools.partial(fold, len(got), part_of),
        [(shape, F32)] + [(shape, BF16)] * (count - 1),
        (where, keep, *got),
        [pltpu.VMEM(keep.shape, F32)],
        smem=(0,),
        us=0.7,
    )


def last_fold(where, keep, got, *refs):
    outs, slots = refs[:-1], refs[-1]
    count = len(outs)
    total = keep[...] + got[...].astype(F32)
    size = total.shape[1] // count
    for i in range(count):
        slots[i] = total[:, i * size : (i + 1) * size, :]
    for i, out in enumerate(outs):
        out[...] = slots[lax.rem(where[9] + i, count)]


def arrange(where, *refs):
    held, out = refs[0][...], refs[-1]
    for g in refs[1:-1]:
        held = held + g[...]
    held = held * (1.0 / where[5].astype(F32))
    keys = HEADS * KEY
    for h in range(HEADS):
        part = held[h]
        out[:, h * KEY : (h + 1) * KEY] = part[:, :KEY]
        low = 2 * keys + HEADS * VALUE + h * VALUE
        out[:, low : low + VALUE] = part[:, KEY:WIDE]
        out[:, keys + h * KEY : keys + (h + 1) * KEY] = part[:, WIDE : WIDE + KEY]
        low = 2 * keys + h * VALUE
        out[:, low : low + VALUE] = part[:, WIDE + KEY :]


def column_order(nz0, nzh, size):
    y, core, xl, z0, zh, j = np.meshgrid(
        *(np.arange(n) for n in (4, 2, 2, nz0, nzh, size)), indexing="ij"
    )
    column = ((((zh * nz0 + z0) * 4 + y) * 2 + xl) * 2 + core) * size + j
    return column.reshape(1, -1).astype(np.int32)


def shift(array, axis, count, step):
    return lax.ppermute(array, axis, [(i, (i + step) % count) for i in range(count)])


def ring(array, axis, count):
    half = array.shape[0] // 2
    before, after = shift(array, axis, count, 1), shift(array, axis, count, -1)
    low = shift(before[:half], axis, count, 1)
    high = shift(after[half:], axis, count, -1)
    return [array, before, low, high, after]


def flip(array, axis):
    return lax.ppermute(array, axis, [(0, 1), (1, 0)])


def halo(rows, nseq):
    width = HALO
    left = lax.ppermute(rows[-width:], SEQ, [(i, i + 1) for i in range(nseq - 1)])
    right = lax.ppermute(rows[:width], SEQ, [(i + 1, i) for i in range(nseq - 1)])
    return left, right


def local(
    sizes, inputs, dilations, taps, gains, bias_table, buckets, w_query, w_key, w_value, w_out, cotangent
):
    nxh, nz, ny = sizes
    nz0 = 2 if nz % 2 == 0 else 1
    nzh = nz // nz0
    nseq = ny * 4
    rows, upstream = inputs[0], cotangent[0]
    tok, chan = rows.shape
    iy, ixl, icore = lax.axis_index("y"), lax.axis_index("xl"), lax.axis_index("core")
    ixh, iz = lax.axis_index("xh"), lax.axis_index("z")
    c = ixl * 2 + icore
    loci = inputs.shape[0] * nxh * nz
    where = jnp.stack(
        [iy, iy * 4 + c, jnp.int32(nseq), c, icore, jnp.int32(loci), ixl, ixh, iz % nz0, iz // nz0]
    ).astype(jnp.int32)
    taps = taps.transpose(1, 0, 2)
    big = (tok, chan)

    left, right = halo(rows, nseq)
    share = chan // (nxh * nz * nseq)
    order = jnp.asarray(column_order(nz0, nzh, share))
    act, d_att = call(
        prelude,
        [(big, BF16), ((tok, HEADS * VALUE), BF16)],
        (rows, gains, upstream, w_out),
        [pltpu.VMEM(big, BF16), pltpu.VMEM(big, BF16), pltpu.VMEM(w_out.shape, BF16),
         pltpu.SemaphoreType.DMA((3,))],
        hbm=(0, 2, 3),
        us=3.0,
        limit=LARGE,
    )
    ext = (tok + 2 * HALO, chan)
    mid = (tok + 2 * DMAX, chan)
    shifted = [pltpu.VMEM((2 * mid[0], chan), F32), pltpu.VMEM((2 * tok, chan), F32)]
    *ms, normed, z, near = call(
        forward,
        [((tok, 2 * WIDE), BF16)] * 4 + [(big, BF16), (big, BF16), (mid, BF16)],
        (where, dilations, left, right, rows, act, d_att, taps, gains, w_query, w_key, w_value),
        [pltpu.VMEM(ext, BF16), pltpu.VMEM(ext, BF16), pltpu.VMEM(mid, BF16),
         pltpu.VMEM((HEADS, tok, 2 * WIDE), BF16), *shifted,
         *(pltpu.VMEM(w.shape, BF16) for w in (w_query, w_key, w_value)), pltpu.SemaphoreType.DMA((3,))],
        smem=(0, 1),
        hbm=(9, 10, 11),
        us=5.0,
        limit=LARGE,
    )
    ms = [ms[0]] + [shift(ms[k], "y", ny, k) for k in (1, 2, 3)]
    unit = order.shape[1]
    fs = call(
        shuffle,
        [((tok, 2 * nxh * unit // 4), BF16)] * 4,
        (where, order, normed, upstream),
        [pltpu.VMEM((4, tok, 2 * nxh * unit // 4), BF16)],
        smem=(0,),
        us=1.6,
    )
    ms, fs, table = lax.optimization_barrier((ms, fs, bias_table.T))
    size = buckets.shape[0]
    (master,) = call(
        expand,
        [((128, size + 1), F32)],
        (where, table, buckets[None]),
        [pltpu.VMEM((1, size + 1), F32)],
        smem=(0,),
        us=1.5,
    )
    kv0 = jnp.concatenate([m[:, :WIDE] for m in ms], axis=0)
    kv2 = flip(kv0, "xl")
    kv1 = flip(kv0, "core")
    fs = [fs[0]] + [shift(fs[k], "y", ny, k) for k in (1, 2, 3)]
    kv2, fs[1], fs[3], master = lax.optimization_barrier((kv2, fs[1], fs[3], master))
    kv3 = flip(kv2, "core")
    many = HEADS * tok
    t, own, far, give = call(
        attend,
        [((many, WIDE), BF16)] + [((many, WIDE), F32)] * 2 + [((2 * many, WIDE), BF16)],
        (where, *ms, kv1, kv2, kv3, master),
        [pltpu.VMEM((many, WIDE), BF16), pltpu.VMEM((many, WIDE), BF16),
         pltpu.VMEM((4 * many, many), F32), pltpu.VMEM((4 * many, many), F32),
         pltpu.VMEM((4 * many, many), BF16), pltpu.VMEM((4 * many, many), BF16)],
        smem=(0,),
        us=7.0,
        limit=24,
    )
    give, fs = lax.optimization_barrier((give, fs))
    got = flip(give, "core")
    own, far = call(
        first_sum, [((many, WIDE), F32), ((many, WIDE), BF16)], (own, far, got), us=0.5
    )
    far, t = lax.optimization_barrier((far, t))
    got = flip(far, "xl")
    ts = ring(t, "y", ny)
    (d,) = call(second_sum, [((many, WIDE), BF16)], (where, own, got), smem=(0,), us=0.5)
    d, near, held = lax.optimization_barrier((d, near, rows))
    ds = ring(d, "y", ny)
    fields = ((many, nxh * unit // 4), BF16)
    cuts = (nxh, nz0, nzh * share)
    half = nxh * nz * 2 * share
    whole = pltpu.VMEM((many, WIDE), BF16)
    (before,) = call(
        functools.partial(weigh_first, cuts),
        [((2, HEADS, half, WIDE), F32)],
        (where, *fs, *ts),
        [pltpu.VMEM(*fields), pltpu.VMEM(*fields), whole],
        smem=(0,),
        us=2.0,
    )
    result, g_query = call(
        project,
        [(big, BF16), (big, F32)],
        (where, *ts, z, w_out, w_query),
        [pltpu.VMEM((HEADS, tok, WIDE), BF16), whole],
        smem=(0,),
        us=2.0,
    )
    slope0, slope1 = call(slopes, [(big, F32), (mid, F32)], (held, near, gains), us=2.6)
    ds, before, result, g_query, slope0, slope1 = lax.optimization_barrier(
        (ds, before, result, g_query, slope0, slope1)
    )
    keep, give = call(
        functools.partial(weigh_second, cuts),
        [((HEADS, half, 2 * WIDE), F32), ((HEADS, half, 2 * WIDE), BF16)],
        (where, *fs, *ds, before),
        [pltpu.VMEM(*fields), pltpu.VMEM((2, HEADS, half, WIDE), F32), whole],
        smem=(0,),
        us=1.5,
    )
    got = flip(give, "core")
    (grad,) = call(
        grad_top,
        [(big, BF16)],
        (where, *ds, g_query, z, upstream, w_key, w_value, gains),
        [pltpu.VMEM((HEADS, tok, WIDE), BF16), pltpu.VMEM(big, F32), whole],
        smem=(0,),
        us=3.0,
    )
    left, right = halo(grad, nseq)

    pairs = [(a, b) for b in range(nxh) for a in range(2)]

    def ring_part(where, i):
        a, b = pairs[i]
        return jnp.bitwise_xor(where[6], a) * nxh + jnp.bitwise_xor(where[7], b)

    keep, *sends = fold_call(keep, [got], where, ring_part, len(pairs))
    got = []
    for (a, b), send in zip(pairs[1:], sends):
        way = [(s, ((s // 2) ^ b) * 2 + ((s % 2) ^ a)) for s in range(2 * nxh)]
        got.append(lax.ppermute(send, ("xh", "xl"), way))
    left, right, got = lax.optimization_barrier((left, right, got))
    if nz0 == 2:
        keep, send = fold_call(
            keep, got, where, lambda where, i: jnp.bitwise_xor(where[8], i), 2
        )
        got = [lax.ppermute(send, "z", [(s, s ^ 1) for s in range(nz)])]
    (input_grad,) = call(
        backward,
        [(big, BF16)],
        (where, dilations, left, right, grad, slope0, slope1, rows, near, taps),
        [pltpu.VMEM(ext, BF16), pltpu.VMEM(mid, BF16), *shifted],
        smem=(0, 1),
        us=4.6,
    )
    input_grad, got = lax.optimization_barrier((input_grad, got))
    part = ((HEADS, share, 2 * WIDE), F32)
    parts = call(
        last_fold,
        [part] * nzh,
        (where, keep, got[0]),
        [pltpu.VMEM((nzh, *part[0]), F32)],
        smem=(0,),
        us=0.6,
    )
    parts = [parts[0]] + [shift(parts[k], "z", nz, k * nz0) for k in range(1, nzh)]
    (weight_sum,) = call(
        arrange, [((share, 8 * WIDE), F32)], (where, *parts), smem=(0,), us=1.0
    )
    return (result[None], input_grad[None], weight_sum)


def solution(mesh):
    nseq = mesh.shape["seq"]
    ny = nseq // 4
    ndp = mesh.shape["dp"]
    nxh = 2 if ndp % 2 == 0 else 1
    sizes = (nxh, ndp // nxh, ny)
    fine = Mesh(mesh.devices.reshape(*sizes, 2, 2), EVERY)
    cells = P(("xh", "z"), SEQ, None)
    return jax.shard_map(
        functools.partial(local, sizes),
        mesh=fine,
        in_specs=(cells, *(P() for _ in range(9)), cells),
        out_specs=(cells, cells, P(EVERY, None)),
        check_vma=False,
    )
```

profile of v0, /device:TPU:24, one launch (start us, length us, event | category | flops | bytes accessed | tf_op | source)
XLA Modules:
  0.0 121.9 jit_solution(3454156032396720344)
XLA Ops:
  0.6 1.0 slice_bitcast_fusion
  1.6 3.0 %collective-permute-start.1 = (bf16[32,1536]{1,0:T(8,128)(2,1)S(1)}, bf16[32,1536]{1,0:T(8,128)(2,1)S(1)}, u32[]{:S(2)}, u32[]{:S(2)}) collective-permute-start(bf16[32,1536]{1,0:T(8,128)(2,1)S(1)} %get-tuple-element.155), channel_id=1, source_target_pairs={{1,0},{2,1},{3,2},{4,3},{5,4},{6,5},{7,6},{8,7},{9,8},{10,9},{11,1... | collective-permute-start | bytes 294920 | tf_op jit(solution)/shard_map/ppermute | solution.py:536
  4.6 1.9 %collective-permute-start = (bf16[32,1536]{1,0:T(8,128)(2,1)S(1)}, bf16[32,1536]{1,0:T(8,128)(2,1)S(1)}, u32[]{:S(2)}, u32[]{:S(2)}) collective-permute-start(bf16[32,1536]{1,0:T(8,128)(2,1)S(1)} %get-tuple-element.156), channel_id=1, source_target_pairs={{0,1},{1,2},{2,3},{3,4},{4,5},{5,6},{6,7},{7,8},{8,9},{9,10},{10,1... | collective-permute-start | bytes 294920 | tf_op jit(solution)/shard_map/ppermute | solution.py:535
  6.5 4.2 %prelude.1 = (bf16[128,1536]{1,0:T(8,128)(2,1)}, bf16[128,768]{1,0:T(8,128)(2,1)}) custom-call(bf16[128,1536]{1,0:T(8,128)(2,1)} %bitcast.19, f32[3,1536]{1,0:T(4,128)} %gains.7, bf16[128,1536]{1,0:T(8,128)(2,1)} %bitcast.23, bf16[768,1536]{1,0:T(8,128)(2,1)} %w_out.1), custom_call_target="tpu_custom_call" | custom-call | flops 1000 | bytes 10800000 | tf_op jit(solution)/shard_map/prelude/pallas_call | solution.py:39
  10.8 0.6 stack.35.where
  11.5 0.6 copy-done.17
  12.1 6.0 %forward.1 = (bf16[128,512]{1,0:T(8,128)(2,1)}, bf16[128,512]{1,0:T(8,128)(2,1)}, bf16[128,512]{1,0:T(8,128)(2,1)}, bf16[128,512]{1,0:T(8,128)(2,1)}, bf16[128,1...) custom-call(s32[10]{0:T(128)} %stack.35.where, s32[2]{0:T(128)} %dil.3, ...), custom_call_target="tpu_custom_call" | custom-call | flops 1000 | bytes 18000000 | tf_op jit(solution)/shard_map/forward/pallas_call | solution.py:39
  18.2 1.4 %collective-permute-start.2 = (bf16[128,512]{1,0:T(8,128)(2,1)}, bf16[128,512]{1,0:T(8,128)(2,1)S(1)}, u32[]{:S(2)}, u32[]{:S(2)}) collective-permute-start(bf16[128,512]{1,0:T(8,128)(2,1)} %get-tuple-element.81), channel_id=1, source_target_pairs={{0,4},{4,8},{8,12},{12,0},{1,5},{5,9},{9,13},{13,1},{2,6},{6,10},{... | collective-permute-start | bytes 393224 | tf_op jit(solution)/shard_map/ppermute | solution.py:518
  19.6 1.2 collective-permute-start.3
  20.8 1.0 copy-done.9
  21.8 1.6 %shuffle.1 = (bf16[128,768]{1,0:T(8,128)(2,1)S(1)}, bf16[128,768]{1,0:T(8,128)(2,1)S(1)}, bf16[128,768]{1,0:T(8,128)(2,1)S(1)}, bf16[128,768]{1,0:T(8,128)(2,1)S(1)}) custom-call(s32[10]{0:T(128)S(1)} %copy-done.12, s32[1,768]{1,0:T(1,128)S(1)} %copy-done.14, bf16[128,1536]{1,0:T(8,128)(2,1)S(1)} %copy-done.9, bf16[128,1536]{1,0:T(8,128)(2,1)S(1)} %bitcast.24), custom_call_target="tpu_custom_call" | custom-call | flops 1000 | bytes 5760000 | tf_op jit(solution)/shard_map/shuffle/pallas_call | solution.py:39
  23.4 1.4 %collective-permute-done.2.m1 = bf16[128,512]{1,0:T(8,128)(2,1)S(1)} collective-permute-done((bf16[128,512]{1,0:T(8,128)(2,1)}, bf16[128,512]{1,0:T(8,128)(2,1)S(1)}, u32[]{:S(2)}, u32[]{:S(2)}) %collective-permute-start.2) | collective-permute-done | bytes 131104 | tf_op jit(solution)/shard_map/ppermute | solution.py:518
  24.7 2.9 %collective-permute-done.3.m2 = bf16[128,512]{1,0:T(8,128)(2,1)S(1)} collective-permute-done((bf16[128,512]{1,0:T(8,128)(2,1)}, bf16[128,512]{1,0:T(8,128)(2,1)S(1)}, u32[]{:S(2)}, u32[]{:S(2)}) %collective-permute-start.3) | collective-permute-done | bytes 131104 | tf_op jit(solution)/shard_map/ppermute | solution.py:518
  27.7 1.5 %collective-permute-done.4.m3 = bf16[128,512]{1,0:T(8,128)(2,1)S(1)} collective-permute-done((bf16[128,512]{1,0:T(8,128)(2,1)}, bf16[128,512]{1,0:T(8,128)(2,1)S(1)}, u32[]{:S(2)}, u32[]{:S(2)}) %collective-permute-start.4) | collective-permute-done | bytes 131104 | tf_op jit(solution)/shard_map/ppermute | solution.py:518
  29.2 0.8 slice.46
  30.1 0.9 collective-permute-start.6
  31.1 1.1 collective-permute-start.7
  32.2 0.9 collective-permute-start.8
  33.1 1.5 %expand.1.master = f32[128,4096]{1,0:T(8,128)S(1)} custom-call(s32[10]{0:T(128)S(1)} %copy-done.12, f32[4,64]{1,0:T(4,128)S(1)} %bitcast.29, s32[1,4095]{1,0:T(1,128)S(1)} %bitcast.28), custom_call_target="tpu_custom_call" | custom-call | flops 1000 | bytes 5400000 | tf_op jit(solution)/shard_map/expand/pallas_call | solution.py:39
  34.6 3.1 %collective-permute-done.7.f1 = bf16[128,768]{1,0:T(8,128)(2,1)S(1)} collective-permute-done((bf16[128,768]{1,0:T(8,128)(2,1)S(1)}, bf16[128,768]{1,0:T(8,128)(2,1)S(1)}, u32[]{:S(2)}, u32[]{:S(2)}) %collective-permute-start.7) | collective-permute-done | bytes 196640 | tf_op jit(solution)/shard_map/ppermute | solution.py:518
  37.7 2.0 %collective-permute-done.8.f3 = bf16[128,768]{1,0:T(8,128)(2,1)S(1)} collective-permute-done((bf16[128,768]{1,0:T(8,128)(2,1)S(1)}, bf16[128,768]{1,0:T(8,128)(2,1)S(1)}, u32[]{:S(2)}, u32[]{:S(2)}) %collective-permute-start.8) | collective-permute-done | bytes 196640 | tf_op jit(solution)/shard_map/ppermute | solution.py:518
  39.7 0.7 collective-permute-start.10
  40.5 0.8 collective-permute-done.9.kv3
  41.3 6.9 %attend.1 = (bf16[512,256]{1,0:T(8,128)(2,1)S(1)}, f32[512,256]{1,0:T(8,128)S(1)}, f32[512,256]{1,0:T(8,128)S(1)}, bf16[1024,256]{1,0:T(8,128)(2,1)S(1)}) custom-call(s32[10]{0:T(128)S(1)} %copy-done.12, bf16[128,512]{1,0:T(8,128)(2,1)S(1)} %copy-done.10, bf16[128,512]{1,0:T(8,128)(2,1)S(1)} %collective-permute-done.2.m1, ...), custom_call_target="tpu_custom_call" | custom-call | flops 1000 | bytes 25200000 | tf_op jit(solution)/shard_map/attend/pallas_call | solution.py:39
  48.2 0.4 collective-permute-done.10.f2
  48.6 1.9 %collective-permute-done.11.got = bf16[1024,256]{1,0:T(8,128)(2,1)S(1)} collective-permute-done((bf16[1024,256]{1,0:T(8,128)(2,1)S(1)}, bf16[1024,256]{1,0:T(8,128)(2,1)S(1)}, u32[]{:S(2)}, u32[]{:S(2)}) %collective-permute-start.11) | collective-permute-done | bytes 524320 | tf_op jit(solution)/shard_map/ppermute | solution.py:530
  50.5 0.1 first_sum.1
  50.6 0.5 collective-permute-start.12
  51.1 0.3 collective-permute-start.19
  51.3 3.0 %collective-permute-start.17 = (bf16[512,256]{1,0:T(8,128)(2,1)S(1)}, bf16[512,256]{1,0:T(8,128)(2,1)S(1)}, u32[]{:S(2)}, u32[]{:S(2)}) collective-permute-start(bf16[512,256]{1,0:T(8,128)(2,1)S(1)} %get-tuple-element.116.t0), channel_id=1, source_target_pairs={{0,4},{4,8},{8,12},{12,0},{1,5},{5,9},{9,13},{13,1},{2,6},{6,10},{... | collective-permute-start | bytes 786440 | tf_op jit(solution)/shard_map/ppermute | solution.py:518
  54.3 4.7 %collective-permute-done.12.got = bf16[512,256]{1,0:T(8,128)(2,1)S(1)} collective-permute-done((bf16[512,256]{1,0:T(8,128)(2,1)S(1)}, bf16[512,256]{1,0:T(8,128)(2,1)S(1)}, u32[]{:S(2)}, u32[]{:S(2)}) %collective-permute-start.12) | collective-permute-done | bytes 262176 | tf_op jit(solution)/shard_map/ppermute | solution.py:530
  59.0 0.6 second_sum.1.d0
  59.6 0.1 collective-permute-start.15
  59.7 3.2 %collective-permute-start.13 = (bf16[512,256]{1,0:T(8,128)(2,1)S(1)}, bf16[512,256]{1,0:T(8,128)(2,1)S(1)}, u32[]{:S(2)}, u32[]{:S(2)}) collective-permute-start(bf16[512,256]{1,0:T(8,128)(2,1)S(1)} %second_sum.1.d0), channel_id=1, source_target_pairs={{0,4},{4,8},{8,12},{12,0},{1,5},{5,9},{9,13},{13,1},{2,6},{6,10},{... | collective-permute-start | bytes 786440 | tf_op jit(solution)/shard_map/ppermute | solution.py:518
  63.1 3.3 %collective-permute-start.18 = (bf16[256,256]{1,0:T(8,128)(2,1)S(1)}, bf16[256,256]{1,0:T(8,128)(2,1)S(1)}, u32[]{:S(2)}, u32[]{:S(2)}) collective-permute-start(bf16[256,256]{1,0:T(8,128)(2,1)S(1)} %slice.58), channel_id=1, source_target_pairs={{0,4},{4,8},{8,12},{12,0},{1,5},{5,9},{9,13},{13,1},{2,6},{6,10},{... | collective-permute-start | bytes 393224 | tf_op jit(solution)/shard_map/ppermute | solution.py:518
  66.4 3.5 %collective-permute-done.15.d4 = bf16[512,256]{1,0:T(8,128)(2,1)S(1)} collective-permute-done((bf16[512,256]{1,0:T(8,128)(2,1)S(1)}, bf16[512,256]{1,0:T(8,128)(2,1)S(1)}, u32[]{:S(2)}, u32[]{:S(2)}) %collective-permute-start.15) | collective-permute-done | bytes 262176 | tf_op jit(solution)/shard_map/ppermute | solution.py:518
  70.0 3.5 %collective-permute-start.14 = (bf16[256,256]{1,0:T(8,128)(2,1)S(1)}, bf16[256,256]{1,0:T(8,128)(2,1)S(1)}, u32[]{:S(2)}, u32[]{:S(2)}) collective-permute-start(bf16[256,256]{1,0:T(8,128)(2,1)S(1)} %slice.56), channel_id=1, source_target_pairs={{0,4},{4,8},{8,12},{12,0},{1,5},{5,9},{9,13},{13,1},{2,6},{6,10},{... | collective-permute-start | bytes 393224 | tf_op jit(solution)/shard_map/ppermute | solution.py:518
  73.5 1.7 %slopes.1 = (f32[128,1536]{1,0:T(8,128)S(1)}, f32[160,1536]{1,0:T(8,128)S(1)}) custom-call(bf16[128,1536]{1,0:T(8,128)(2,1)S(1)} %bitcast.21, bf16[160,1536]{1,0:T(8,128)(2,1)S(1)} %copy-done.6, f32[3,1536]{1,0:T(4,128)S(1)} %copy-done.8), custom_call_target="tpu_custom_call" | custom-call | flops 1000 | bytes 9360000 | tf_op jit(solution)/shard_map/slopes/pallas_call | solution.py:39
  75.3 1.9 %project.1 = (bf16[128,1536]{1,0:T(8,128)(2,1)}, f32[128,1536]{1,0:T(8,128)S(1)}) custom-call(s32[10]{0:T(128)S(1)} %copy-done.12, bf16[512,256]{1,0:T(8,128)(2,1)S(1)} %get-tuple-element.116.t0, bf16[512,256]{1,0:T(8,128)(2,1)S(1)} %collective-permute-done.17.t1, bf16[256,256]{1,0:T(8,128)(2,1)S(1)} %collective-permute-done.18.t2, ...), custom_call_target="tpu_custom_call" | custom-call | flops 1000 | bytes 7200000 | tf_op jit(solution)/shard_map/project/pallas_call | solution.py:39
  77.2 1.7 %weigh_first.1.before = f32[2,4,192,256]{3,2,1,0:T(8,128)S(1)} custom-call(s32[10]{0:T(128)S(1)} %copy-done.12, bf16[128,768]{1,0:T(8,128)(2,1)S(1)} %get-tuple-element.112.f0, bf16[128,768]{1,0:T(8,128)(2,1)S(1)} %collective-permute-done.7.f1, bf16[128,768]{1,0:T(8,128)(2,1)S(1)} %collective-permute-done.10.f2, ...), custom_call_target="tpu_custom_call" | custom-call | flops 1000 | bytes 7200000 | tf_op jit(solution)/shard_map/weigh_first/pallas_call | solution.py:39
  78.9 1.4 %weigh_second.1 = (f32[4,192,512]{2,1,0:T(8,128)S(1)}, bf16[4,192,512]{2,1,0:T(8,128)(2,1)S(1)}) custom-call(s32[10]{0:T(128)S(1)} %copy-done.12, bf16[128,768]{1,0:T(8,128)(2,1)S(1)} %get-tuple-element.112.f0, bf16[128,768]{1,0:T(8,128)(2,1)S(1)} %collective-permute-done.7.f1, bf16[128,768]{1,0:T(8,128)(2,1)S(1)} %collective-permute-done.10.f2, ...), custom_call_target="tpu_custom_call" | custom-call | flops 1000 | bytes 5400000 | tf_op jit(solution)/shard_map/weigh_second/pallas_call | solution.py:39
  80.3 0.1 collective-permute-start.23
  80.4 0.1 copy-done.1
  80.5 0.2 copy-done.5
  80.7 2.3 %grad_top.1.grad = bf16[128,1536]{1,0:T(8,128)(2,1)S(1)} custom-call(s32[10]{0:T(128)S(1)} %copy-done.12, bf16[512,256]{1,0:T(8,128)(2,1)S(1)} %second_sum.1.d0, bf16[512,256]{1,0:T(8,128)(2,1)S(1)} %collective-permute-done.13.d1, bf16[256,256]{1,0:T(8,128)(2,1)S(1)} %collective-permute-done.14.d2, bf16[256,256]{1,0:T(8,128)(2,1)S(1)} %collective-permute-done.16.d3, ...), custom_call_target="tpu_custom_call" | custom-call | flops 1000 | bytes 10800000 | tf_op jit(solution)/shard_map/grad_top/pallas_call | solution.py:39
  83.0 0.8 fold.2
  83.9 0.5 collective-permute-start.24
  84.3 3.1 %collective-permute-start.25 = (bf16[4,48,512]{2,1,0:T(8,128)(2,1)S(1)}, bf16[4,48,512]{2,1,0:T(8,128)(2,1)S(1)}, u32[]{:S(2)}, u32[]{:S(2)}) collective-permute-start(bf16[4,48,512]{2,1,0:T(8,128)(2,1)S(1)} %get-tuple-element.135), channel_id=1, source_target_pairs={{0,128},{2,130},{128,0},{130,2},{1,129},{3,131},{129,1},{131,3},{4... | collective-permute-start | bytes 589832 | tf_op jit(solution)/shard_map/ppermute | solution.py:689
  87.4 1.3 %collective-permute-start.26 = (bf16[4,48,512]{2,1,0:T(8,128)(2,1)S(1)}, bf16[4,48,512]{2,1,0:T(8,128)(2,1)S(1)}, u32[]{:S(2)}, u32[]{:S(2)}) collective-permute-start(bf16[4,48,512]{2,1,0:T(8,128)(2,1)S(1)} %get-tuple-element.136), channel_id=1, source_target_pairs={{0,130},{2,128},{128,2},{130,0},{1,131},{3,129},{129,3},{131,1},{4... | collective-permute-start | bytes 589832 | tf_op jit(solution)/shard_map/ppermute | solution.py:689
  88.7 1.9 %collective-permute-start.22 = (bf16[32,1536]{1,0:T(8,128)(2,1)S(1)}, bf16[32,1536]{1,0:T(8,128)(2,1)S(1)}, u32[]{:S(2)}, u32[]{:S(2)}) collective-permute-start(bf16[32,1536]{1,0:T(8,128)(2,1)S(1)} %get-tuple-element.153), channel_id=1, source_target_pairs={{1,0},{2,1},{3,2},{4,3},{5,4},{6,5},{7,6},{8,7},{9,8},{10,9},{11,1... | collective-permute-start | bytes 294920 | tf_op jit(solution)/shard_map/ppermute | solution.py:536
  90.6 2.4 %collective-permute-start.21 = (bf16[32,1536]{1,0:T(8,128)(2,1)S(1)}, bf16[32,1536]{1,0:T(8,128)(2,1)S(1)}, u32[]{:S(2)}, u32[]{:S(2)}) collective-permute-start(bf16[32,1536]{1,0:T(8,128)(2,1)S(1)} %get-tuple-element.154), channel_id=1, source_target_pairs={{0,1},{1,2},{2,3},{3,4},{4,5},{5,6},{6,7},{7,8},{8,9},{9,10},{10,1... | collective-permute-start | bytes 294920 | tf_op jit(solution)/shard_map/ppermute | solution.py:535
  93.0 1.3 %collective-permute-done.22.right = bf16[32,1536]{1,0:T(8,128)(2,1)S(1)} collective-permute-done((bf16[32,1536]{1,0:T(8,128)(2,1)S(1)}, bf16[32,1536]{1,0:T(8,128)(2,1)S(1)}, u32[]{:S(2)}, u32[]{:S(2)}) %collective-permute-start.22) | collective-permute-done | bytes 98336 | tf_op jit(solution)/shard_map/ppermute | solution.py:536
  94.3 3.1 %collective-permute-done.21.left = bf16[32,1536]{1,0:T(8,128)(2,1)S(1)} collective-permute-done((bf16[32,1536]{1,0:T(8,128)(2,1)S(1)}, bf16[32,1536]{1,0:T(8,128)(2,1)S(1)}, u32[]{:S(2)}, u32[]{:S(2)}) %collective-permute-start.21) | collective-permute-done | bytes 98336 | tf_op jit(solution)/shard_map/ppermute | solution.py:535
  97.4 1.8 %collective-permute-done.26.refs_2_ = bf16[4,48,512]{2,1,0:T(8,128)(2,1)S(1)} collective-permute-done((bf16[4,48,512]{2,1,0:T(8,128)(2,1)S(1)}, bf16[4,48,512]{2,1,0:T(8,128)(2,1)S(1)}, u32[]{:S(2)}, u32[]{:S(2)}) %collective-permute-start.26) | collective-permute-done | bytes 196640 | tf_op jit(solution)/shard_map/ppermute | solution.py:689
  99.3 0.7 fold.3
  100.0 2.0 %collective-permute-start.27 = (bf16[4,24,512]{2,1,0:T(8,128)(2,1)S(1)}, bf16[4,24,512]{2,1,0:T(8,128)(2,1)S(1)}, u32[]{:S(2)}, u32[]{:S(2)}) collective-permute-start(bf16[4,24,512]{2,1,0:T(8,128)(2,1)S(1)} %get-tuple-element.145), channel_id=1, source_target_pairs={{0,16},{16,0},{32,48},{48,32},{64,80},{80,64},{96,112},{112,96},{1... | collective-permute-start | bytes 294920 | tf_op jit(solution)/shard_map/ppermute | solution.py:695
  102.0 3.7 %backward.1 = bf16[128,1536]{1,0:T(8,128)(2,1)} custom-call(s32[10]{0:T(128)S(1)} %copy-done.12, s32[2]{0:T(128)S(1)} %copy-done.15, bf16[32,1536]{1,0:T(8,128)(2,1)S(1)} %collective-permute-done.21.left, bf16[32,1536]{1,0:T(8,128)(2,1)S(1)} %collective-permute-done.22.right, bf16[128,1536]{1,0:T(8,128)(2,1)S(1)} %grad_top.1.grad, ...), custom_call_target="tpu_custom_call" | custom-call | flops 1000 | bytes 16559999 | tf_op jit(solution)/shard_map/backward/pallas_call | solution.py:39
  105.7 0.6 last_fold.1
  106.3 3.3 %collective-permute-start.28 = (f32[4,6,512]{2,1,0:T(8,128)S(1)}, f32[4,6,512]{2,1,0:T(8,128)S(1)}, u32[]{:S(2)}, u32[]{:S(2)}) collective-permute-start(f32[4,6,512]{2,1,0:T(8,128)S(1)} %get-tuple-element.150), channel_id=1, source_target_pairs={{0,32},{16,48},{32,64},{48,80},{64,96},{80,112},{96,0},{112,16},{1... | collective-permute-start | bytes 147464 | tf_op jit(solution)/shard_map/ppermute | solution.py:518
  109.6 4.5 %collective-permute-start.29 = (f32[4,6,512]{2,1,0:T(8,128)S(1)}, f32[4,6,512]{2,1,0:T(8,128)S(1)}, u32[]{:S(2)}, u32[]{:S(2)}) collective-permute-start(f32[4,6,512]{2,1,0:T(8,128)S(1)} %get-tuple-element.151), channel_id=1, source_target_pairs={{0,64},{16,80},{32,96},{48,112},{64,0},{80,16},{96,32},{112,48},{1... | collective-permute-start | bytes 147464 | tf_op jit(solution)/shard_map/ppermute | solution.py:518
  114.1 2.7 %collective-permute-start.30 = (f32[4,6,512]{2,1,0:T(8,128)S(1)}, f32[4,6,512]{2,1,0:T(8,128)S(1)}, u32[]{:S(2)}, u32[]{:S(2)}) collective-permute-start(f32[4,6,512]{2,1,0:T(8,128)S(1)} %get-tuple-element.152), channel_id=1, source_target_pairs={{0,96},{16,112},{32,0},{48,16},{64,32},{80,48},{96,64},{112,80},{1... | collective-permute-start | bytes 147464 | tf_op jit(solution)/shard_map/ppermute | solution.py:518
  116.8 1.6 %collective-permute-done.29.refs_2_ = f32[4,6,512]{2,1,0:T(8,128)S(1)} collective-permute-done((f32[4,6,512]{2,1,0:T(8,128)S(1)}, f32[4,6,512]{2,1,0:T(8,128)S(1)}, u32[]{:S(2)}, u32[]{:S(2)}) %collective-permute-start.29) | collective-permute-done | bytes 49184 | tf_op jit(solution)/shard_map/ppermute | solution.py:518
  118.4 2.1 %collective-permute-done.30.refs_3_ = f32[4,6,512]{2,1,0:T(8,128)S(1)} collective-permute-done((f32[4,6,512]{2,1,0:T(8,128)S(1)}, f32[4,6,512]{2,1,0:T(8,128)S(1)}, u32[]{:S(2)}, u32[]{:S(2)}) %collective-permute-start.30) | collective-permute-done | bytes 49184 | tf_op jit(solution)/shard_map/ppermute | solution.py:518
  120.6 1.3 %arrange.1 = f32[6,2048]{1,0:T(8,128)} custom-call(s32[10]{0:T(128)S(1)} %copy-done.12, f32[4,6,512]{2,1,0:T(8,128)S(1)} %get-tuple-element.149.refs_0_, f32[4,6,512]{2,1,0:T(8,128)S(1)} %collective-permute-done.28.refs_1_, f32[4,6,512]{2,1,0:T(8,128)S(1)} %collective-permute-done.29.refs_2_, f32[4,6,512]{2,1,0:T(8,128)S(1)} %collective-permute-done.30.refs_3_), custom_call_target="tpu_custom_call" | custom-call | flops 1000 | bytes 3600000 | tf_op jit(solution)/shard_map/arrange/pallas_call | solution.py:39
  (65 shorter events, 0.5 us)
Async XLA Ops:
  1.6 9.8 %collective-permute-start.1 = (bf16[32,1536]{1,0:T(8,128)(2,1)S(1)}, bf16[32,1536]{1,0:T(8,128)(2,1)S(1)}, u32[]{:S(2)}, u32[]{:S(2)}) collective-permute-start(bf16[32,1536]{1,0:T(8,128)(2,1)S(1)} %get-tuple-element.155), channel_id=1, source_target_pairs={{1,0},{2,1},{3,2},{4,3},{5,4},{6,5},{7,6},{8,7},{9,8},{10,9},{11,1... | collective-permute-start | bytes 294920 | tf_op jit(solution)/shard_map/ppermute | solution.py:536
  4.6 6.8 %collective-permute-start = (bf16[32,1536]{1,0:T(8,128)(2,1)S(1)}, bf16[32,1536]{1,0:T(8,128)(2,1)S(1)}, u32[]{:S(2)}, u32[]{:S(2)}) collective-permute-start(bf16[32,1536]{1,0:T(8,128)(2,1)S(1)} %get-tuple-element.156), channel_id=1, source_target_pairs={{0,1},{1,2},{2,3},{3,4},{4,5},{5,6},{6,7},{7,8},{8,9},{9,10},{10,1... | collective-permute-start | bytes 294920 | tf_op jit(solution)/shard_map/ppermute | solution.py:535
  11.4 0.6 copy-start.17
  11.4 0.6 copy-start.18
  12.1 8.7 %copy-start.3 = (bf16[1,128,1536]{2,1,0:T(8,128)(2,1)S(1)}, bf16[1,128,1536]{2,1,0:T(8,128)(2,1)}, u32[]{:S(2)}) copy-start(bf16[1,128,1536]{2,1,0:T(8,128)(2,1)} %param.22) | copy-start | bytes 1179652
  12.1 8.7 %copy-start.12 = (s32[10]{0:T(128)S(1)}, s32[10]{0:T(128)}, u32[]{:S(2)}) copy-start(s32[10]{0:T(128)} %stack.35.where) | copy-start | bytes 124
  12.1 8.7 %copy-start.14 = (s32[1,768]{1,0:T(1,128)S(1)}, s32[1,768]{1,0:T(1,128)}, u32[]{:S(2)}) copy-start(s32[1,768]{1,0:T(1,128)} %constant.50.clone.order) | copy-start | bytes 9220
  12.1 21.0 %copy-start.13 = (s32[4095]{0:T(1024)S(1)}, s32[4095]{0:T(1024)}, u32[]{:S(2)}) copy-start(s32[4095]{0:T(1024)} %param.17) | copy-start | bytes 49144
  12.1 21.0 %copy-start.16 = (f32[64,4]{0,1:T(4,128)S(1)}, f32[64,4]{0,1:T(4,128)}, u32[]{:S(2)}) copy-start(f32[64,4]{0,1:T(4,128)} %param.16) | copy-start | bytes 3076
  18.2 6.6 %collective-permute-start.2 = (bf16[128,512]{1,0:T(8,128)(2,1)}, bf16[128,512]{1,0:T(8,128)(2,1)S(1)}, u32[]{:S(2)}, u32[]{:S(2)}) collective-permute-start(bf16[128,512]{1,0:T(8,128)(2,1)} %get-tuple-element.81), channel_id=1, source_target_pairs={{0,4},{4,8},{8,12},{12,0},{1,5},{5,9},{9,13},{13,1},{2,6},{6,10},{... | collective-permute-start | bytes 393224 | tf_op jit(solution)/shard_map/ppermute | solution.py:518
  19.6 8.1 %collective-permute-start.3 = (bf16[128,512]{1,0:T(8,128)(2,1)}, bf16[128,512]{1,0:T(8,128)(2,1)S(1)}, u32[]{:S(2)}, u32[]{:S(2)}) collective-permute-start(bf16[128,512]{1,0:T(8,128)(2,1)} %get-tuple-element.82), channel_id=1, source_target_pairs={{0,8},{4,12},{8,0},{12,4},{1,9},{5,13},{9,1},{13,5},{2,10},{6,14},... | collective-permute-start | bytes 393224 | tf_op jit(solution)/shard_map/ppermute | solution.py:518
  20.7 8.5 %collective-permute-start.4 = (bf16[128,512]{1,0:T(8,128)(2,1)}, bf16[128,512]{1,0:T(8,128)(2,1)S(1)}, u32[]{:S(2)}, u32[]{:S(2)}) collective-permute-start(bf16[128,512]{1,0:T(8,128)(2,1)} %get-tuple-element.83), channel_id=1, source_target_pairs={{0,12},{4,0},{8,4},{12,8},{1,13},{5,1},{9,5},{13,9},{2,14},{6,2},{... | collective-permute-start | bytes 393224 | tf_op jit(solution)/shard_map/ppermute | solution.py:518
  20.8 1.0 copy-start.9
  21.8 19.5 %copy-start.10 = (bf16[128,512]{1,0:T(8,128)(2,1)S(1)}, bf16[128,512]{1,0:T(8,128)(2,1)}, u32[]{:S(2)}) copy-start(bf16[128,512]{1,0:T(8,128)(2,1)} %get-tuple-element.89.m0) | copy-start | bytes 393220
  30.1 9.6 %collective-permute-start.6 = (bf16[512,256]{1,0:T(8,128)(2,1)S(1)}, bf16[512,256]{1,0:T(8,128)(2,1)S(1)}, u32[]{:S(2)}, u32[]{:S(2)}) collective-permute-start(bf16[512,256]{1,0:T(8,128)(2,1)S(1)} %pad_maximum_fusion), channel_id=1, source_target_pairs={{0,2},{2,0},{1,3},{3,1},{4,6},{6,4},{5,7},{7,5},{8,10},{10,8},{9,1... | collective-permute-start | bytes 786440 | tf_op jit(solution)/shard_map/ppermute | solution.py:530
  31.1 6.6 %collective-permute-start.7 = (bf16[128,768]{1,0:T(8,128)(2,1)S(1)}, bf16[128,768]{1,0:T(8,128)(2,1)S(1)}, u32[]{:S(2)}, u32[]{:S(2)}) collective-permute-start(bf16[128,768]{1,0:T(8,128)(2,1)S(1)} %get-tuple-element.93), channel_id=1, source_target_pairs={{0,4},{4,8},{8,12},{12,0},{1,5},{5,9},{9,13},{13,1},{2,6},{6,10},{... | collective-permute-start | bytes 589832 | tf_op jit(solution)/shard_map/ppermute | solution.py:518
  32.2 7.6 %collective-permute-start.8 = (bf16[128,768]{1,0:T(8,128)(2,1)S(1)}, bf16[128,768]{1,0:T(8,128)(2,1)S(1)}, u32[]{:S(2)}, u32[]{:S(2)}) collective-permute-start(bf16[128,768]{1,0:T(8,128)(2,1)S(1)} %get-tuple-element.94), channel_id=1, source_target_pairs={{0,12},{4,0},{8,4},{12,8},{1,13},{5,1},{9,5},{13,9},{2,14},{6,2},{... | collective-permute-start | bytes 589832 | tf_op jit(solution)/shard_map/ppermute | solution.py:518
  33.1 7.4 %collective-permute-start.5 = (bf16[512,256]{1,0:T(8,128)(2,1)S(1)}, bf16[512,256]{1,0:T(8,128)(2,1)S(1)}, u32[]{:S(2)}, u32[]{:S(2)}) collective-permute-start(bf16[512,256]{1,0:T(8,128)(2,1)S(1)} %pad_maximum_fusion), channel_id=1, source_target_pairs={{0,1},{1,0},{2,3},{3,2},{4,5},{5,4},{6,7},{7,6},{8,9},{9,8},{10,11... | collective-permute-start | bytes 786440 | tf_op jit(solution)/shard_map/ppermute | solution.py:530
  39.7 1.5 %collective-permute-start.9 = (bf16[512,256]{1,0:T(8,128)(2,1)S(1)}, bf16[512,256]{1,0:T(8,128)(2,1)S(1)}, u32[]{:S(2)}, u32[]{:S(2)}) collective-permute-start(bf16[512,256]{1,0:T(8,128)(2,1)S(1)} %collective-permute-done.6.kv2), channel_id=1, source_target_pairs={{0,1},{1,0},{2,3},{3,2},{4,5},{5,4},{6,7},{7,6},{8,9},{9,8},{10,11... | collective-permute-start | bytes 786440 | tf_op jit(solution)/shard_map/ppermute | solution.py:530
  39.7 8.8 %collective-permute-start.10 = (bf16[128,768]{1,0:T(8,128)(2,1)S(1)}, bf16[128,768]{1,0:T(8,128)(2,1)S(1)}, u32[]{:S(2)}, u32[]{:S(2)}) collective-permute-start(bf16[128,768]{1,0:T(8,128)(2,1)S(1)} %get-tuple-element.103), channel_id=1, source_target_pairs={{0,8},{4,12},{8,0},{12,4},{1,9},{5,13},{9,1},{13,5},{2,10},{6,14},... | collective-permute-start | bytes 589832 | tf_op jit(solution)/shard_map/ppermute | solution.py:518
  48.2 25.3 %copy-start.2 = (bf16[1,128,1536]{2,1,0:T(8,128)(2,1)S(1)}, bf16[1,128,1536]{2,1,0:T(8,128)(2,1)}, u32[]{:S(2)}) copy-start(bf16[1,128,1536]{2,1,0:T(8,128)(2,1)} %param.12) | copy-start | bytes 1179652
  48.2 25.3 %copy-start.6 = (bf16[160,1536]{1,0:T(8,128)(2,1)S(1)}, bf16[160,1536]{1,0:T(8,128)(2,1)}, u32[]{:S(2)}) copy-start(bf16[160,1536]{1,0:T(8,128)(2,1)} %get-tuple-element.121.near) | copy-start | bytes 1474564
  48.2 25.3 %copy-start.8 = (f32[3,1536]{1,0:T(4,128)S(1)}, f32[3,1536]{1,0:T(4,128)}, u32[]{:S(2)}) copy-start(f32[3,1536]{1,0:T(4,128)} %gains.7) | copy-start | bytes 55300
  48.6 1.9 %collective-permute-start.11 = (bf16[1024,256]{1,0:T(8,128)(2,1)S(1)}, bf16[1024,256]{1,0:T(8,128)(2,1)S(1)}, u32[]{:S(2)}, u32[]{:S(2)}) collective-permute-start(bf16[1024,256]{1,0:T(8,128)(2,1)S(1)} %get-tuple-element.105), channel_id=1, source_target_pairs={{0,1},{1,0},{2,3},{3,2},{4,5},{5,4},{6,7},{7,6},{8,9},{9,8},{10,11... | collective-permute-start | bytes 1572872 | tf_op jit(solution)/shard_map/ppermute | solution.py:530
  50.5 24.8 %copy-start = (bf16[768,1536]{1,0:T(8,128)(2,1)S(1)}, bf16[768,1536]{1,0:T(8,128)(2,1)}, u32[]{:S(2)}) copy-start(bf16[768,1536]{1,0:T(8,128)(2,1)} %w_out.1) | copy-start | bytes 7077892
  50.5 24.8 %copy-start.4 = (bf16[1536,256]{1,0:T(8,128)(2,1)S(1)}, bf16[1536,256]{1,0:T(8,128)(2,1)}, u32[]{:S(2)}) copy-start(bf16[1536,256]{1,0:T(8,128)(2,1)} %w_query.1) | copy-start | bytes 2359300
  50.5 24.8 %copy-start.7 = (bf16[128,1536]{1,0:T(8,128)(2,1)S(1)}, bf16[128,1536]{1,0:T(8,128)(2,1)}, u32[]{:S(2)}) copy-start(bf16[128,1536]{1,0:T(8,128)(2,1)} %get-tuple-element.117.z) | copy-start | bytes 1179652
  50.6 8.4 %collective-permute-start.12 = (bf16[512,256]{1,0:T(8,128)(2,1)S(1)}, bf16[512,256]{1,0:T(8,128)(2,1)S(1)}, u32[]{:S(2)}, u32[]{:S(2)}) collective-permute-start(bf16[512,256]{1,0:T(8,128)(2,1)S(1)} %get-tuple-element.109), channel_id=1, source_target_pairs={{0,2},{2,0},{1,3},{3,1},{4,6},{6,4},{5,7},{7,5},{8,10},{10,8},{9,1... | collective-permute-start | bytes 786440 | tf_op jit(solution)/shard_map/ppermute | solution.py:530
  51.1 11.9 %collective-permute-start.19 = (bf16[512,256]{1,0:T(8,128)(2,1)S(1)}, bf16[512,256]{1,0:T(8,128)(2,1)S(1)}, u32[]{:S(2)}, u32[]{:S(2)}) collective-permute-start(bf16[512,256]{1,0:T(8,128)(2,1)S(1)} %get-tuple-element.116.t0), channel_id=1, source_target_pairs={{0,12},{4,0},{8,4},{12,8},{1,13},{5,1},{9,5},{13,9},{2,14},{6,2},{... | collective-permute-start | bytes 786440 | tf_op jit(solution)/shard_map/ppermute | solution.py:518
  51.3 11.7 %collective-permute-start.17 = (bf16[512,256]{1,0:T(8,128)(2,1)S(1)}, bf16[512,256]{1,0:T(8,128)(2,1)S(1)}, u32[]{:S(2)}, u32[]{:S(2)}) collective-permute-start(bf16[512,256]{1,0:T(8,128)(2,1)S(1)} %get-tuple-element.116.t0), channel_id=1, source_target_pairs={{0,4},{4,8},{8,12},{12,0},{1,5},{5,9},{9,13},{13,1},{2,6},{6,10},{... | collective-permute-start | bytes 786440 | tf_op jit(solution)/shard_map/ppermute | solution.py:518
  59.6 10.2 %collective-permute-start.15 = (bf16[512,256]{1,0:T(8,128)(2,1)S(1)}, bf16[512,256]{1,0:T(8,128)(2,1)S(1)}, u32[]{:S(2)}, u32[]{:S(2)}) collective-permute-start(bf16[512,256]{1,0:T(8,128)(2,1)S(1)} %second_sum.1.d0), channel_id=1, source_target_pairs={{0,12},{4,0},{8,4},{12,8},{1,13},{5,1},{9,5},{13,9},{2,14},{6,2},{... | collective-permute-start | bytes 786440 | tf_op jit(solution)/shard_map/ppermute | solution.py:518
  59.7 10.2 %collective-permute-start.13 = (bf16[512,256]{1,0:T(8,128)(2,1)S(1)}, bf16[512,256]{1,0:T(8,128)(2,1)S(1)}, u32[]{:S(2)}, u32[]{:S(2)}) collective-permute-start(bf16[512,256]{1,0:T(8,128)(2,1)S(1)} %second_sum.1.d0), channel_id=1, source_target_pairs={{0,4},{4,8},{8,12},{12,0},{1,5},{5,9},{9,13},{13,1},{2,6},{6,10},{... | collective-permute-start | bytes 786440 | tf_op jit(solution)/shard_map/ppermute | solution.py:518
  63.0 12.3 %collective-permute-start.20 = (bf16[256,256]{1,0:T(8,128)(2,1)S(1)}, bf16[256,256]{1,0:T(8,128)(2,1)S(1)}, u32[]{:S(2)}, u32[]{:S(2)}) collective-permute-start(bf16[256,256]{1,0:T(8,128)(2,1)S(1)} %slice.59), channel_id=1, source_target_pairs={{0,12},{4,0},{8,4},{12,8},{1,13},{5,1},{9,5},{13,9},{2,14},{6,2},{... | collective-permute-start | bytes 393224 | tf_op jit(solution)/shard_map/ppermute | solution.py:518
  63.1 12.2 %collective-permute-start.18 = (bf16[256,256]{1,0:T(8,128)(2,1)S(1)}, bf16[256,256]{1,0:T(8,128)(2,1)S(1)}, u32[]{:S(2)}, u32[]{:S(2)}) collective-permute-start(bf16[256,256]{1,0:T(8,128)(2,1)S(1)} %slice.58), channel_id=1, source_target_pairs={{0,4},{4,8},{8,12},{12,0},{1,5},{5,9},{9,13},{13,1},{2,6},{6,10},{... | collective-permute-start | bytes 393224 | tf_op jit(solution)/shard_map/ppermute | solution.py:518
  69.9 9.0 %collective-permute-start.16 = (bf16[256,256]{1,0:T(8,128)(2,1)S(1)}, bf16[256,256]{1,0:T(8,128)(2,1)S(1)}, u32[]{:S(2)}, u32[]{:S(2)}) collective-permute-start(bf16[256,256]{1,0:T(8,128)(2,1)S(1)} %slice.57), channel_id=1, source_target_pairs={{0,12},{4,0},{8,4},{12,8},{1,13},{5,1},{9,5},{13,9},{2,14},{6,2},{... | collective-permute-start | bytes 393224 | tf_op jit(solution)/shard_map/ppermute | solution.py:518
  70.0 8.9 %collective-permute-start.14 = (bf16[256,256]{1,0:T(8,128)(2,1)S(1)}, bf16[256,256]{1,0:T(8,128)(2,1)S(1)}, u32[]{:S(2)}, u32[]{:S(2)}) collective-permute-start(bf16[256,256]{1,0:T(8,128)(2,1)S(1)} %slice.56), channel_id=1, source_target_pairs={{0,4},{4,8},{8,12},{12,0},{1,5},{5,9},{9,13},{13,1},{2,6},{6,10},{... | collective-permute-start | bytes 393224 | tf_op jit(solution)/shard_map/ppermute | solution.py:518
  78.8 1.7 %copy-start.1 = (bf16[1536,768]{1,0:T(8,128)(2,1)S(1)}, bf16[1536,768]{1,0:T(8,128)(2,1)}, u32[]{:S(2)}) copy-start(bf16[1536,768]{1,0:T(8,128)(2,1)} %w_value.1) | copy-start | bytes 7077892
  78.8 1.8 %copy-start.5 = (bf16[1536,256]{1,0:T(8,128)(2,1)S(1)}, bf16[1536,256]{1,0:T(8,128)(2,1)}, u32[]{:S(2)}) copy-start(bf16[1536,256]{1,0:T(8,128)(2,1)} %w_key.1) | copy-start | bytes 2359300
  80.3 2.7 %collective-permute-start.23 = (bf16[4,192,512]{2,1,0:T(8,128)(2,1)S(1)}, bf16[4,192,512]{2,1,0:T(8,128)(2,1)S(1)}, u32[]{:S(2)}, u32[]{:S(2)}) collective-permute-start(bf16[4,192,512]{2,1,0:T(8,128)(2,1)S(1)} %get-tuple-element.133), channel_id=1, source_target_pairs={{0,1},{1,0},{2,3},{3,2},{4,5},{5,4},{6,7},{7,6},{8,9},{9,8},{10,11... | collective-permute-start | bytes 2359304 | tf_op jit(solution)/shard_map/ppermute | solution.py:530
  83.0 19.0 %copy-start.11 = (f32[2,3,1536]{2,0,1:T(2,128)S(1)}, f32[2,3,1536]{2,0,1:T(2,128)}, u32[]{:S(2)}) copy-start(f32[2,3,1536]{2,0,1:T(2,128)} %param.14) | copy-start | bytes 110596
  83.0 19.0 %copy-start.15 = (s32[2]{0:T(128)S(1)}, s32[2]{0:T(128)}, u32[]{:S(2)}) copy-start(s32[2]{0:T(128)} %dil.3) | copy-start | bytes 28
  83.9 13.6 %collective-permute-start.24 = (bf16[4,48,512]{2,1,0:T(8,128)(2,1)S(1)}, bf16[4,48,512]{2,1,0:T(8,128)(2,1)S(1)}, u32[]{:S(2)}, u32[]{:S(2)}) collective-permute-start(bf16[4,48,512]{2,1,0:T(8,128)(2,1)S(1)} %get-tuple-element.134), channel_id=1, source_target_pairs={{0,2},{2,0},{128,130},{130,128},{1,3},{3,1},{129,131},{131,129},{4... | collective-permute-start | bytes 589832 | tf_op jit(solution)/shard_map/ppermute | solution.py:689
  84.3 13.1 %collective-permute-start.25 = (bf16[4,48,512]{2,1,0:T(8,128)(2,1)S(1)}, bf16[4,48,512]{2,1,0:T(8,128)(2,1)S(1)}, u32[]{:S(2)}, u32[]{:S(2)}) collective-permute-start(bf16[4,48,512]{2,1,0:T(8,128)(2,1)S(1)} %get-tuple-element.135), channel_id=1, source_target_pairs={{0,128},{2,130},{128,0},{130,2},{1,129},{3,131},{129,1},{131,3},{4... | collective-permute-start | bytes 589832 | tf_op jit(solution)/shard_map/ppermute | solution.py:689
  87.4 11.9 %collective-permute-start.26 = (bf16[4,48,512]{2,1,0:T(8,128)(2,1)S(1)}, bf16[4,48,512]{2,1,0:T(8,128)(2,1)S(1)}, u32[]{:S(2)}, u32[]{:S(2)}) collective-permute-start(bf16[4,48,512]{2,1,0:T(8,128)(2,1)S(1)} %get-tuple-element.136), channel_id=1, source_target_pairs={{0,130},{2,128},{128,2},{130,0},{1,131},{3,129},{129,3},{131,1},{4... | collective-permute-start | bytes 589832 | tf_op jit(solution)/shard_map/ppermute | solution.py:689
  88.7 5.6 %collective-permute-start.22 = (bf16[32,1536]{1,0:T(8,128)(2,1)S(1)}, bf16[32,1536]{1,0:T(8,128)(2,1)S(1)}, u32[]{:S(2)}, u32[]{:S(2)}) collective-permute-start(bf16[32,1536]{1,0:T(8,128)(2,1)S(1)} %get-tuple-element.153), channel_id=1, source_target_pairs={{1,0},{2,1},{3,2},{4,3},{5,4},{6,5},{7,6},{8,7},{9,8},{10,9},{11,1... | collective-permute-start | bytes 294920 | tf_op jit(solution)/shard_map/ppermute | solution.py:536
  90.6 6.8 %collective-permute-start.21 = (bf16[32,1536]{1,0:T(8,128)(2,1)S(1)}, bf16[32,1536]{1,0:T(8,128)(2,1)S(1)}, u32[]{:S(2)}, u32[]{:S(2)}) collective-permute-start(bf16[32,1536]{1,0:T(8,128)(2,1)S(1)} %get-tuple-element.154), channel_id=1, source_target_pairs={{0,1},{1,2},{2,3},{3,4},{4,5},{5,6},{6,7},{7,8},{8,9},{9,10},{10,1... | collective-permute-start | bytes 294920 | tf_op jit(solution)/shard_map/ppermute | solution.py:535
  100.0 5.7 %collective-permute-start.27 = (bf16[4,24,512]{2,1,0:T(8,128)(2,1)S(1)}, bf16[4,24,512]{2,1,0:T(8,128)(2,1)S(1)}, u32[]{:S(2)}, u32[]{:S(2)}) collective-permute-start(bf16[4,24,512]{2,1,0:T(8,128)(2,1)S(1)} %get-tuple-element.145), channel_id=1, source_target_pairs={{0,16},{16,0},{32,48},{48,32},{64,80},{80,64},{96,112},{112,96},{1... | collective-permute-start | bytes 294920 | tf_op jit(solution)/shard_map/ppermute | solution.py:695
  106.3 10.5 %collective-permute-start.28 = (f32[4,6,512]{2,1,0:T(8,128)S(1)}, f32[4,6,512]{2,1,0:T(8,128)S(1)}, u32[]{:S(2)}, u32[]{:S(2)}) collective-permute-start(f32[4,6,512]{2,1,0:T(8,128)S(1)} %get-tuple-element.150), channel_id=1, source_target_pairs={{0,32},{16,48},{32,64},{48,80},{64,96},{80,112},{96,0},{112,16},{1... | collective-permute-start | bytes 147464 | tf_op jit(solution)/shard_map/ppermute | solution.py:518
  109.6 8.8 %collective-permute-start.29 = (f32[4,6,512]{2,1,0:T(8,128)S(1)}, f32[4,6,512]{2,1,0:T(8,128)S(1)}, u32[]{:S(2)}, u32[]{:S(2)}) collective-permute-start(f32[4,6,512]{2,1,0:T(8,128)S(1)} %get-tuple-element.151), channel_id=1, source_target_pairs={{0,64},{16,80},{32,96},{48,112},{64,0},{80,16},{96,32},{112,48},{1... | collective-permute-start | bytes 147464 | tf_op jit(solution)/shard_map/ppermute | solution.py:518
  114.1 6.4 %collective-permute-start.30 = (f32[4,6,512]{2,1,0:T(8,128)S(1)}, f32[4,6,512]{2,1,0:T(8,128)S(1)}, u32[]{:S(2)}, u32[]{:S(2)}) collective-permute-start(f32[4,6,512]{2,1,0:T(8,128)S(1)} %get-tuple-element.152), channel_id=1, source_target_pairs={{0,96},{16,112},{32,0},{48,16},{64,32},{80,48},{96,64},{112,80},{1... | collective-permute-start | bytes 147464 | tf_op jit(solution)/shard_map/ppermute | solution.py:518
where the time goes:
time: 122 us
  starting transfers between devices  46.9 us (38%)
  Pallas kernels  37 us (30%)
  waiting for transfers between devices  32.4 us (27%)
  local copies, waits for them, and re-layouts  4.46 us (4%)
    pallas_call x17, Pallas kernels, call(): pl.pallas_call(body, out_shape=tuple((jax.ShapeDtypeStruct(s, d) for s, d...  37 us
    ppermute x17, starting transfers between devices, shift(): lax.ppermute(array, axis, [(i, (i + step) % count) for i in range(count)])  29.4 us
    ppermute x17, waiting for transfers between devices, shift(): lax.ppermute(array, axis, [(i, (i + step) % count) for i in range(count)])  18.6 us
    ppermute x6, waiting for transfers between devices, flip(): return lax.ppermute(array, axis, [(0, 1), (1, 0)])  7.44 us
    ppermute x2, starting transfers between devices, halo(): lax.ppermute(rows[:width], SEQ, [(i + 1, i) for i in range(nseq - 1)])  4.94 us
    ppermute x3, starting transfers between devices, local(): got.append(lax.ppermute(send, ('xh', 'xl'), way))  4.79 us
    ppermute x2, starting transfers between devices, halo(): lax.ppermute(rows[-width:], SEQ, [(i, i + 1) for i in range(nseq - 1)])  4.33 us
    ppermute x2, waiting for transfers between devices, halo(): lax.ppermute(rows[-width:], SEQ, [(i, i + 1) for i in range(nseq - 1)])  3.16 us
  transfers between devices with their start and end apart: 31, of which 15 were waited for; matrix products, arithmetic and copies ran while one was open for 1% of the time, Pallas kernels for 21%

commit v1 on v0

--- a/solution.py
+++ b/solution.py
@@ -68,7 +68,8 @@
         body(pl.multiple_of(i * STEP, STEP))
         return carry
 
-    lax.fori_loop(0, count // STEP, step, 0, unroll=2)
+    steps = count // STEP
+    lax.fori_loop(0, steps, step, 0, unroll=next(u for u in (4, 5, 2, 1) if steps % u == 0))
 
 
 def inside(start, first, last, edge, count):
@@ -161,12 +162,14 @@
 
 
 def forward(
-    where, dil, left, right, rows, act, d_att, taps, gains, wq_far, wk_far, wv_far,
+    dil, left, right, rows, act, d_att, taps, gains, wq_far, wk_far, wv_far,
     m0, m1, m2, m3, normed, z, near,
     x_ext, a_ext, b_ext, slots, moved1, moved2, w_query, w_key, w_value, sems,
 ):
     copies = fetch(((wq_far, w_query), (wk_far, w_key), (wv_far, w_value)), sems)
-    iy, iseq, nseq = where[0], where[1], where[2]
+    iy = lax.axis_index("y")
+    first = (iy == 0) & (lax.axis_index("xl") == 0) & (lax.axis_index("core") == 0)
+    last = (iy == HEADS - 1) & (lax.axis_index("xl") == 1) & (lax.axis_index("core") == 1)
     tok = rows.shape[0]
     x_ext[0:HALO, :] = left[...]
     x_ext[HALO : HALO + tok, :] = rows[...]
@@ -176,7 +179,6 @@
     for r in [*range(0, HALO, STEP), *range(HALO + tok, 2 * HALO + tok, STEP)]:
         a_ext[r : r + STEP, :] = activate(x_ext[r : r + STEP, :].astype(F32), gain).astype(BF16)
     gap, wide = dil[0], dil[1]
-    first, last = iseq == 0, iseq == nseq - 1
     count = tok + 2 * DMAX
     gain = gains[1:2, :]
     move(moved1, a_ext, gap)
@@ -575,12 +577,12 @@
     *ms, normed, z, near = call(
         forward,
         [((tok, 2 * WIDE), BF16)] * 4 + [(big, BF16), (big, BF16), (mid, BF16)],
-        (where, dilations, left, right, rows, act, d_att, taps, gains, w_query, w_key, w_value),
+        (dilations, left, right, rows, act, d_att, taps, gains, w_query, w_key, w_value),
         [pltpu.VMEM(ext, BF16), pltpu.VMEM(ext, BF16), pltpu.VMEM(mid, BF16),
          pltpu.VMEM((HEADS, tok, 2 * WIDE), BF16), *shifted,
          *(pltpu.VMEM(w.shape, BF16) for w in (w_query, w_key, w_value)), pltpu.SemaphoreType.DMA((3,))],
-        smem=(0, 1),
-        hbm=(9, 10, 11),
+        smem=(0,),
+        hbm=(8, 9, 10),
         us=5.0,
         limit=LARGE,
     )
@@ -627,11 +629,12 @@
     own, far = call(
         first_sum, [((many, WIDE), F32), ((many, WIDE), BF16)], (own, far, got), us=0.5
     )
-    far, t = lax.optimization_barrier((far, t))
+    far, t, near, held = lax.optimization_barrier((far, t, near, rows))
     got = flip(far, "xl")
+    slope0, slope1 = call(slopes, [(big, F32), (mid, F32)], (held, near, gains), us=0.01)
+    got, slope0, slope1 = lax.optimization_barrier((got, slope0, slope1))
     ts = ring(t, "y", ny)
     (d,) = call(second_sum, [((many, WIDE), BF16)], (where, own, got), smem=(0,), us=0.5)
-    d, near, held = lax.optimization_barrier((d, near, rows))
     ds = ring(d, "y", ny)
     fields = ((many, nxh * unit // 4), BF16)
     cuts = (nxh, nz0, nzh * share)
@@ -653,10 +656,7 @@
         smem=(0,),
         us=2.0,
     )
-    slope0, slope1 = call(slopes, [(big, F32), (mid, F32)], (held, near, gains), us=2.6)
-    ds, before, result, g_query, slope0, slope1 = lax.optimization_barrier(
-        (ds, before, result, g_query, slope0, slope1)
-    )
+    ds, before, result, g_query = lax.optimization_barrier((ds, before, result, g_query))
     keep, give = call(
         functools.partial(weigh_second, cuts),
         [((HEADS, half, 2 * WIDE), F32), ((HEADS, half, 2 * WIDE), BF16)],
@@ -711,7 +711,8 @@
         smem=(0,),
         us=0.6,
     )
-    parts = [parts[0]] + [shift(parts[k], "z", nz, k * nz0) for k in range(1, nzh)]
+    away = sorted(range(1, nzh), key=lambda k: -min(k, nzh - k))
+    parts = [parts[0]] + [shift(parts[k], "z", nz, k * nz0) for k in away]
     (weight_sum,) = call(
         arrange, [((share, 8 * WIDE), F32)], (where, *parts), smem=(0,), us=1.0
     )

time: 122 us -> 119 us (0.975); the launches traced: 122 us -> 117 us
  waiting for transfers between devices: 32.4 us -> 29.8 us
  Pallas kernels: 37 us -> 35.4 us
    pallas_call x17, Pallas kernels: 37 us -> 35.4 us  [call(): pl.pallas_call(body, out_shape=tuple((jax.ShapeDtypeStruct(s, d) for s, d...]
    ppermute x17, waiting for transfers between devices: 18.6 us -> 17.1 us  [shift(): lax.ppermute(array, axis, [(i, (i + step) % count) for i in range(count)])]
    ppermute x6, waiting for transfers between devices: 7.44 us -> 6.15 us  [flip(): return lax.ppermute(array, axis, [(0, 1), (1, 0)])]
  transfers between devices with their start and end apart: 31 -> 31, of which waited for: 15 -> 16; matrix products, arithmetic and copies ran while one was open for 1% -> 0% of each run, Pallas kernels for 21% -> 21%
where the time goes in v1:
time: 119 us; the launch traced here: 117 us
  starting transfers between devices  47.2 us (40%)
  Pallas kernels  35.4 us (30%)
  waiting for transfers between devices  29.8 us (25%)
  local copies, waits for them, and re-layouts  3.94 us (3%)
    pallas_call x17, Pallas kernels, call(): pl.pallas_call(body, out_shape=tuple((jax.ShapeDtypeStruct(s, d) for s, d...  35.4 us
    ppermute x17, starting transfers between devices, shift(): lax.ppermute(array, axis, [(i, (i + step) % count) for i in range(count)])  29.7 us
    ppermute x17, waiting for transfers between devices, shift(): lax.ppermute(array, axis, [(i, (i + step) % count) for i in range(count)])  17.1 us
    ppermute x6, waiting for transfers between devices, flip(): return lax.ppermute(array, axis, [(0, 1), (1, 0)])  6.15 us
    ppermute x2, starting transfers between devices, halo(): lax.ppermute(rows[:width], SEQ, [(i + 1, i) for i in range(nseq - 1)])  4.94 us
    ppermute x3, starting transfers between devices, local(): got.append(lax.ppermute(send, ('xh', 'xl'), way))  4.79 us
    ppermute x2, starting transfers between devices, halo(): lax.ppermute(rows[-width:], SEQ, [(i, i + 1) for i in range(nseq - 1)])  4.33 us
    ppermute x2, waiting for transfers between devices, halo(): lax.ppermute(rows[-width:], SEQ, [(i, i + 1) for i in range(nseq - 1)])  3.76 us
  transfers between devices with their start and end apart: 31, of which 16 were waited for; matrix products, arithmetic and copies ran while one was open for 0% of the time, Pallas kernels for 21%

profile of v1, /device:TPU:24, one launch (start us, length us, event | category | flops | bytes accessed | tf_op | source)
XLA Modules:
  0.0 117.4 jit_solution(17315938665601836665)
XLA Ops:
  0.6 1.0 slice_bitcast_fusion
  1.6 3.0 %collective-permute-start.1 = (bf16[32,1536]{1,0:T(8,128)(2,1)S(1)}, bf16[32,1536]{1,0:T(8,128)(2,1)S(1)}, u32[]{:S(2)}, u32[]{:S(2)}) collective-permute-start(bf16[32,1536]{1,0:T(8,128)(2,1)S(1)} %get-tuple-element.155), channel_id=1, source_target_pairs={{1,0},{2,1},{3,2},{4,3},{5,4},{6,5},{7,6},{8,7},{9,8},{10,9},{11,1... | collective-permute-start | bytes 294920 | tf_op jit(solution)/shard_map/ppermute | solution.py:538
  4.6 1.9 %collective-permute-start = (bf16[32,1536]{1,0:T(8,128)(2,1)S(1)}, bf16[32,1536]{1,0:T(8,128)(2,1)S(1)}, u32[]{:S(2)}, u32[]{:S(2)}) collective-permute-start(bf16[32,1536]{1,0:T(8,128)(2,1)S(1)} %get-tuple-element.156), channel_id=1, source_target_pairs={{0,1},{1,2},{2,3},{3,4},{4,5},{5,6},{6,7},{7,8},{8,9},{9,10},{10,1... | collective-permute-start | bytes 294920 | tf_op jit(solution)/shard_map/ppermute | solution.py:537
  6.5 4.2 %prelude.1 = (bf16[128,1536]{1,0:T(8,128)(2,1)}, bf16[128,768]{1,0:T(8,128)(2,1)}) custom-call(bf16[128,1536]{1,0:T(8,128)(2,1)} %bitcast.19, f32[3,1536]{1,0:T(4,128)} %gains.7, bf16[128,1536]{1,0:T(8,128)(2,1)} %bitcast.23, bf16[768,1536]{1,0:T(8,128)(2,1)} %w_out.1), custom_call_target="tpu_custom_call" | custom-call | flops 1000 | bytes 10800000 | tf_op jit(solution)/shard_map/prelude/pallas_call | solution.py:39
  10.8 0.6 collective-permute-done.left
  11.5 0.6 copy-done.17
  12.1 5.5 %forward.1 = (bf16[128,512]{1,0:T(8,128)(2,1)}, bf16[128,512]{1,0:T(8,128)(2,1)}, bf16[128,512]{1,0:T(8,128)(2,1)}, bf16[128,512]{1,0:T(8,128)(2,1)}, bf16[128,1...) custom-call(s32[2]{0:T(128)} %dil.3, bf16[32,1536]{1,0:T(8,128)(2,1)} %copy-done.17, ...), custom_call_target="tpu_custom_call" | custom-call | flops 1000 | bytes 18000000 | tf_op jit(solution)/shard_map/forward/pallas_call | solution.py:39
  17.6 0.8 collective-permute-start.2
  18.4 1.8 %collective-permute-start.3 = (bf16[128,512]{1,0:T(8,128)(2,1)}, bf16[128,512]{1,0:T(8,128)(2,1)S(1)}, u32[]{:S(2)}, u32[]{:S(2)}) collective-permute-start(bf16[128,512]{1,0:T(8,128)(2,1)} %get-tuple-element.82), channel_id=1, source_target_pairs={{0,8},{4,12},{8,0},{12,4},{1,9},{5,13},{9,1},{13,5},{2,10},{6,14},... | collective-permute-start | bytes 393224 | tf_op jit(solution)/shard_map/ppermute | solution.py:520
  20.3 1.0 copy-done.9
  21.3 1.6 %shuffle.1 = (bf16[128,768]{1,0:T(8,128)(2,1)S(1)}, bf16[128,768]{1,0:T(8,128)(2,1)S(1)}, bf16[128,768]{1,0:T(8,128)(2,1)S(1)}, bf16[128,768]{1,0:T(8,128)(2,1)S(1)}) custom-call(s32[10]{0:T(128)S(1)} %stack.35.where, s32[1,768]{1,0:T(1,128)S(1)} %copy-done.13, bf16[128,1536]{1,0:T(8,128)(2,1)S(1)} %copy-done.9, bf16[128,1536]{1,0:T(8,128)(2,1)S(1)} %bitcast.24), custom_call_target="tpu_custom_call" | custom-call | flops 1000 | bytes 5760000 | tf_op jit(solution)/shard_map/shuffle/pallas_call | solution.py:39
  22.9 1.4 %collective-permute-done.2.m1 = bf16[128,512]{1,0:T(8,128)(2,1)S(1)} collective-permute-done((bf16[128,512]{1,0:T(8,128)(2,1)}, bf16[128,512]{1,0:T(8,128)(2,1)S(1)}, u32[]{:S(2)}, u32[]{:S(2)}) %collective-permute-start.2) | collective-permute-done | bytes 131104 | tf_op jit(solution)/shard_map/ppermute | solution.py:520
  24.3 2.3 %collective-permute-done.3.m2 = bf16[128,512]{1,0:T(8,128)(2,1)S(1)} collective-permute-done((bf16[128,512]{1,0:T(8,128)(2,1)}, bf16[128,512]{1,0:T(8,128)(2,1)S(1)}, u32[]{:S(2)}, u32[]{:S(2)}) %collective-permute-start.3) | collective-permute-done | bytes 131104 | tf_op jit(solution)/shard_map/ppermute | solution.py:520
  26.5 1.5 %collective-permute-done.4.m3 = bf16[128,512]{1,0:T(8,128)(2,1)S(1)} collective-permute-done((bf16[128,512]{1,0:T(8,128)(2,1)}, bf16[128,512]{1,0:T(8,128)(2,1)S(1)}, u32[]{:S(2)}, u32[]{:S(2)}) %collective-permute-start.4) | collective-permute-done | bytes 131104 | tf_op jit(solution)/shard_map/ppermute | solution.py:520
  28.1 0.8 slice.46
  29.0 0.9 collective-permute-start.6
  29.9 1.1 collective-permute-start.7
  31.0 0.9 collective-permute-start.8
  31.9 1.5 %expand.1.master = f32[128,4096]{1,0:T(8,128)S(1)} custom-call(s32[10]{0:T(128)S(1)} %stack.35.where, f32[4,64]{1,0:T(4,128)S(1)} %bitcast.29, s32[1,4095]{1,0:T(1,128)S(1)} %bitcast.28), custom_call_target="tpu_custom_call" | custom-call | flops 1000 | bytes 5400000 | tf_op jit(solution)/shard_map/expand/pallas_call | solution.py:39
  33.5 3.1 %collective-permute-done.7.f1 = bf16[128,768]{1,0:T(8,128)(2,1)S(1)} collective-permute-done((bf16[128,768]{1,0:T(8,128)(2,1)S(1)}, bf16[128,768]{1,0:T(8,128)(2,1)S(1)}, u32[]{:S(2)}, u32[]{:S(2)}) %collective-permute-start.7) | collective-permute-done | bytes 196640 | tf_op jit(solution)/shard_map/ppermute | solution.py:520
  36.6 2.0 %collective-permute-done.8.f3 = bf16[128,768]{1,0:T(8,128)(2,1)S(1)} collective-permute-done((bf16[128,768]{1,0:T(8,128)(2,1)S(1)}, bf16[128,768]{1,0:T(8,128)(2,1)S(1)}, u32[]{:S(2)}, u32[]{:S(2)}) %collective-permute-start.8) | collective-permute-done | bytes 196640 | tf_op jit(solution)/shard_map/ppermute | solution.py:520
  38.6 0.8 collective-permute-start.10
  39.3 0.8 collective-permute-done.9.kv3
  40.1 6.8 %attend.1 = (bf16[512,256]{1,0:T(8,128)(2,1)S(1)}, f32[512,256]{1,0:T(8,128)S(1)}, f32[512,256]{1,0:T(8,128)S(1)}, bf16[1024,256]{1,0:T(8,128)(2,1)S(1)}) custom-call(s32[10]{0:T(128)S(1)} %stack.35.where, bf16[128,512]{1,0:T(8,128)(2,1)S(1)} %copy-done.10, bf16[128,512]{1,0:T(8,128)(2,1)S(1)} %collective-permute-done.2.m1, ...), custom_call_target="tpu_custom_call" | custom-call | flops 1000 | bytes 25200000 | tf_op jit(solution)/shard_map/attend/pallas_call | solution.py:39
  47.0 0.4 collective-permute-done.10.f2
  47.4 1.9 %collective-permute-done.11.got = bf16[1024,256]{1,0:T(8,128)(2,1)S(1)} collective-permute-done((bf16[1024,256]{1,0:T(8,128)(2,1)S(1)}, bf16[1024,256]{1,0:T(8,128)(2,1)S(1)}, u32[]{:S(2)}, u32[]{:S(2)}) %collective-permute-start.11) | collective-permute-done | bytes 524320 | tf_op jit(solution)/shard_map/ppermute | solution.py:532
  49.3 0.1 first_sum.1
  49.4 0.5 collective-permute-start.12
  49.9 0.3 collective-permute-start.19
  50.2 3.0 %collective-permute-start.17 = (bf16[512,256]{1,0:T(8,128)(2,1)S(1)}, bf16[512,256]{1,0:T(8,128)(2,1)S(1)}, u32[]{:S(2)}, u32[]{:S(2)}) collective-permute-start(bf16[512,256]{1,0:T(8,128)(2,1)S(1)} %get-tuple-element.120.t0), channel_id=1, source_target_pairs={{0,4},{4,8},{8,12},{12,0},{1,5},{5,9},{9,13},{13,1},{2,6},{6,10},{... | collective-permute-start | bytes 786440 | tf_op jit(solution)/shard_map/ppermute | solution.py:520
  53.1 1.3 %slopes.1 = (f32[128,1536]{1,0:T(8,128)S(1)}, f32[160,1536]{1,0:T(8,128)S(1)}) custom-call(bf16[128,1536]{1,0:T(8,128)(2,1)S(1)} %bitcast.21, bf16[160,1536]{1,0:T(8,128)(2,1)S(1)} %copy-done.6, f32[3,1536]{1,0:T(4,128)S(1)} %copy-done.8), custom_call_target="tpu_custom_call" | custom-call | flops 1000 | bytes 36000 | tf_op jit(solution)/shard_map/slopes/pallas_call | solution.py:39
  54.4 3.5 %collective-permute-done.12.got = bf16[512,256]{1,0:T(8,128)(2,1)S(1)} collective-permute-done((bf16[512,256]{1,0:T(8,128)(2,1)S(1)}, bf16[512,256]{1,0:T(8,128)(2,1)S(1)}, u32[]{:S(2)}, u32[]{:S(2)}) %collective-permute-start.12) | collective-permute-done | bytes 262176 | tf_op jit(solution)/shard_map/ppermute | solution.py:532
  57.9 0.6 second_sum.1.d0
  58.5 3.2 %collective-permute-start.13 = (bf16[512,256]{1,0:T(8,128)(2,1)S(1)}, bf16[512,256]{1,0:T(8,128)(2,1)S(1)}, u32[]{:S(2)}, u32[]{:S(2)}) collective-permute-start(bf16[512,256]{1,0:T(8,128)(2,1)S(1)} %second_sum.1.d0), channel_id=1, source_target_pairs={{0,4},{4,8},{8,12},{12,0},{1,5},{5,9},{9,13},{13,1},{2,6},{6,10},{... | collective-permute-start | bytes 786440 | tf_op jit(solution)/shard_map/ppermute | solution.py:520
  61.9 3.3 %collective-permute-start.18 = (bf16[256,256]{1,0:T(8,128)(2,1)S(1)}, bf16[256,256]{1,0:T(8,128)(2,1)S(1)}, u32[]{:S(2)}, u32[]{:S(2)}) collective-permute-start(bf16[256,256]{1,0:T(8,128)(2,1)S(1)} %slice.58), channel_id=1, source_target_pairs={{0,4},{4,8},{8,12},{12,0},{1,5},{5,9},{9,13},{13,1},{2,6},{6,10},{... | collective-permute-start | bytes 393224 | tf_op jit(solution)/shard_map/ppermute | solution.py:520
  65.2 3.5 %collective-permute-done.15.d4 = bf16[512,256]{1,0:T(8,128)(2,1)S(1)} collective-permute-done((bf16[512,256]{1,0:T(8,128)(2,1)S(1)}, bf16[512,256]{1,0:T(8,128)(2,1)S(1)}, u32[]{:S(2)}, u32[]{:S(2)}) %collective-permute-start.15) | collective-permute-done | bytes 262176 | tf_op jit(solution)/shard_map/ppermute | solution.py:520
  68.7 0.3 collective-permute-start.16
  69.0 3.3 %collective-permute-start.14 = (bf16[256,256]{1,0:T(8,128)(2,1)S(1)}, bf16[256,256]{1,0:T(8,128)(2,1)S(1)}, u32[]{:S(2)}, u32[]{:S(2)}) collective-permute-start(bf16[256,256]{1,0:T(8,128)(2,1)S(1)} %slice.56), channel_id=1, source_target_pairs={{0,4},{4,8},{8,12},{12,0},{1,5},{5,9},{9,13},{13,1},{2,6},{6,10},{... | collective-permute-start | bytes 393224 | tf_op jit(solution)/shard_map/ppermute | solution.py:520
  72.3 1.9 %project.1 = (bf16[128,1536]{1,0:T(8,128)(2,1)}, f32[128,1536]{1,0:T(8,128)S(1)}) custom-call(s32[10]{0:T(128)S(1)} %stack.35.where, bf16[512,256]{1,0:T(8,128)(2,1)S(1)} %get-tuple-element.120.t0, bf16[512,256]{1,0:T(8,128)(2,1)S(1)} %collective-permute-done.17.t1, bf16[256,256]{1,0:T(8,128)(2,1)S(1)} %collective-permute-done.18.t2, ...), custom_call_target="tpu_custom_call" | custom-call | flops 1000 | bytes 7200000 | tf_op jit(solution)/shard_map/project/pallas_call | solution.py:39
  74.2 1.7 %weigh_first.1.before = f32[2,4,192,256]{3,2,1,0:T(8,128)S(1)} custom-call(s32[10]{0:T(128)S(1)} %stack.35.where, bf16[128,768]{1,0:T(8,128)(2,1)S(1)} %get-tuple-element.116.f0, bf16[128,768]{1,0:T(8,128)(2,1)S(1)} %collective-permute-done.7.f1, bf16[128,768]{1,0:T(8,128)(2,1)S(1)} %collective-permute-done.10.f2, ...), custom_call_target="tpu_custom_call" | custom-call | flops 1000 | bytes 7200000 | tf_op jit(solution)/shard_map/weigh_first/pallas_call | solution.py:39
  75.9 1.4 %weigh_second.1 = (f32[4,192,512]{2,1,0:T(8,128)S(1)}, bf16[4,192,512]{2,1,0:T(8,128)(2,1)S(1)}) custom-call(s32[10]{0:T(128)S(1)} %stack.35.where, bf16[128,768]{1,0:T(8,128)(2,1)S(1)} %get-tuple-element.116.f0, bf16[128,768]{1,0:T(8,128)(2,1)S(1)} %collective-permute-done.7.f1, bf16[128,768]{1,0:T(8,128)(2,1)S(1)} %collective-permute-done.10.f2, ...), custom_call_target="tpu_custom_call" | custom-call | flops 1000 | bytes 5400000 | tf_op jit(solution)/shard_map/weigh_second/pallas_call | solution.py:39
  77.3 0.1 collective-permute-start.23
  77.4 0.1 copy-done.1
  77.6 0.2 copy-done.5
  77.7 2.1 %grad_top.1.grad = bf16[128,1536]{1,0:T(8,128)(2,1)S(1)} custom-call(s32[10]{0:T(128)S(1)} %stack.35.where, bf16[512,256]{1,0:T(8,128)(2,1)S(1)} %second_sum.1.d0, bf16[512,256]{1,0:T(8,128)(2,1)S(1)} %collective-permute-done.13.d1, bf16[256,256]{1,0:T(8,128)(2,1)S(1)} %collective-permute-done.14.d2, bf16[256,256]{1,0:T(8,128)(2,1)S(1)} %collective-permute-done.16.d3, ...), custom_call_target="tpu_custom_call" | custom-call | flops 1000 | bytes 10800000 | tf_op jit(solution)/shard_map/grad_top/pallas_call | solution.py:39
  79.9 0.8 fold.2
  80.7 0.5 collective-permute-start.24
  81.2 2.7 %collective-permute-start.25 = (bf16[4,48,512]{2,1,0:T(8,128)(2,1)S(1)}, bf16[4,48,512]{2,1,0:T(8,128)(2,1)S(1)}, u32[]{:S(2)}, u32[]{:S(2)}) collective-permute-start(bf16[4,48,512]{2,1,0:T(8,128)(2,1)S(1)} %get-tuple-element.135), channel_id=1, source_target_pairs={{0,128},{2,130},{128,0},{130,2},{1,129},{3,131},{129,1},{131,3},{4... | collective-permute-start | bytes 589832 | tf_op jit(solution)/shard_map/ppermute | solution.py:689
  83.9 1.6 %collective-permute-start.26 = (bf16[4,48,512]{2,1,0:T(8,128)(2,1)S(1)}, bf16[4,48,512]{2,1,0:T(8,128)(2,1)S(1)}, u32[]{:S(2)}, u32[]{:S(2)}) collective-permute-start(bf16[4,48,512]{2,1,0:T(8,128)(2,1)S(1)} %get-tuple-element.136), channel_id=1, source_target_pairs={{0,130},{2,128},{128,2},{130,0},{1,131},{3,129},{129,3},{131,1},{4... | collective-permute-start | bytes 589832 | tf_op jit(solution)/shard_map/ppermute | solution.py:689
  85.5 1.9 %collective-permute-start.22 = (bf16[32,1536]{1,0:T(8,128)(2,1)S(1)}, bf16[32,1536]{1,0:T(8,128)(2,1)S(1)}, u32[]{:S(2)}, u32[]{:S(2)}) collective-permute-start(bf16[32,1536]{1,0:T(8,128)(2,1)S(1)} %get-tuple-element.153), channel_id=1, source_target_pairs={{1,0},{2,1},{3,2},{4,3},{5,4},{6,5},{7,6},{8,7},{9,8},{10,9},{11,1... | collective-permute-start | bytes 294920 | tf_op jit(solution)/shard_map/ppermute | solution.py:538
  87.5 2.4 %collective-permute-start.21 = (bf16[32,1536]{1,0:T(8,128)(2,1)S(1)}, bf16[32,1536]{1,0:T(8,128)(2,1)S(1)}, u32[]{:S(2)}, u32[]{:S(2)}) collective-permute-start(bf16[32,1536]{1,0:T(8,128)(2,1)S(1)} %get-tuple-element.154), channel_id=1, source_target_pairs={{0,1},{1,2},{2,3},{3,4},{4,5},{5,6},{6,7},{7,8},{8,9},{9,10},{10,1... | collective-permute-start | bytes 294920 | tf_op jit(solution)/shard_map/ppermute | solution.py:537
  89.9 1.3 %collective-permute-done.22.right = bf16[32,1536]{1,0:T(8,128)(2,1)S(1)} collective-permute-done((bf16[32,1536]{1,0:T(8,128)(2,1)S(1)}, bf16[32,1536]{1,0:T(8,128)(2,1)S(1)}, u32[]{:S(2)}, u32[]{:S(2)}) %collective-permute-start.22) | collective-permute-done | bytes 98336 | tf_op jit(solution)/shard_map/ppermute | solution.py:538
  91.2 3.1 %collective-permute-done.21.left = bf16[32,1536]{1,0:T(8,128)(2,1)S(1)} collective-permute-done((bf16[32,1536]{1,0:T(8,128)(2,1)S(1)}, bf16[32,1536]{1,0:T(8,128)(2,1)S(1)}, u32[]{:S(2)}, u32[]{:S(2)}) %collective-permute-start.21) | collective-permute-done | bytes 98336 | tf_op jit(solution)/shard_map/ppermute | solution.py:537
  94.3 1.5 %collective-permute-done.26.refs_2_ = bf16[4,48,512]{2,1,0:T(8,128)(2,1)S(1)} collective-permute-done((bf16[4,48,512]{2,1,0:T(8,128)(2,1)S(1)}, bf16[4,48,512]{2,1,0:T(8,128)(2,1)S(1)}, u32[]{:S(2)}, u32[]{:S(2)}) %collective-permute-start.26) | collective-permute-done | bytes 196640 | tf_op jit(solution)/shard_map/ppermute | solution.py:689
  95.8 0.7 fold.3
  96.5 2.0 %collective-permute-start.27 = (bf16[4,24,512]{2,1,0:T(8,128)(2,1)S(1)}, bf16[4,24,512]{2,1,0:T(8,128)(2,1)S(1)}, u32[]{:S(2)}, u32[]{:S(2)}) collective-permute-start(bf16[4,24,512]{2,1,0:T(8,128)(2,1)S(1)} %get-tuple-element.145), channel_id=1, source_target_pairs={{0,16},{16,0},{32,48},{48,32},{64,80},{80,64},{96,112},{112,96},{1... | collective-permute-start | bytes 294920 | tf_op jit(solution)/shard_map/ppermute | solution.py:695
  98.5 3.3 %backward.1 = bf16[128,1536]{1,0:T(8,128)(2,1)} custom-call(s32[10]{0:T(128)S(1)} %stack.35.where, s32[2]{0:T(128)S(1)} %copy-done.14, bf16[32,1536]{1,0:T(8,128)(2,1)S(1)} %collective-permute-done.21.left, bf16[32,1536]{1,0:T(8,128)(2,1)S(1)} %collective-permute-done.22.right, bf16[128,1536]{1,0:T(8,128)(2,1)S(1)} %grad_top.1.grad, ...), custom_call_target="tpu_custom_call" | custom-call | flops 1000 | bytes 16559999 | tf_op jit(solution)/shard_map/backward/pallas_call | solution.py:39
  101.8 0.6 last_fold.1
  102.4 6.7 %collective-permute-start.28 = (f32[4,6,512]{2,1,0:T(8,128)S(1)}, f32[4,6,512]{2,1,0:T(8,128)S(1)}, u32[]{:S(2)}, u32[]{:S(2)}) collective-permute-start(f32[4,6,512]{2,1,0:T(8,128)S(1)} %get-tuple-element.150), channel_id=1, source_target_pairs={{0,64},{16,80},{32,96},{48,112},{64,0},{80,16},{96,32},{112,48},{1... | collective-permute-start | bytes 147464 | tf_op jit(solution)/shard_map/ppermute | solution.py:520
  109.1 1.5 %collective-permute-start.29 = (f32[4,6,512]{2,1,0:T(8,128)S(1)}, f32[4,6,512]{2,1,0:T(8,128)S(1)}, u32[]{:S(2)}, u32[]{:S(2)}) collective-permute-start(f32[4,6,512]{2,1,0:T(8,128)S(1)} %get-tuple-element.151), channel_id=1, source_target_pairs={{0,32},{16,48},{32,64},{48,80},{64,96},{80,112},{96,0},{112,16},{1... | collective-permute-start | bytes 147464 | tf_op jit(solution)/shard_map/ppermute | solution.py:520
  110.6 2.7 %collective-permute-start.30 = (f32[4,6,512]{2,1,0:T(8,128)S(1)}, f32[4,6,512]{2,1,0:T(8,128)S(1)}, u32[]{:S(2)}, u32[]{:S(2)}) collective-permute-start(f32[4,6,512]{2,1,0:T(8,128)S(1)} %get-tuple-element.152), channel_id=1, source_target_pairs={{0,96},{16,112},{32,0},{48,16},{64,32},{80,48},{96,64},{112,80},{1... | collective-permute-start | bytes 147464 | tf_op jit(solution)/shard_map/ppermute | solution.py:520
  113.2 2.4 %collective-permute-done.29.refs_2_ = f32[4,6,512]{2,1,0:T(8,128)S(1)} collective-permute-done((f32[4,6,512]{2,1,0:T(8,128)S(1)}, f32[4,6,512]{2,1,0:T(8,128)S(1)}, u32[]{:S(2)}, u32[]{:S(2)}) %collective-permute-start.29) | collective-permute-done | bytes 49184 | tf_op jit(solution)/shard_map/ppermute | solution.py:520
  115.6 0.5 collective-permute-done.30.refs_3_
  116.1 1.3 %arrange.1 = f32[6,2048]{1,0:T(8,128)} custom-call(s32[10]{0:T(128)S(1)} %stack.35.where, f32[4,6,512]{2,1,0:T(8,128)S(1)} %get-tuple-element.149.refs_0_, f32[4,6,512]{2,1,0:T(8,128)S(1)} %collective-permute-done.28.refs_1_, f32[4,6,512]{2,1,0:T(8,128)S(1)} %collective-permute-done.29.refs_2_, f32[4,6,512]{2,1,0:T(8,128)S(1)} %collective-permute-done.30.refs_3_), custom_call_target="tpu_custom_call" | custom-call | flops 1000 | bytes 3600000 | tf_op jit(solution)/shard_map/arrange/pallas_call | solution.py:39
  (63 shorter events, 0.5 us)
Async XLA Ops:
  1.6 9.2 %collective-permute-start.1 = (bf16[32,1536]{1,0:T(8,128)(2,1)S(1)}, bf16[32,1536]{1,0:T(8,128)(2,1)S(1)}, u32[]{:S(2)}, u32[]{:S(2)}) collective-permute-start(bf16[32,1536]{1,0:T(8,128)(2,1)S(1)} %get-tuple-element.155), channel_id=1, source_target_pairs={{1,0},{2,1},{3,2},{4,3},{5,4},{6,5},{7,6},{8,7},{9,8},{10,9},{11,1... | collective-permute-start | bytes 294920 | tf_op jit(solution)/shard_map/ppermute | solution.py:538
  4.6 6.8 %collective-permute-start = (bf16[32,1536]{1,0:T(8,128)(2,1)S(1)}, bf16[32,1536]{1,0:T(8,128)(2,1)S(1)}, u32[]{:S(2)}, u32[]{:S(2)}) collective-permute-start(bf16[32,1536]{1,0:T(8,128)(2,1)S(1)} %get-tuple-element.156), channel_id=1, source_target_pairs={{0,1},{1,2},{2,3},{3,4},{4,5},{5,6},{6,7},{7,8},{8,9},{9,10},{10,1... | collective-permute-start | bytes 294920 | tf_op jit(solution)/shard_map/ppermute | solution.py:537
  10.8 0.7 copy-start.16
  11.4 0.6 copy-start.17
  12.1 8.2 %copy-start.3 = (bf16[1,128,1536]{2,1,0:T(8,128)(2,1)S(1)}, bf16[1,128,1536]{2,1,0:T(8,128)(2,1)}, u32[]{:S(2)}) copy-start(bf16[1,128,1536]{2,1,0:T(8,128)(2,1)} %param.22) | copy-start | bytes 1179652
  12.1 8.2 %copy-start.13 = (s32[1,768]{1,0:T(1,128)S(1)}, s32[1,768]{1,0:T(1,128)}, u32[]{:S(2)}) copy-start(s32[1,768]{1,0:T(1,128)} %constant.50.clone.order) | copy-start | bytes 9220
  12.1 19.9 %copy-start.12 = (s32[4095]{0:T(1024)S(1)}, s32[4095]{0:T(1024)}, u32[]{:S(2)}) copy-start(s32[4095]{0:T(1024)} %param.17) | copy-start | bytes 49144
  12.1 19.9 %copy-start.15 = (f32[64,4]{0,1:T(4,128)S(1)}, f32[64,4]{0,1:T(4,128)}, u32[]{:S(2)}) copy-start(f32[64,4]{0,1:T(4,128)} %param.16) | copy-start | bytes 3076
  17.6 6.7 %collective-permute-start.2 = (bf16[128,512]{1,0:T(8,128)(2,1)}, bf16[128,512]{1,0:T(8,128)(2,1)S(1)}, u32[]{:S(2)}, u32[]{:S(2)}) collective-permute-start(bf16[128,512]{1,0:T(8,128)(2,1)} %get-tuple-element.81), channel_id=1, source_target_pairs={{0,4},{4,8},{8,12},{12,0},{1,5},{5,9},{9,13},{13,1},{2,6},{6,10},{... | collective-permute-start | bytes 393224 | tf_op jit(solution)/shard_map/ppermute | solution.py:520
  18.4 8.1 %collective-permute-start.3 = (bf16[128,512]{1,0:T(8,128)(2,1)}, bf16[128,512]{1,0:T(8,128)(2,1)S(1)}, u32[]{:S(2)}, u32[]{:S(2)}) collective-permute-start(bf16[128,512]{1,0:T(8,128)(2,1)} %get-tuple-element.82), channel_id=1, source_target_pairs={{0,8},{4,12},{8,0},{12,4},{1,9},{5,13},{9,1},{13,5},{2,10},{6,14},... | collective-permute-start | bytes 393224 | tf_op jit(solution)/shard_map/ppermute | solution.py:520
  20.2 7.9 %collective-permute-start.4 = (bf16[128,512]{1,0:T(8,128)(2,1)}, bf16[128,512]{1,0:T(8,128)(2,1)S(1)}, u32[]{:S(2)}, u32[]{:S(2)}) collective-permute-start(bf16[128,512]{1,0:T(8,128)(2,1)} %get-tuple-element.83), channel_id=1, source_target_pairs={{0,12},{4,0},{8,4},{12,8},{1,13},{5,1},{9,5},{13,9},{2,14},{6,2},{... | collective-permute-start | bytes 393224 | tf_op jit(solution)/shard_map/ppermute | solution.py:520
  20.3 1.0 copy-start.9
  21.3 18.8 %copy-start.10 = (bf16[128,512]{1,0:T(8,128)(2,1)S(1)}, bf16[128,512]{1,0:T(8,128)(2,1)}, u32[]{:S(2)}) copy-start(bf16[128,512]{1,0:T(8,128)(2,1)} %get-tuple-element.89.m0) | copy-start | bytes 393220
  29.0 9.6 %collective-permute-start.6 = (bf16[512,256]{1,0:T(8,128)(2,1)S(1)}, bf16[512,256]{1,0:T(8,128)(2,1)S(1)}, u32[]{:S(2)}, u32[]{:S(2)}) collective-permute-start(bf16[512,256]{1,0:T(8,128)(2,1)S(1)} %pad_maximum_fusion), channel_id=1, source_target_pairs={{0,2},{2,0},{1,3},{3,1},{4,6},{6,4},{5,7},{7,5},{8,10},{10,8},{9,1... | collective-permute-start | bytes 786440 | tf_op jit(solution)/shard_map/ppermute | solution.py:532
  29.9 6.6 %collective-permute-start.7 = (bf16[128,768]{1,0:T(8,128)(2,1)S(1)}, bf16[128,768]{1,0:T(8,128)(2,1)S(1)}, u32[]{:S(2)}, u32[]{:S(2)}) collective-permute-start(bf16[128,768]{1,0:T(8,128)(2,1)S(1)} %get-tuple-element.93), channel_id=1, source_target_pairs={{0,4},{4,8},{8,12},{12,0},{1,5},{5,9},{9,13},{13,1},{2,6},{6,10},{... | collective-permute-start | bytes 589832 | tf_op jit(solution)/shard_map/ppermute | solution.py:520
  31.0 7.6 %collective-permute-start.8 = (bf16[128,768]{1,0:T(8,128)(2,1)S(1)}, bf16[128,768]{1,0:T(8,128)(2,1)S(1)}, u32[]{:S(2)}, u32[]{:S(2)}) collective-permute-start(bf16[128,768]{1,0:T(8,128)(2,1)S(1)} %get-tuple-element.94), channel_id=1, source_target_pairs={{0,12},{4,0},{8,4},{12,8},{1,13},{5,1},{9,5},{13,9},{2,14},{6,2},{... | collective-permute-start | bytes 589832 | tf_op jit(solution)/shard_map/ppermute | solution.py:520
  31.9 7.4 %collective-permute-start.5 = (bf16[512,256]{1,0:T(8,128)(2,1)S(1)}, bf16[512,256]{1,0:T(8,128)(2,1)S(1)}, u32[]{:S(2)}, u32[]{:S(2)}) collective-permute-start(bf16[512,256]{1,0:T(8,128)(2,1)S(1)} %pad_maximum_fusion), channel_id=1, source_target_pairs={{0,1},{1,0},{2,3},{3,2},{4,5},{5,4},{6,7},{7,6},{8,9},{9,8},{10,11... | collective-permute-start | bytes 786440 | tf_op jit(solution)/shard_map/ppermute | solution.py:532
  33.4 19.7 %copy-start.2 = (bf16[1,128,1536]{2,1,0:T(8,128)(2,1)S(1)}, bf16[1,128,1536]{2,1,0:T(8,128)(2,1)}, u32[]{:S(2)}) copy-start(bf16[1,128,1536]{2,1,0:T(8,128)(2,1)} %param.12) | copy-start | bytes 1179652
  33.5 19.7 %copy-start.6 = (bf16[160,1536]{1,0:T(8,128)(2,1)S(1)}, bf16[160,1536]{1,0:T(8,128)(2,1)}, u32[]{:S(2)}) copy-start(bf16[160,1536]{1,0:T(8,128)(2,1)} %get-tuple-element.112.near) | copy-start | bytes 1474564
  33.5 19.7 %copy-start.8 = (f32[3,1536]{1,0:T(4,128)S(1)}, f32[3,1536]{1,0:T(4,128)}, u32[]{:S(2)}) copy-start(f32[3,1536]{1,0:T(4,128)} %gains.7) | copy-start | bytes 55300
  38.6 1.5 %collective-permute-start.9 = (bf16[512,256]{1,0:T(8,128)(2,1)S(1)}, bf16[512,256]{1,0:T(8,128)(2,1)S(1)}, u32[]{:S(2)}, u32[]{:S(2)}) collective-permute-start(bf16[512,256]{1,0:T(8,128)(2,1)S(1)} %collective-permute-done.6.kv2), channel_id=1, source_target_pairs={{0,1},{1,0},{2,3},{3,2},{4,5},{5,4},{6,7},{7,6},{8,9},{9,8},{10,11... | collective-permute-start | bytes 786440 | tf_op jit(solution)/shard_map/ppermute | solution.py:532
  38.6 8.8 %collective-permute-start.10 = (bf16[128,768]{1,0:T(8,128)(2,1)S(1)}, bf16[128,768]{1,0:T(8,128)(2,1)S(1)}, u32[]{:S(2)}, u32[]{:S(2)}) collective-permute-start(bf16[128,768]{1,0:T(8,128)(2,1)S(1)} %get-tuple-element.103), channel_id=1, source_target_pairs={{0,8},{4,12},{8,0},{12,4},{1,9},{5,13},{9,1},{13,5},{2,10},{6,14},... | collective-permute-start | bytes 589832 | tf_op jit(solution)/shard_map/ppermute | solution.py:520
  47.4 1.9 %collective-permute-start.11 = (bf16[1024,256]{1,0:T(8,128)(2,1)S(1)}, bf16[1024,256]{1,0:T(8,128)(2,1)S(1)}, u32[]{:S(2)}, u32[]{:S(2)}) collective-permute-start(bf16[1024,256]{1,0:T(8,128)(2,1)S(1)} %get-tuple-element.105), channel_id=1, source_target_pairs={{0,1},{1,0},{2,3},{3,2},{4,5},{5,4},{6,7},{7,6},{8,9},{9,8},{10,11... | collective-permute-start | bytes 1572872 | tf_op jit(solution)/shard_map/ppermute | solution.py:532
  49.3 23.0 %copy-start = (bf16[768,1536]{1,0:T(8,128)(2,1)S(1)}, bf16[768,1536]{1,0:T(8,128)(2,1)}, u32[]{:S(2)}) copy-start(bf16[768,1536]{1,0:T(8,128)(2,1)} %w_out.1) | copy-start | bytes 7077892
  49.3 23.0 %copy-start.4 = (bf16[1536,256]{1,0:T(8,128)(2,1)S(1)}, bf16[1536,256]{1,0:T(8,128)(2,1)}, u32[]{:S(2)}) copy-start(bf16[1536,256]{1,0:T(8,128)(2,1)} %w_query.1) | copy-start | bytes 2359300
  49.3 23.0 %copy-start.7 = (bf16[128,1536]{1,0:T(8,128)(2,1)S(1)}, bf16[128,1536]{1,0:T(8,128)(2,1)}, u32[]{:S(2)}) copy-start(bf16[128,1536]{1,0:T(8,128)(2,1)} %get-tuple-element.121.z) | copy-start | bytes 1179652
  49.4 8.4 %collective-permute-start.12 = (bf16[512,256]{1,0:T(8,128)(2,1)S(1)}, bf16[512,256]{1,0:T(8,128)(2,1)S(1)}, u32[]{:S(2)}, u32[]{:S(2)}) collective-permute-start(bf16[512,256]{1,0:T(8,128)(2,1)S(1)} %get-tuple-element.110), channel_id=1, source_target_pairs={{0,2},{2,0},{1,3},{3,1},{4,6},{6,4},{5,7},{7,5},{8,10},{10,8},{9,1... | collective-permute-start | bytes 786440 | tf_op jit(solution)/shard_map/ppermute | solution.py:532
  49.9 11.9 %collective-permute-start.19 = (bf16[512,256]{1,0:T(8,128)(2,1)S(1)}, bf16[512,256]{1,0:T(8,128)(2,1)S(1)}, u32[]{:S(2)}, u32[]{:S(2)}) collective-permute-start(bf16[512,256]{1,0:T(8,128)(2,1)S(1)} %get-tuple-element.120.t0), channel_id=1, source_target_pairs={{0,12},{4,0},{8,4},{12,8},{1,13},{5,1},{9,5},{13,9},{2,14},{6,2},{... | collective-permute-start | bytes 786440 | tf_op jit(solution)/shard_map/ppermute | solution.py:520
  50.2 11.7 %collective-permute-start.17 = (bf16[512,256]{1,0:T(8,128)(2,1)S(1)}, bf16[512,256]{1,0:T(8,128)(2,1)S(1)}, u32[]{:S(2)}, u32[]{:S(2)}) collective-permute-start(bf16[512,256]{1,0:T(8,128)(2,1)S(1)} %get-tuple-element.120.t0), channel_id=1, source_target_pairs={{0,4},{4,8},{8,12},{12,0},{1,5},{5,9},{9,13},{13,1},{2,6},{6,10},{... | collective-permute-start | bytes 786440 | tf_op jit(solution)/shard_map/ppermute | solution.py:520
  58.5 10.2 %collective-permute-start.15 = (bf16[512,256]{1,0:T(8,128)(2,1)S(1)}, bf16[512,256]{1,0:T(8,128)(2,1)S(1)}, u32[]{:S(2)}, u32[]{:S(2)}) collective-permute-start(bf16[512,256]{1,0:T(8,128)(2,1)S(1)} %second_sum.1.d0), channel_id=1, source_target_pairs={{0,12},{4,0},{8,4},{12,8},{1,13},{5,1},{9,5},{13,9},{2,14},{6,2},{... | collective-permute-start | bytes 786440 | tf_op jit(solution)/shard_map/ppermute | solution.py:520
  58.5 10.4 %collective-permute-start.13 = (bf16[512,256]{1,0:T(8,128)(2,1)S(1)}, bf16[512,256]{1,0:T(8,128)(2,1)S(1)}, u32[]{:S(2)}, u32[]{:S(2)}) collective-permute-start(bf16[512,256]{1,0:T(8,128)(2,1)S(1)} %second_sum.1.d0), channel_id=1, source_target_pairs={{0,4},{4,8},{8,12},{12,0},{1,5},{5,9},{9,13},{13,1},{2,6},{6,10},{... | collective-permute-start | bytes 786440 | tf_op jit(solution)/shard_map/ppermute | solution.py:520
  61.8 10.5 %collective-permute-start.20 = (bf16[256,256]{1,0:T(8,128)(2,1)S(1)}, bf16[256,256]{1,0:T(8,128)(2,1)S(1)}, u32[]{:S(2)}, u32[]{:S(2)}) collective-permute-start(bf16[256,256]{1,0:T(8,128)(2,1)S(1)} %slice.59), channel_id=1, source_target_pairs={{0,12},{4,0},{8,4},{12,8},{1,13},{5,1},{9,5},{13,9},{2,14},{6,2},{... | collective-permute-start | bytes 393224 | tf_op jit(solution)/shard_map/ppermute | solution.py:520
  61.9 10.4 %collective-permute-start.18 = (bf16[256,256]{1,0:T(8,128)(2,1)S(1)}, bf16[256,256]{1,0:T(8,128)(2,1)S(1)}, u32[]{:S(2)}, u32[]{:S(2)}) collective-permute-start(bf16[256,256]{1,0:T(8,128)(2,1)S(1)} %slice.58), channel_id=1, source_target_pairs={{0,4},{4,8},{8,12},{12,0},{1,5},{5,9},{9,13},{13,1},{2,6},{6,10},{... | collective-permute-start | bytes 393224 | tf_op jit(solution)/shard_map/ppermute | solution.py:520
  68.7 7.2 %collective-permute-start.16 = (bf16[256,256]{1,0:T(8,128)(2,1)S(1)}, bf16[256,256]{1,0:T(8,128)(2,1)S(1)}, u32[]{:S(2)}, u32[]{:S(2)}) collective-permute-start(bf16[256,256]{1,0:T(8,128)(2,1)S(1)} %slice.57), channel_id=1, source_target_pairs={{0,12},{4,0},{8,4},{12,8},{1,13},{5,1},{9,5},{13,9},{2,14},{6,2},{... | collective-permute-start | bytes 393224 | tf_op jit(solution)/shard_map/ppermute | solution.py:520
  69.0 6.9 %collective-permute-start.14 = (bf16[256,256]{1,0:T(8,128)(2,1)S(1)}, bf16[256,256]{1,0:T(8,128)(2,1)S(1)}, u32[]{:S(2)}, u32[]{:S(2)}) collective-permute-start(bf16[256,256]{1,0:T(8,128)(2,1)S(1)} %slice.56), channel_id=1, source_target_pairs={{0,4},{4,8},{8,12},{12,0},{1,5},{5,9},{9,13},{13,1},{2,6},{6,10},{... | collective-permute-start | bytes 393224 | tf_op jit(solution)/shard_map/ppermute | solution.py:520
  75.9 1.7 %copy-start.1 = (bf16[1536,768]{1,0:T(8,128)(2,1)S(1)}, bf16[1536,768]{1,0:T(8,128)(2,1)}, u32[]{:S(2)}) copy-start(bf16[1536,768]{1,0:T(8,128)(2,1)} %w_value.1) | copy-start | bytes 7077892
  75.9 1.8 %copy-start.5 = (bf16[1536,256]{1,0:T(8,128)(2,1)S(1)}, bf16[1536,256]{1,0:T(8,128)(2,1)}, u32[]{:S(2)}) copy-start(bf16[1536,256]{1,0:T(8,128)(2,1)} %w_key.1) | copy-start | bytes 2359300
  77.3 2.5 %collective-permute-start.23 = (bf16[4,192,512]{2,1,0:T(8,128)(2,1)S(1)}, bf16[4,192,512]{2,1,0:T(8,128)(2,1)S(1)}, u32[]{:S(2)}, u32[]{:S(2)}) collective-permute-start(bf16[4,192,512]{2,1,0:T(8,128)(2,1)S(1)} %get-tuple-element.133), channel_id=1, source_target_pairs={{0,1},{1,0},{2,3},{3,2},{4,5},{5,4},{6,7},{7,6},{8,9},{9,8},{10,11... | collective-permute-start | bytes 2359304 | tf_op jit(solution)/shard_map/ppermute | solution.py:532
  79.9 18.6 %copy-start.11 = (f32[2,3,1536]{2,0,1:T(2,128)S(1)}, f32[2,3,1536]{2,0,1:T(2,128)}, u32[]{:S(2)}) copy-start(f32[2,3,1536]{2,0,1:T(2,128)} %param.14) | copy-start | bytes 110596
  79.9 18.6 %copy-start.14 = (s32[2]{0:T(128)S(1)}, s32[2]{0:T(128)}, u32[]{:S(2)}) copy-start(s32[2]{0:T(128)} %dil.3) | copy-start | bytes 28
  80.7 13.6 %collective-permute-start.24 = (bf16[4,48,512]{2,1,0:T(8,128)(2,1)S(1)}, bf16[4,48,512]{2,1,0:T(8,128)(2,1)S(1)}, u32[]{:S(2)}, u32[]{:S(2)}) collective-permute-start(bf16[4,48,512]{2,1,0:T(8,128)(2,1)S(1)} %get-tuple-element.134), channel_id=1, source_target_pairs={{0,2},{2,0},{128,130},{130,128},{1,3},{3,1},{129,131},{131,129},{4... | collective-permute-start | bytes 589832 | tf_op jit(solution)/shard_map/ppermute | solution.py:689
  81.2 13.1 %collective-permute-start.25 = (bf16[4,48,512]{2,1,0:T(8,128)(2,1)S(1)}, bf16[4,48,512]{2,1,0:T(8,128)(2,1)S(1)}, u32[]{:S(2)}, u32[]{:S(2)}) collective-permute-start(bf16[4,48,512]{2,1,0:T(8,128)(2,1)S(1)} %get-tuple-element.135), channel_id=1, source_target_pairs={{0,128},{2,130},{128,0},{130,2},{1,129},{3,131},{129,1},{131,3},{4... | collective-permute-start | bytes 589832 | tf_op jit(solution)/shard_map/ppermute | solution.py:689
  83.9 11.9 %collective-permute-start.26 = (bf16[4,48,512]{2,1,0:T(8,128)(2,1)S(1)}, bf16[4,48,512]{2,1,0:T(8,128)(2,1)S(1)}, u32[]{:S(2)}, u32[]{:S(2)}) collective-permute-start(bf16[4,48,512]{2,1,0:T(8,128)(2,1)S(1)} %get-tuple-element.136), channel_id=1, source_target_pairs={{0,130},{2,128},{128,2},{130,0},{1,131},{3,129},{129,3},{131,1},{4... | collective-permute-start | bytes 589832 | tf_op jit(solution)/shard_map/ppermute | solution.py:689
  85.5 5.6 %collective-permute-start.22 = (bf16[32,1536]{1,0:T(8,128)(2,1)S(1)}, bf16[32,1536]{1,0:T(8,128)(2,1)S(1)}, u32[]{:S(2)}, u32[]{:S(2)}) collective-permute-start(bf16[32,1536]{1,0:T(8,128)(2,1)S(1)} %get-tuple-element.153), channel_id=1, source_target_pairs={{1,0},{2,1},{3,2},{4,3},{5,4},{6,5},{7,6},{8,7},{9,8},{10,9},{11,1... | collective-permute-start | bytes 294920 | tf_op jit(solution)/shard_map/ppermute | solution.py:538
  87.5 6.8 %collective-permute-start.21 = (bf16[32,1536]{1,0:T(8,128)(2,1)S(1)}, bf16[32,1536]{1,0:T(8,128)(2,1)S(1)}, u32[]{:S(2)}, u32[]{:S(2)}) collective-permute-start(bf16[32,1536]{1,0:T(8,128)(2,1)S(1)} %get-tuple-element.154), channel_id=1, source_target_pairs={{0,1},{1,2},{2,3},{3,4},{4,5},{5,6},{6,7},{7,8},{8,9},{9,10},{10,1... | collective-permute-start | bytes 294920 | tf_op jit(solution)/shard_map/ppermute | solution.py:537
  96.5 5.3 %collective-permute-start.27 = (bf16[4,24,512]{2,1,0:T(8,128)(2,1)S(1)}, bf16[4,24,512]{2,1,0:T(8,128)(2,1)S(1)}, u32[]{:S(2)}, u32[]{:S(2)}) collective-permute-start(bf16[4,24,512]{2,1,0:T(8,128)(2,1)S(1)} %get-tuple-element.145), channel_id=1, source_target_pairs={{0,16},{16,0},{32,48},{48,32},{64,80},{80,64},{96,112},{112,96},{1... | collective-permute-start | bytes 294920 | tf_op jit(solution)/shard_map/ppermute | solution.py:695
  102.4 10.8 %collective-permute-start.28 = (f32[4,6,512]{2,1,0:T(8,128)S(1)}, f32[4,6,512]{2,1,0:T(8,128)S(1)}, u32[]{:S(2)}, u32[]{:S(2)}) collective-permute-start(f32[4,6,512]{2,1,0:T(8,128)S(1)} %get-tuple-element.150), channel_id=1, source_target_pairs={{0,64},{16,80},{32,96},{48,112},{64,0},{80,16},{96,32},{112,48},{1... | collective-permute-start | bytes 147464 | tf_op jit(solution)/shard_map/ppermute | solution.py:520
  109.1 6.5 %collective-permute-start.29 = (f32[4,6,512]{2,1,0:T(8,128)S(1)}, f32[4,6,512]{2,1,0:T(8,128)S(1)}, u32[]{:S(2)}, u32[]{:S(2)}) collective-permute-start(f32[4,6,512]{2,1,0:T(8,128)S(1)} %get-tuple-element.151), channel_id=1, source_target_pairs={{0,32},{16,48},{32,64},{48,80},{64,96},{80,112},{96,0},{112,16},{1... | collective-permute-start | bytes 147464 | tf_op jit(solution)/shard_map/ppermute | solution.py:520
  110.6 5.6 %collective-permute-start.30 = (f32[4,6,512]{2,1,0:T(8,128)S(1)}, f32[4,6,512]{2,1,0:T(8,128)S(1)}, u32[]{:S(2)}, u32[]{:S(2)}) collective-permute-start(f32[4,6,512]{2,1,0:T(8,128)S(1)} %get-tuple-element.152), channel_id=1, source_target_pairs={{0,96},{16,112},{32,0},{48,16},{64,32},{80,48},{96,64},{112,80},{1... | collective-permute-start | bytes 147464 | tf_op jit(solution)/shard_map/ppermute | solution.py:520

commit v2 on v1

--- a/solution.py
+++ b/solution.py
@@ -32,9 +32,13 @@
     )
 
 
-def call(body, outs, args, scratch=(), smem=(), hbm=(), us=1.0, limit=24):
+def call(body, outs, args, scratch=(), smem=(), hbm=(), anywhere=(), us=1.0, limit=24):
     spaces = [
-        pltpu.SMEM if i in smem else pltpu.HBM if i in hbm else pltpu.VMEM for i in range(len(args))
+        pltpu.SMEM if i in smem
+        else pltpu.HBM if i in hbm
+        else pl.ANY if i in anywhere
+        else pltpu.VMEM
+        for i in range(len(args))
     ]
     return pl.pallas_call(
         body,
@@ -69,7 +73,7 @@
         return carry
 
     steps = count // STEP
-    lax.fori_loop(0, steps, step, 0, unroll=next(u for u in (4, 5, 2, 1) if steps % u == 0))
+    lax.fori_loop(0, steps, step, 0, unroll=True)
 
 
 def inside(start, first, last, edge, count):
@@ -162,25 +166,39 @@
 
 
 def forward(
-    dil, left, right, rows, act, d_att, taps, gains, wq_far, wk_far, wv_far,
+    dil, left, right, rows, act, d_att_far, taps, gains, wq_far, wk_far, wv_far,
     m0, m1, m2, m3, normed, z, near,
-    x_ext, a_ext, b_ext, slots, moved1, moved2, w_query, w_key, w_value, sems,
+    x_ext, a_ext, b_ext, slots, moved1, moved2, w_query, w_key, w_value, d_att, sems,
 ):
-    copies = fetch(((wq_far, w_query), (wk_far, w_key), (wv_far, w_value)), sems)
+    tok = rows.shape[0]
+    own = slice(HALO, HALO + tok)
+    after = slice(HALO + tok, 2 * HALO + tok)
+    copies = fetch(
+        (
+            (left, x_ext.at[0:HALO]),
+            (right, x_ext.at[after]),
+            (rows, x_ext.at[own]),
+            (act, a_ext.at[own]),
+            (d_att_far, d_att),
+            (wq_far, w_query),
+            (wk_far, w_key),
+            (wv_far, w_value),
+        ),
+        sems,
+    )
     iy = lax.axis_index("y")
     first = (iy == 0) & (lax.axis_index("xl") == 0) & (lax.axis_index("core") == 0)
     last = (iy == HEADS - 1) & (lax.axis_index("xl") == 1) & (lax.axis_index("core") == 1)
-    tok = rows.shape[0]
-    x_ext[0:HALO, :] = left[...]
-    x_ext[HALO : HALO + tok, :] = rows[...]
-    x_ext[HALO + tok :, :] = right[...]
-    a_ext[HALO : HALO + tok, :] = act[...]
+    copies[0].wait()
+    copies[1].wait()
     gain = gains[0:1, :]
     for r in [*range(0, HALO, STEP), *range(HALO + tok, 2 * HALO + tok, STEP)]:
         a_ext[r : r + STEP, :] = activate(x_ext[r : r + STEP, :].astype(F32), gain).astype(BF16)
     gap, wide = dil[0], dil[1]
     count = tok + 2 * DMAX
     gain = gains[1:2, :]
+    copies[2].wait()
+    copies[3].wait()
     move(moved1, a_ext, gap)
 
     def middle(r):
@@ -205,7 +223,7 @@
 
     loop(tok, top)
     field = normed[...]
-    for copy in copies:
+    for copy in copies[4:]:
         copy.wait()
     queries = (rounded(contract(field, w_query[...], 1, 0)) * KEY**-0.5).astype(BF16)
     keys = contract(field, w_key[...], 1, 0).astype(BF16)
@@ -344,11 +362,10 @@
     return jnp.concatenate([slots[h][:, low:high] for h in range(HEADS)], axis=1)
 
 
-def project(where, t0, t1, t2, t3, t4, z, w_out, w_query, result, g_query, slots, whole):
+def project(where, t0, t1, t2, t3, t4, z, w_out, result, slots, whole):
     gathered(slots, (t0, t1, t2, t3, t4), whole, where[0])
     att = heads_of(slots, KEY, WIDE)
     result[...] = (z[...].astype(F32) + contract(att, w_out[...], 1, 0)).astype(BF16)
-    g_query[...] = contract(heads_of(slots, 0, KEY), w_query[...], 1, 1)
 
 
 def pull_norm(held, scaled):
@@ -357,11 +374,14 @@
 
 
 def grad_top(
-    where, d0, d1, d2, d3, d4, g_query, z, upstream, w_key, w_value, gains, out, slots, total, whole
+    where, t0, t1, t2, t3, t4, d0, d1, d2, d3, d4, z, upstream, w_query, w_key, w_value, gains,
+    out, slots, total, whole, slots_t, whole_t,
 ):
+    gathered(slots_t, (t0, t1, t2, t3, t4), whole_t, where[0])
+    d_query = heads_of(slots_t, 0, KEY)
     gathered(slots, (d0, d1, d2, d3, d4), whole, where[0])
     total[...] = (
-        g_query[...]
+        contract(d_query, w_query[...], 1, 1)
         + contract(heads_of(slots, 0, KEY), w_key[...], 1, 1)
         + contract(heads_of(slots, KEY, WIDE), w_value[...], 1, 1)
     )
@@ -429,27 +449,29 @@
         out[pl.ds(pl.multiple_of(band * tok, tok), tok), :] = part[:, low : low + width]
 
 
-def weigh_first(cuts, where, f0, f1, f2, f3, t0, t1, t2, t3, t4, out, n_all, u_all, whole):
+def turn(where, f0, f1, f2, f3, n_turned, u_turned, n_all, u_all):
+    parts = (f0, f1, f2, f3)
+    for low, out, held in ((0, n_turned, n_all), (n_all.shape[1], u_turned, u_all)):
+        naturally(parts, held, low, where[0])
+        out[...] = held[...].astype(F32).T.astype(BF16)
+
+
+def weigh_first(cuts, where, n_turned, u_turned, t0, t1, t2, t3, t4, out, whole):
     iy = where[0]
-    parts = (f0, f1, f2, f3)
-    naturally(parts, n_all, 0, iy)
-    naturally(parts, u_all, n_all.shape[1], iy)
     is_key = lax.broadcasted_iota(jnp.int32, (1, WIDE), 1) < KEY
     for i, t in enumerate(joined((t0, t1, t2, t3, t4), whole)):
         held = t[...]
         first = jnp.where(
-            is_key, contract(n_all[...], held, 0, 0), contract(u_all[...], held, 0, 0)
+            is_key, contract(n_turned[...], held, 1, 0), contract(u_turned[...], held, 1, 0)
         )
         placed(out, cuts, lax.rem(iy - i + HEADS, HEADS), first)
 
 
-def weigh_second(
-    cuts, where, f0, f1, f2, f3, d0, d1, d2, d3, d4, before, keep, give, n_all, out, whole
-):
+def weigh_second(cuts, where, n_turned, d0, d1, d2, d3, d4, before, keep, give, out, whole):
     iy, core = where[0], where[4]
-    naturally((f0, f1, f2, f3), n_all, 0, iy)
     for i, d in enumerate(joined((d0, d1, d2, d3, d4), whole)):
-        placed(out, cuts, lax.rem(iy - i + HEADS, HEADS), contract(n_all[...], d[...], 0, 0))
+        head = lax.rem(iy - i + HEADS, HEADS)
+        placed(out, cuts, head, contract(n_turned[...], d[...], 1, 0))
     keep[:, :, :WIDE] = before[core]
     keep[:, :, WIDE:] = out[core]
     give[:, :, :WIDE] = before[1 - core].astype(BF16)
@@ -580,8 +602,10 @@
         (dilations, left, right, rows, act, d_att, taps, gains, w_query, w_key, w_value),
         [pltpu.VMEM(ext, BF16), pltpu.VMEM(ext, BF16), pltpu.VMEM(mid, BF16),
          pltpu.VMEM((HEADS, tok, 2 * WIDE), BF16), *shifted,
-         *(pltpu.VMEM(w.shape, BF16) for w in (w_query, w_key, w_value)), pltpu.SemaphoreType.DMA((3,))],
-        smem=(0,),
+         *(pltpu.VMEM(w.shape, BF16) for w in (w_query, w_key, w_value)),
+         pltpu.VMEM((tok, HEADS * VALUE), BF16), pltpu.SemaphoreType.DMA((8,))],
+        smem=(0,),
+        anywhere=(1, 2, 3, 4, 5),
         hbm=(8, 9, 10),
         us=5.0,
         limit=LARGE,
@@ -629,39 +653,41 @@
     own, far = call(
         first_sum, [((many, WIDE), F32), ((many, WIDE), BF16)], (own, far, got), us=0.5
     )
-    far, t, near, held = lax.optimization_barrier((far, t, near, rows))
+    far, t, near, held, fs = lax.optimization_barrier((far, t, near, rows, fs))
     got = flip(far, "xl")
     slope0, slope1 = call(slopes, [(big, F32), (mid, F32)], (held, near, gains), us=0.01)
-    got, slope0, slope1 = lax.optimization_barrier((got, slope0, slope1))
+    fields = (many, nxh * unit // 4)
+    n_turned, u_turned = call(
+        turn,
+        [(fields[::-1], BF16)] * 2,
+        (where, *fs),
+        [pltpu.VMEM(fields, BF16)] * 2,
+        smem=(0,),
+        us=0.01,
+    )
+    got, slope0, slope1, n_turned, u_turned = lax.optimization_barrier(
+        (got, slope0, slope1, n_turned, u_turned)
+    )
     ts = ring(t, "y", ny)
     (d,) = call(second_sum, [((many, WIDE), BF16)], (where, own, got), smem=(0,), us=0.5)
     ds = ring(d, "y", ny)
-    fields = ((many, nxh * unit // 4), BF16)
     cuts = (nxh, nz0, nzh * share)
     half = nxh * nz * 2 * share
     whole = pltpu.VMEM((many, WIDE), BF16)
     (before,) = call(
         functools.partial(weigh_first, cuts),
         [((2, HEADS, half, WIDE), F32)],
-        (where, *fs, *ts),
-        [pltpu.VMEM(*fields), pltpu.VMEM(*fields), whole],
+        (where, n_turned, u_turned, *ts),
+        [whole],
         smem=(0,),
         us=2.0,
     )
-    result, g_query = call(
-        project,
-        [(big, BF16), (big, F32)],
-        (where, *ts, z, w_out, w_query),
-        [pltpu.VMEM((HEADS, tok, WIDE), BF16), whole],
-        smem=(0,),
-        us=2.0,
-    )
-    ds, before, result, g_query = lax.optimization_barrier((ds, before, result, g_query))
+    ds, before = lax.optimization_barrier((ds, before))
     keep, give = call(
         functools.partial(weigh_second, cuts),
         [((HEADS, half, 2 * WIDE), F32), ((HEADS, half, 2 * WIDE), BF16)],
-        (where, *fs, *ds, before),
-        [pltpu.VMEM(*fields), pltpu.VMEM((2, HEADS, half, WIDE), F32), whole],
+        (where, n_turned, *ds, before),
+        [pltpu.VMEM((2, HEADS, half, WIDE), F32), whole],
         smem=(0,),
         us=1.5,
     )
@@ -669,8 +695,9 @@
     (grad,) = call(
         grad_top,
         [(big, BF16)],
-        (where, *ds, g_query, z, upstream, w_key, w_value, gains),
-        [pltpu.VMEM((HEADS, tok, WIDE), BF16), pltpu.VMEM(big, F32), whole],
+        (where, *ts, *ds, z, upstream, w_query, w_key, w_value, gains),
+        [pltpu.VMEM((HEADS, tok, WIDE), BF16), pltpu.VMEM(big, F32), whole,
+         pltpu.VMEM((HEADS, tok, WIDE), BF16), whole],
         smem=(0,),
         us=3.0,
     )
@@ -712,7 +739,17 @@
         us=0.6,
     )
     away = sorted(range(1, nzh), key=lambda k: -min(k, nzh - k))
+    *held, z = lax.optimization_barrier((*ts, z, parts[0]))[:-1]
+    (result,) = call(
+        project,
+        [(big, BF16)],
+        (where, *held, z, w_out),
+        [pltpu.VMEM((HEADS, tok, WIDE), BF16), whole],
+        smem=(0,),
+        us=0.01,
+    )
     parts = [parts[0]] + [shift(parts[k], "z", nz, k * nz0) for k in away]
+    result, parts = lax.optimization_barrier((result, parts))
     (weight_sum,) = call(
         arrange, [((share, 8 * WIDE), F32)], (where, *parts), smem=(0,), us=1.0
     )

time: 119 us -> 118 us (level); the launches traced: 117 us -> 118 us
  starting transfers between devices: 47.2 us -> 48.9 us
    ppermute x2, starting transfers between devices: 4.94 us -> 9.08 us  [halo(): lax.ppermute(rows[:width], SEQ, [(i + 1, i) for i in range(nseq - 1)])]
    ppermute x17, starting transfers between devices: 29.7 us -> 26.8 us  [shift(): lax.ppermute(array, axis, [(i, (i + step) % count) for i in range(count)])]
    ppermute x2, waiting for transfers between devices: 3.76 us -> 1.06 us  [halo(): lax.ppermute(rows[-width:], SEQ, [(i, i + 1) for i in range(nseq - 1)])]
    pallas_call x17 -> x18, Pallas kernels: 35.4 us -> 35.3 us  [call(): pl.pallas_call(body, out_shape=tuple((jax.ShapeDtypeStruct(s, d) for s, d...]
  transfers between devices with their start and end apart: 31 -> 31, of which waited for: 16 -> 18; matrix products, arithmetic and copies ran while one was open for 0% -> 0% of each run, Pallas kernels for 21% -> 21%
where the time goes in v2:
time: 118 us
  starting transfers between devices  48.9 us (41%)
  Pallas kernels  35.3 us (30%)
  waiting for transfers between devices  29 us (25%)
  local copies, waits for them, and re-layouts  3.66 us (3%)
    pallas_call x18, Pallas kernels, call(): pl.pallas_call(body, out_shape=tuple((jax.ShapeDtypeStruct(s, d) for s, d...  35.3 us
    ppermute x17, starting transfers between devices, shift(): lax.ppermute(array, axis, [(i, (i + step) % count) for i in range(count)])  26.8 us
    ppermute x17, waiting for transfers between devices, shift(): lax.ppermute(array, axis, [(i, (i + step) % count) for i in range(count)])  18.2 us
    ppermute x2, starting transfers between devices, halo(): lax.ppermute(rows[:width], SEQ, [(i + 1, i) for i in range(nseq - 1)])  9.08 us
    ppermute x6, waiting for transfers between devices, flip(): return lax.ppermute(array, axis, [(0, 1), (1, 0)])  6.11 us
    ppermute x3, starting transfers between devices, local(): got.append(lax.ppermute(send, ('xh', 'xl'), way))  4.79 us
    ppermute x2, starting transfers between devices, halo(): lax.ppermute(rows[-width:], SEQ, [(i, i + 1) for i in range(nseq - 1)])  3.84 us
    ppermute x3, waiting for transfers between devices, local(): got.append(lax.ppermute(send, ('xh', 'xl'), way))  2.51 us
  transfers between devices with their start and end apart: 31, of which 18 were waited for; matrix products, arithmetic and copies ran while one was open for 0% of the time, Pallas kernels for 21%

profile of v2, /device:TPU:24, one launch (start us, length us, event | category | flops | bytes accessed | tf_op | source)
XLA Modules:
  0.0 117.9 jit_solution(937652237358057128)
XLA Ops:
  0.6 1.0 slice_bitcast_fusion
  1.6 1.9 %collective-permute-start = (bf16[32,1536]{1,0:T(8,128)(2,1)S(1)}, bf16[32,1536]{1,0:T(8,128)(2,1)S(1)}, u32[]{:S(2)}, u32[]{:S(2)}) collective-permute-start(bf16[32,1536]{1,0:T(8,128)(2,1)S(1)} %get-tuple-element.186), channel_id=1, source_target_pairs={{0,1},{1,2},{2,3},{3,4},{4,5},{5,6},{6,7},{7,8},{8,9},{9,10},{10,1... | collective-permute-start | bytes 294920 | tf_op jit(solution)/shard_map/ppermute | solution.py:559
  3.5 4.5 %collective-permute-start.1 = (bf16[32,1536]{1,0:T(8,128)(2,1)S(1)}, bf16[32,1536]{1,0:T(8,128)(2,1)S(1)}, u32[]{:S(2)}, u32[]{:S(2)}) collective-permute-start(bf16[32,1536]{1,0:T(8,128)(2,1)S(1)} %get-tuple-element.185), channel_id=1, source_target_pairs={{1,0},{2,1},{3,2},{4,3},{5,4},{6,5},{7,6},{8,7},{9,8},{10,9},{11,1... | collective-permute-start | bytes 294920 | tf_op jit(solution)/shard_map/ppermute | solution.py:560
  8.1 4.2 %prelude.1 = (bf16[128,1536]{1,0:T(8,128)(2,1)}, bf16[128,768]{1,0:T(8,128)(2,1)}) custom-call(bf16[128,1536]{1,0:T(8,128)(2,1)} %bitcast.19, f32[3,1536]{1,0:T(4,128)} %gains.7, bf16[128,1536]{1,0:T(8,128)(2,1)} %bitcast.23, bf16[768,1536]{1,0:T(8,128)(2,1)} %w_out.1), custom_call_target="tpu_custom_call" | custom-call | flops 1000 | bytes 10800000 | tf_op jit(solution)/shard_map/prelude/pallas_call | solution.py:43
  12.4 0.6 copy-done.16
  13.0 5.3 %forward.1 = (bf16[128,512]{1,0:T(8,128)(2,1)}, bf16[128,512]{1,0:T(8,128)(2,1)}, bf16[128,512]{1,0:T(8,128)(2,1)}, bf16[128,512]{1,0:T(8,128)(2,1)}, bf16[128,1...) custom-call(s32[2]{0:T(128)} %dil.3, bf16[32,1536]{1,0:T(8,128)(2,1)} %copy-done.16, ...), custom_call_target="tpu_custom_call" | custom-call | flops 1000 | bytes 18000000 | tf_op jit(solution)/shard_map/forward/pallas_call | solution.py:43
  18.5 2.8 %collective-permute-start.3 = (bf16[128,512]{1,0:T(8,128)(2,1)}, bf16[128,512]{1,0:T(8,128)(2,1)S(1)}, u32[]{:S(2)}, u32[]{:S(2)}) collective-permute-start(bf16[128,512]{1,0:T(8,128)(2,1)} %get-tuple-element.97), channel_id=1, source_target_pairs={{0,8},{4,12},{8,0},{12,4},{1,9},{5,13},{9,1},{13,5},{2,10},{6,14},... | collective-permute-start | bytes 393224 | tf_op jit(solution)/shard_map/ppermute | solution.py:542
  21.4 1.0 copy-done.8
  22.4 1.6 %shuffle.1 = (bf16[128,768]{1,0:T(8,128)(2,1)S(1)}, bf16[128,768]{1,0:T(8,128)(2,1)S(1)}, bf16[128,768]{1,0:T(8,128)(2,1)S(1)}, bf16[128,768]{1,0:T(8,128)(2,1)S(1)}) custom-call(s32[10]{0:T(128)S(1)} %stack.35.where, s32[1,768]{1,0:T(1,128)S(1)} %copy-done.13, bf16[128,1536]{1,0:T(8,128)(2,1)S(1)} %copy-done.8, bf16[128,1536]{1,0:T(8,128)(2,1)S(1)} %bitcast.24), custom_call_target="tpu_custom_call" | custom-call | flops 1000 | bytes 5760000 | tf_op jit(solution)/shard_map/shuffle/pallas_call | solution.py:43
  23.9 0.5 collective-permute-done.2.m1
  24.4 2.3 %collective-permute-done.3.m2 = bf16[128,512]{1,0:T(8,128)(2,1)S(1)} collective-permute-done((bf16[128,512]{1,0:T(8,128)(2,1)}, bf16[128,512]{1,0:T(8,128)(2,1)S(1)}, u32[]{:S(2)}, u32[]{:S(2)}) %collective-permute-start.3) | collective-permute-done | bytes 131104 | tf_op jit(solution)/shard_map/ppermute | solution.py:542
  26.7 1.2 %collective-permute-done.4.m3 = bf16[128,512]{1,0:T(8,128)(2,1)S(1)} collective-permute-done((bf16[128,512]{1,0:T(8,128)(2,1)}, bf16[128,512]{1,0:T(8,128)(2,1)S(1)}, u32[]{:S(2)}, u32[]{:S(2)}) %collective-permute-start.4) | collective-permute-done | bytes 131104 | tf_op jit(solution)/shard_map/ppermute | solution.py:542
  27.9 0.8 slice.46
  28.8 1.6 %collective-permute-start.6 = (bf16[512,256]{1,0:T(8,128)(2,1)S(1)}, bf16[512,256]{1,0:T(8,128)(2,1)S(1)}, u32[]{:S(2)}, u32[]{:S(2)}) collective-permute-start(bf16[512,256]{1,0:T(8,128)(2,1)S(1)} %pad_maximum_fusion), channel_id=1, source_target_pairs={{0,2},{2,0},{1,3},{3,1},{4,6},{6,4},{5,7},{7,5},{8,10},{10,8},{9,1... | collective-permute-start | bytes 786440 | tf_op jit(solution)/shard_map/ppermute | solution.py:554
  30.4 0.6 collective-permute-start.7
  31.0 1.5 %collective-permute-start.8 = (bf16[128,768]{1,0:T(8,128)(2,1)S(1)}, bf16[128,768]{1,0:T(8,128)(2,1)S(1)}, u32[]{:S(2)}, u32[]{:S(2)}) collective-permute-start(bf16[128,768]{1,0:T(8,128)(2,1)S(1)} %get-tuple-element.109), channel_id=1, source_target_pairs={{0,12},{4,0},{8,4},{12,8},{1,13},{5,1},{9,5},{13,9},{2,14},{6,2},{... | collective-permute-start | bytes 589832 | tf_op jit(solution)/shard_map/ppermute | solution.py:542
  32.5 1.5 %expand.1.master = f32[128,4096]{1,0:T(8,128)S(1)} custom-call(s32[10]{0:T(128)S(1)} %stack.35.where, f32[4,64]{1,0:T(4,128)S(1)} %bitcast.29, s32[1,4095]{1,0:T(1,128)S(1)} %bitcast.28), custom_call_target="tpu_custom_call" | custom-call | flops 1000 | bytes 5400000 | tf_op jit(solution)/shard_map/expand/pallas_call | solution.py:43
  34.0 2.6 %collective-permute-done.7.f1 = bf16[128,768]{1,0:T(8,128)(2,1)S(1)} collective-permute-done((bf16[128,768]{1,0:T(8,128)(2,1)S(1)}, bf16[128,768]{1,0:T(8,128)(2,1)S(1)}, u32[]{:S(2)}, u32[]{:S(2)}) %collective-permute-start.7) | collective-permute-done | bytes 196640 | tf_op jit(solution)/shard_map/ppermute | solution.py:542
  36.6 1.3 %collective-permute-done.8.f3 = bf16[128,768]{1,0:T(8,128)(2,1)S(1)} collective-permute-done((bf16[128,768]{1,0:T(8,128)(2,1)S(1)}, bf16[128,768]{1,0:T(8,128)(2,1)S(1)}, u32[]{:S(2)}, u32[]{:S(2)}) %collective-permute-start.8) | collective-permute-done | bytes 196640 | tf_op jit(solution)/shard_map/ppermute | solution.py:542
  37.9 1.1 collective-permute-start.10
  39.0 0.4 collective-permute-done.9.kv3
  39.4 6.8 %attend.1 = (bf16[512,256]{1,0:T(8,128)(2,1)S(1)}, f32[512,256]{1,0:T(8,128)S(1)}, f32[512,256]{1,0:T(8,128)S(1)}, bf16[1024,256]{1,0:T(8,128)(2,1)S(1)}) custom-call(s32[10]{0:T(128)S(1)} %stack.35.where, bf16[128,512]{1,0:T(8,128)(2,1)S(1)} %copy-done.10, bf16[128,512]{1,0:T(8,128)(2,1)S(1)} %collective-permute-done.2.m1, ...), custom_call_target="tpu_custom_call" | custom-call | flops 1000 | bytes 25200000 | tf_op jit(solution)/shard_map/attend/pallas_call | solution.py:43
  46.2 0.5 collective-permute-done.10.f2
  46.7 1.9 %collective-permute-done.11.got = bf16[1024,256]{1,0:T(8,128)(2,1)S(1)} collective-permute-done((bf16[1024,256]{1,0:T(8,128)(2,1)S(1)}, bf16[1024,256]{1,0:T(8,128)(2,1)S(1)}, u32[]{:S(2)}, u32[]{:S(2)}) %collective-permute-start.11) | collective-permute-done | bytes 524320 | tf_op jit(solution)/shard_map/ppermute | solution.py:554
  48.6 0.1 first_sum.1
  48.7 0.7 collective-permute-start.16
  49.4 1.0 collective-permute-start.12
  50.4 1.0 collective-permute-start.14
  51.5 1.0 slopes.1
  52.5 0.9 turn.1
  53.4 3.8 %collective-permute-done.16.got = bf16[512,256]{1,0:T(8,128)(2,1)S(1)} collective-permute-done((bf16[512,256]{1,0:T(8,128)(2,1)S(1)}, bf16[512,256]{1,0:T(8,128)(2,1)S(1)}, u32[]{:S(2)}, u32[]{:S(2)}) %collective-permute-start.16) | collective-permute-done | bytes 262176 | tf_op jit(solution)/shard_map/ppermute | solution.py:554
  57.2 0.6 second_sum.1.d0
  57.8 1.4 %collective-permute-start.17 = (bf16[512,256]{1,0:T(8,128)(2,1)S(1)}, bf16[512,256]{1,0:T(8,128)(2,1)S(1)}, u32[]{:S(2)}, u32[]{:S(2)}) collective-permute-start(bf16[512,256]{1,0:T(8,128)(2,1)S(1)} %second_sum.1.d0), channel_id=1, source_target_pairs={{0,4},{4,8},{8,12},{12,0},{1,5},{5,9},{9,13},{13,1},{2,6},{6,10},{... | collective-permute-start | bytes 786440 | tf_op jit(solution)/shard_map/ppermute | solution.py:542
  59.2 0.7 collective-permute-start.19
  59.9 2.6 %collective-permute-start.13 = (bf16[256,256]{1,0:T(8,128)(2,1)S(1)}, bf16[256,256]{1,0:T(8,128)(2,1)S(1)}, u32[]{:S(2)}, u32[]{:S(2)}) collective-permute-start(bf16[256,256]{1,0:T(8,128)(2,1)S(1)} %slice.56), channel_id=1, source_target_pairs={{0,4},{4,8},{8,12},{12,0},{1,5},{5,9},{9,13},{13,1},{2,6},{6,10},{... | collective-permute-start | bytes 393224 | tf_op jit(solution)/shard_map/ppermute | solution.py:542
  62.5 0.3 collective-permute-start.15
  62.8 4.2 %collective-permute-done.17.d1 = bf16[512,256]{1,0:T(8,128)(2,1)S(1)} collective-permute-done((bf16[512,256]{1,0:T(8,128)(2,1)S(1)}, bf16[512,256]{1,0:T(8,128)(2,1)S(1)}, u32[]{:S(2)}, u32[]{:S(2)}) %collective-permute-start.17) | collective-permute-done | bytes 262176 | tf_op jit(solution)/shard_map/ppermute | solution.py:542
  67.1 2.4 %collective-permute-start.18 = (bf16[256,256]{1,0:T(8,128)(2,1)S(1)}, bf16[256,256]{1,0:T(8,128)(2,1)S(1)}, u32[]{:S(2)}, u32[]{:S(2)}) collective-permute-start(bf16[256,256]{1,0:T(8,128)(2,1)S(1)} %slice.58), channel_id=1, source_target_pairs={{0,4},{4,8},{8,12},{12,0},{1,5},{5,9},{9,13},{13,1},{2,6},{6,10},{... | collective-permute-start | bytes 393224 | tf_op jit(solution)/shard_map/ppermute | solution.py:542
  69.6 1.2 %collective-permute-done.15.t3 = bf16[256,256]{1,0:T(8,128)(2,1)S(1)} collective-permute-done((bf16[256,256]{1,0:T(8,128)(2,1)S(1)}, bf16[256,256]{1,0:T(8,128)(2,1)S(1)}, u32[]{:S(2)}, u32[]{:S(2)}) %collective-permute-start.15) | collective-permute-done | bytes 131104 | tf_op jit(solution)/shard_map/ppermute | solution.py:542
  70.8 1.5 %weigh_first.1.before = f32[2,4,192,256]{3,2,1,0:T(8,128)S(1)} custom-call(s32[10]{0:T(128)S(1)} %stack.35.where, bf16[384,512]{1,0:T(8,128)(2,1)S(1)} %get-tuple-element.141.n_turned, bf16[384,512]{1,0:T(8,128)(2,1)S(1)} %get-tuple-element.144.u_turned, bf16[512,256]{1,0:T(8,128)(2,1)S(1)} %get-tuple-element.168.t0, ...), custom_call_target="tpu_custom_call" | custom-call | flops 1000 | bytes 7200000 | tf_op jit(solution)/shard_map/weigh_first/pallas_call | solution.py:43
  72.3 3.4 %collective-permute-done.20.d3 = bf16[256,256]{1,0:T(8,128)(2,1)S(1)} collective-permute-done((bf16[256,256]{1,0:T(8,128)(2,1)S(1)}, bf16[256,256]{1,0:T(8,128)(2,1)S(1)}, u32[]{:S(2)}, u32[]{:S(2)}) %collective-permute-start.20) | collective-permute-done | bytes 131104 | tf_op jit(solution)/shard_map/ppermute | solution.py:542
  75.8 1.3 %weigh_second.1 = (f32[4,192,512]{2,1,0:T(8,128)S(1)}, bf16[4,192,512]{2,1,0:T(8,128)(2,1)S(1)}) custom-call(s32[10]{0:T(128)S(1)} %stack.35.where, bf16[384,512]{1,0:T(8,128)(2,1)S(1)} %get-tuple-element.141.n_turned, bf16[512,256]{1,0:T(8,128)(2,1)S(1)} %second_sum.1.d0, bf16[512,256]{1,0:T(8,128)(2,1)S(1)} %collective-permute-done.17.d1, ...), custom_call_target="tpu_custom_call" | custom-call | flops 1000 | bytes 5400000 | tf_op jit(solution)/shard_map/weigh_second/pallas_call | solution.py:43
  77.2 2.2 %grad_top.1.grad = bf16[128,1536]{1,0:T(8,128)(2,1)S(1)} custom-call(s32[10]{0:T(128)S(1)} %stack.35.where, bf16[512,256]{1,0:T(8,128)(2,1)S(1)} %get-tuple-element.168.t0, bf16[512,256]{1,0:T(8,128)(2,1)S(1)} %collective-permute-done.12.t1, bf16[256,256]{1,0:T(8,128)(2,1)S(1)} %collective-permute-done.13.t2, ...), custom_call_target="tpu_custom_call" | custom-call | flops 1000 | bytes 10800000 | tf_op jit(solution)/shard_map/grad_top/pallas_call | solution.py:43
  79.5 0.8 fold.2
  80.3 0.4 collective-permute-start.24
  80.7 3.4 %collective-permute-start.25 = (bf16[4,48,512]{2,1,0:T(8,128)(2,1)S(1)}, bf16[4,48,512]{2,1,0:T(8,128)(2,1)S(1)}, u32[]{:S(2)}, u32[]{:S(2)}) collective-permute-start(bf16[4,48,512]{2,1,0:T(8,128)(2,1)S(1)} %get-tuple-element.155), channel_id=1, source_target_pairs={{0,128},{2,130},{128,0},{130,2},{1,129},{3,131},{129,1},{131,3},{4... | collective-permute-start | bytes 589832 | tf_op jit(solution)/shard_map/ppermute | solution.py:716
  84.1 1.0 collective-permute-start.26
  85.1 1.9 %collective-permute-start.22 = (bf16[32,1536]{1,0:T(8,128)(2,1)S(1)}, bf16[32,1536]{1,0:T(8,128)(2,1)S(1)}, u32[]{:S(2)}, u32[]{:S(2)}) collective-permute-start(bf16[32,1536]{1,0:T(8,128)(2,1)S(1)} %get-tuple-element.184), channel_id=1, source_target_pairs={{0,1},{1,2},{2,3},{3,4},{4,5},{5,6},{6,7},{7,8},{8,9},{9,10},{10,1... | collective-permute-start | bytes 294920 | tf_op jit(solution)/shard_map/ppermute | solution.py:559
  87.0 4.5 %collective-permute-start.23 = (bf16[32,1536]{1,0:T(8,128)(2,1)S(1)}, bf16[32,1536]{1,0:T(8,128)(2,1)S(1)}, u32[]{:S(2)}, u32[]{:S(2)}) collective-permute-start(bf16[32,1536]{1,0:T(8,128)(2,1)S(1)} %get-tuple-element.183), channel_id=1, source_target_pairs={{1,0},{2,1},{3,2},{4,3},{5,4},{6,5},{7,6},{8,7},{9,8},{10,9},{11,1... | collective-permute-start | bytes 294920 | tf_op jit(solution)/shard_map/ppermute | solution.py:560
  91.6 1.1 collective-permute-done.22.left
  92.6 1.1 collective-permute-done.23.right
  93.8 0.3 collective-permute-done.25.refs_1_
  94.1 2.2 %collective-permute-done.26.refs_2_ = bf16[4,48,512]{2,1,0:T(8,128)(2,1)S(1)} collective-permute-done((bf16[4,48,512]{2,1,0:T(8,128)(2,1)S(1)}, bf16[4,48,512]{2,1,0:T(8,128)(2,1)S(1)}, u32[]{:S(2)}, u32[]{:S(2)}) %collective-permute-start.26) | collective-permute-done | bytes 196640 | tf_op jit(solution)/shard_map/ppermute | solution.py:716
  96.3 0.7 fold.3
  97.0 2.0 %collective-permute-start.27 = (bf16[4,24,512]{2,1,0:T(8,128)(2,1)S(1)}, bf16[4,24,512]{2,1,0:T(8,128)(2,1)S(1)}, u32[]{:S(2)}, u32[]{:S(2)}) collective-permute-start(bf16[4,24,512]{2,1,0:T(8,128)(2,1)S(1)} %get-tuple-element.165), channel_id=1, source_target_pairs={{0,16},{16,0},{32,48},{48,32},{64,80},{80,64},{96,112},{112,96},{1... | collective-permute-start | bytes 294920 | tf_op jit(solution)/shard_map/ppermute | solution.py:722
  99.0 2.9 %backward.1 = bf16[128,1536]{1,0:T(8,128)(2,1)} custom-call(s32[10]{0:T(128)S(1)} %stack.35.where, s32[2]{0:T(128)S(1)} %copy-done.14, bf16[32,1536]{1,0:T(8,128)(2,1)S(1)} %collective-permute-done.22.left, bf16[32,1536]{1,0:T(8,128)(2,1)S(1)} %collective-permute-done.23.right, bf16[128,1536]{1,0:T(8,128)(2,1)S(1)} %grad_top.1.grad, ...), custom_call_target="tpu_custom_call" | custom-call | flops 1000 | bytes 16559999 | tf_op jit(solution)/shard_map/backward/pallas_call | solution.py:43
  101.9 0.6 last_fold.1
  102.5 7.1 %collective-permute-start.28 = (f32[4,6,512]{2,1,0:T(8,128)S(1)}, f32[4,6,512]{2,1,0:T(8,128)S(1)}, u32[]{:S(2)}, u32[]{:S(2)}) collective-permute-start(f32[4,6,512]{2,1,0:T(8,128)S(1)} %get-tuple-element.174), channel_id=1, source_target_pairs={{0,64},{16,80},{32,96},{48,112},{64,0},{80,16},{96,32},{112,48},{1... | collective-permute-start | bytes 147464 | tf_op jit(solution)/shard_map/ppermute | solution.py:542
  109.6 1.5 %collective-permute-start.29 = (f32[4,6,512]{2,1,0:T(8,128)S(1)}, f32[4,6,512]{2,1,0:T(8,128)S(1)}, u32[]{:S(2)}, u32[]{:S(2)}) collective-permute-start(f32[4,6,512]{2,1,0:T(8,128)S(1)} %get-tuple-element.175), channel_id=1, source_target_pairs={{0,32},{16,48},{32,64},{48,80},{64,96},{80,112},{96,0},{112,16},{1... | collective-permute-start | bytes 147464 | tf_op jit(solution)/shard_map/ppermute | solution.py:542
  111.0 2.7 %collective-permute-start.30 = (f32[4,6,512]{2,1,0:T(8,128)S(1)}, f32[4,6,512]{2,1,0:T(8,128)S(1)}, u32[]{:S(2)}, u32[]{:S(2)}) collective-permute-start(f32[4,6,512]{2,1,0:T(8,128)S(1)} %get-tuple-element.176), channel_id=1, source_target_pairs={{0,96},{16,112},{32,0},{48,16},{64,32},{80,48},{96,64},{112,80},{1... | collective-permute-start | bytes 147464 | tf_op jit(solution)/shard_map/ppermute | solution.py:542
  113.7 1.8 %project.1 = bf16[128,1536]{1,0:T(8,128)(2,1)} custom-call(s32[10]{0:T(128)S(1)} %stack.35.where, bf16[512,256]{1,0:T(8,128)(2,1)S(1)} %get-tuple-element.168.t0, bf16[512,256]{1,0:T(8,128)(2,1)S(1)} %collective-permute-done.12.t1, bf16[256,256]{1,0:T(8,128)(2,1)S(1)} %collective-permute-done.13.t2, bf16[256,256]{1,0:T(8,128)(2,1)S(1)} %collective-permute-done.15.t3, ...), custom_call_target="tpu_custom_call" | custom-call | flops 1000 | bytes 36000 | tf_op jit(solution)/shard_map/project/pallas_call | solution.py:43
  115.5 0.5 collective-permute-done.29.refs_2_
  116.0 0.6 collective-permute-done.30.refs_3_
  116.6 1.3 %arrange.1 = f32[6,2048]{1,0:T(8,128)} custom-call(s32[10]{0:T(128)S(1)} %stack.35.where, f32[4,6,512]{2,1,0:T(8,128)S(1)} %get-tuple-element.179.refs_0_, f32[4,6,512]{2,1,0:T(8,128)S(1)} %collective-permute-done.28.refs_1_, f32[4,6,512]{2,1,0:T(8,128)S(1)} %collective-permute-done.29.refs_2_, f32[4,6,512]{2,1,0:T(8,128)S(1)} %collective-permute-done.30.refs_3_), custom_call_target="tpu_custom_call" | custom-call | flops 1000 | bytes 3600000 | tf_op jit(solution)/shard_map/arrange/pallas_call | solution.py:43
  (64 shorter events, 0.6 us)
Async XLA Ops:
  1.6 10.7 %collective-permute-start = (bf16[32,1536]{1,0:T(8,128)(2,1)S(1)}, bf16[32,1536]{1,0:T(8,128)(2,1)S(1)}, u32[]{:S(2)}, u32[]{:S(2)}) collective-permute-start(bf16[32,1536]{1,0:T(8,128)(2,1)S(1)} %get-tuple-element.186), channel_id=1, source_target_pairs={{0,1},{1,2},{2,3},{3,4},{4,5},{5,6},{6,7},{7,8},{8,9},{9,10},{10,1... | collective-permute-start | bytes 294920 | tf_op jit(solution)/shard_map/ppermute | solution.py:559
  3.5 8.8 %collective-permute-start.1 = (bf16[32,1536]{1,0:T(8,128)(2,1)S(1)}, bf16[32,1536]{1,0:T(8,128)(2,1)S(1)}, u32[]{:S(2)}, u32[]{:S(2)}) collective-permute-start(bf16[32,1536]{1,0:T(8,128)(2,1)S(1)} %get-tuple-element.185), channel_id=1, source_target_pairs={{1,0},{2,1},{3,2},{4,3},{5,4},{6,5},{7,6},{8,7},{9,8},{10,9},{11,1... | collective-permute-start | bytes 294920 | tf_op jit(solution)/shard_map/ppermute | solution.py:560
  12.3 0.6 copy-start.16
  12.3 0.6 copy-start.17
  13.0 8.3 %copy-start.3 = (bf16[1,128,1536]{2,1,0:T(8,128)(2,1)S(1)}, bf16[1,128,1536]{2,1,0:T(8,128)(2,1)}, u32[]{:S(2)}) copy-start(bf16[1,128,1536]{2,1,0:T(8,128)(2,1)} %param.22) | copy-start | bytes 1179652
  13.0 8.3 %copy-start.13 = (s32[1,768]{1,0:T(1,128)S(1)}, s32[1,768]{1,0:T(1,128)}, u32[]{:S(2)}) copy-start(s32[1,768]{1,0:T(1,128)} %constant.50.clone.order) | copy-start | bytes 9220
  13.0 19.4 %copy-start.12 = (s32[4095]{0:T(1024)S(1)}, s32[4095]{0:T(1024)}, u32[]{:S(2)}) copy-start(s32[4095]{0:T(1024)} %param.17) | copy-start | bytes 49144
  13.0 19.4 %copy-start.15 = (f32[64,4]{0,1:T(4,128)S(1)}, f32[64,4]{0,1:T(4,128)}, u32[]{:S(2)}) copy-start(f32[64,4]{0,1:T(4,128)} %param.16) | copy-start | bytes 3076
  18.4 6.1 %collective-permute-start.2 = (bf16[128,512]{1,0:T(8,128)(2,1)}, bf16[128,512]{1,0:T(8,128)(2,1)S(1)}, u32[]{:S(2)}, u32[]{:S(2)}) collective-permute-start(bf16[128,512]{1,0:T(8,128)(2,1)} %get-tuple-element.96), channel_id=1, source_target_pairs={{0,4},{4,8},{8,12},{12,0},{1,5},{5,9},{9,13},{13,1},{2,6},{6,10},{... | collective-permute-start | bytes 393224 | tf_op jit(solution)/shard_map/ppermute | solution.py:542
  18.5 8.3 %collective-permute-start.3 = (bf16[128,512]{1,0:T(8,128)(2,1)}, bf16[128,512]{1,0:T(8,128)(2,1)S(1)}, u32[]{:S(2)}, u32[]{:S(2)}) collective-permute-start(bf16[128,512]{1,0:T(8,128)(2,1)} %get-tuple-element.97), channel_id=1, source_target_pairs={{0,8},{4,12},{8,0},{12,4},{1,9},{5,13},{9,1},{13,5},{2,10},{6,14},... | collective-permute-start | bytes 393224 | tf_op jit(solution)/shard_map/ppermute | solution.py:542
  21.3 6.6 %collective-permute-start.4 = (bf16[128,512]{1,0:T(8,128)(2,1)}, bf16[128,512]{1,0:T(8,128)(2,1)S(1)}, u32[]{:S(2)}, u32[]{:S(2)}) collective-permute-start(bf16[128,512]{1,0:T(8,128)(2,1)} %get-tuple-element.98), channel_id=1, source_target_pairs={{0,12},{4,0},{8,4},{12,8},{1,13},{5,1},{9,5},{13,9},{2,14},{6,2},{... | collective-permute-start | bytes 393224 | tf_op jit(solution)/shard_map/ppermute | solution.py:542
  21.4 1.0 copy-start.8
  22.4 17.1 %copy-start.10 = (bf16[128,512]{1,0:T(8,128)(2,1)S(1)}, bf16[128,512]{1,0:T(8,128)(2,1)}, u32[]{:S(2)}) copy-start(bf16[128,512]{1,0:T(8,128)(2,1)} %get-tuple-element.104.m0) | copy-start | bytes 393220
  28.8 9.1 %collective-permute-start.6 = (bf16[512,256]{1,0:T(8,128)(2,1)S(1)}, bf16[512,256]{1,0:T(8,128)(2,1)S(1)}, u32[]{:S(2)}, u32[]{:S(2)}) collective-permute-start(bf16[512,256]{1,0:T(8,128)(2,1)S(1)} %pad_maximum_fusion), channel_id=1, source_target_pairs={{0,2},{2,0},{1,3},{3,1},{4,6},{6,4},{5,7},{7,5},{8,10},{10,8},{9,1... | collective-permute-start | bytes 786440 | tf_op jit(solution)/shard_map/ppermute | solution.py:554
  30.4 6.2 %collective-permute-start.7 = (bf16[128,768]{1,0:T(8,128)(2,1)S(1)}, bf16[128,768]{1,0:T(8,128)(2,1)S(1)}, u32[]{:S(2)}, u32[]{:S(2)}) collective-permute-start(bf16[128,768]{1,0:T(8,128)(2,1)S(1)} %get-tuple-element.108), channel_id=1, source_target_pairs={{0,4},{4,8},{8,12},{12,0},{1,5},{5,9},{9,13},{13,1},{2,6},{6,10},{... | collective-permute-start | bytes 589832 | tf_op jit(solution)/shard_map/ppermute | solution.py:542
  31.0 6.9 %collective-permute-start.8 = (bf16[128,768]{1,0:T(8,128)(2,1)S(1)}, bf16[128,768]{1,0:T(8,128)(2,1)S(1)}, u32[]{:S(2)}, u32[]{:S(2)}) collective-permute-start(bf16[128,768]{1,0:T(8,128)(2,1)S(1)} %get-tuple-element.109), channel_id=1, source_target_pairs={{0,12},{4,0},{8,4},{12,8},{1,13},{5,1},{9,5},{13,9},{2,14},{6,2},{... | collective-permute-start | bytes 589832 | tf_op jit(solution)/shard_map/ppermute | solution.py:542
  32.4 6.6 %collective-permute-start.5 = (bf16[512,256]{1,0:T(8,128)(2,1)S(1)}, bf16[512,256]{1,0:T(8,128)(2,1)S(1)}, u32[]{:S(2)}, u32[]{:S(2)}) collective-permute-start(bf16[512,256]{1,0:T(8,128)(2,1)S(1)} %pad_maximum_fusion), channel_id=1, source_target_pairs={{0,1},{1,0},{2,3},{3,2},{4,5},{5,4},{6,7},{7,6},{8,9},{9,8},{10,11... | collective-permute-start | bytes 786440 | tf_op jit(solution)/shard_map/ppermute | solution.py:554
  34.0 17.5 %copy-start.2 = (bf16[1,128,1536]{2,1,0:T(8,128)(2,1)S(1)}, bf16[1,128,1536]{2,1,0:T(8,128)(2,1)}, u32[]{:S(2)}) copy-start(bf16[1,128,1536]{2,1,0:T(8,128)(2,1)} %param.12) | copy-start | bytes 1179652
  34.0 17.5 %copy-start.6 = (bf16[160,1536]{1,0:T(8,128)(2,1)S(1)}, bf16[160,1536]{1,0:T(8,128)(2,1)}, u32[]{:S(2)}) copy-start(bf16[160,1536]{1,0:T(8,128)(2,1)} %get-tuple-element.132.near) | copy-start | bytes 1474564
  34.0 17.5 %copy-start.9 = (f32[3,1536]{1,0:T(4,128)S(1)}, f32[3,1536]{1,0:T(4,128)}, u32[]{:S(2)}) copy-start(f32[3,1536]{1,0:T(4,128)} %gains.7) | copy-start | bytes 55300
  37.9 1.5 %collective-permute-start.9 = (bf16[512,256]{1,0:T(8,128)(2,1)S(1)}, bf16[512,256]{1,0:T(8,128)(2,1)S(1)}, u32[]{:S(2)}, u32[]{:S(2)}) collective-permute-start(bf16[512,256]{1,0:T(8,128)(2,1)S(1)} %collective-permute-done.6.kv2), channel_id=1, source_target_pairs={{0,1},{1,0},{2,3},{3,2},{4,5},{5,4},{6,7},{7,6},{8,9},{9,8},{10,11... | collective-permute-start | bytes 786440 | tf_op jit(solution)/shard_map/ppermute | solution.py:554
  37.9 8.8 %collective-permute-start.10 = (bf16[128,768]{1,0:T(8,128)(2,1)S(1)}, bf16[128,768]{1,0:T(8,128)(2,1)S(1)}, u32[]{:S(2)}, u32[]{:S(2)}) collective-permute-start(bf16[128,768]{1,0:T(8,128)(2,1)S(1)} %get-tuple-element.118), channel_id=1, source_target_pairs={{0,8},{4,12},{8,0},{12,4},{1,9},{5,13},{9,1},{13,5},{2,10},{6,14},... | collective-permute-start | bytes 589832 | tf_op jit(solution)/shard_map/ppermute | solution.py:542
  46.7 1.9 %collective-permute-start.11 = (bf16[1024,256]{1,0:T(8,128)(2,1)S(1)}, bf16[1024,256]{1,0:T(8,128)(2,1)S(1)}, u32[]{:S(2)}, u32[]{:S(2)}) collective-permute-start(bf16[1024,256]{1,0:T(8,128)(2,1)S(1)} %get-tuple-element.120), channel_id=1, source_target_pairs={{0,1},{1,0},{2,3},{3,2},{4,5},{5,4},{6,7},{7,6},{8,9},{9,8},{10,11... | collective-permute-start | bytes 1572872 | tf_op jit(solution)/shard_map/ppermute | solution.py:554
  48.7 8.4 %collective-permute-start.16 = (bf16[512,256]{1,0:T(8,128)(2,1)S(1)}, bf16[512,256]{1,0:T(8,128)(2,1)S(1)}, u32[]{:S(2)}, u32[]{:S(2)}) collective-permute-start(bf16[512,256]{1,0:T(8,128)(2,1)S(1)} %get-tuple-element.130), channel_id=1, source_target_pairs={{0,2},{2,0},{1,3},{3,1},{4,6},{6,4},{5,7},{7,5},{8,10},{10,8},{9,1... | collective-permute-start | bytes 786440 | tf_op jit(solution)/shard_map/ppermute | solution.py:554
  49.4 10.5 %collective-permute-start.12 = (bf16[512,256]{1,0:T(8,128)(2,1)S(1)}, bf16[512,256]{1,0:T(8,128)(2,1)S(1)}, u32[]{:S(2)}, u32[]{:S(2)}) collective-permute-start(bf16[512,256]{1,0:T(8,128)(2,1)S(1)} %get-tuple-element.168.t0), channel_id=1, source_target_pairs={{0,4},{4,8},{8,12},{12,0},{1,5},{5,9},{9,13},{13,1},{2,6},{6,10},{... | collective-permute-start | bytes 786440 | tf_op jit(solution)/shard_map/ppermute | solution.py:542
  50.4 12.1 %collective-permute-start.14 = (bf16[512,256]{1,0:T(8,128)(2,1)S(1)}, bf16[512,256]{1,0:T(8,128)(2,1)S(1)}, u32[]{:S(2)}, u32[]{:S(2)}) collective-permute-start(bf16[512,256]{1,0:T(8,128)(2,1)S(1)} %get-tuple-element.168.t0), channel_id=1, source_target_pairs={{0,12},{4,0},{8,4},{12,8},{1,13},{5,1},{9,5},{13,9},{2,14},{6,2},{... | collective-permute-start | bytes 786440 | tf_op jit(solution)/shard_map/ppermute | solution.py:542
  57.8 9.3 %collective-permute-start.17 = (bf16[512,256]{1,0:T(8,128)(2,1)S(1)}, bf16[512,256]{1,0:T(8,128)(2,1)S(1)}, u32[]{:S(2)}, u32[]{:S(2)}) collective-permute-start(bf16[512,256]{1,0:T(8,128)(2,1)S(1)} %second_sum.1.d0), channel_id=1, source_target_pairs={{0,4},{4,8},{8,12},{12,0},{1,5},{5,9},{9,13},{13,1},{2,6},{6,10},{... | collective-permute-start | bytes 786440 | tf_op jit(solution)/shard_map/ppermute | solution.py:542
  59.2 10.3 %collective-permute-start.19 = (bf16[512,256]{1,0:T(8,128)(2,1)S(1)}, bf16[512,256]{1,0:T(8,128)(2,1)S(1)}, u32[]{:S(2)}, u32[]{:S(2)}) collective-permute-start(bf16[512,256]{1,0:T(8,128)(2,1)S(1)} %second_sum.1.d0), channel_id=1, source_target_pairs={{0,12},{4,0},{8,4},{12,8},{1,13},{5,1},{9,5},{13,9},{2,14},{6,2},{... | collective-permute-start | bytes 786440 | tf_op jit(solution)/shard_map/ppermute | solution.py:542
  59.9 9.7 %collective-permute-start.13 = (bf16[256,256]{1,0:T(8,128)(2,1)S(1)}, bf16[256,256]{1,0:T(8,128)(2,1)S(1)}, u32[]{:S(2)}, u32[]{:S(2)}) collective-permute-start(bf16[256,256]{1,0:T(8,128)(2,1)S(1)} %slice.56), channel_id=1, source_target_pairs={{0,4},{4,8},{8,12},{12,0},{1,5},{5,9},{9,13},{13,1},{2,6},{6,10},{... | collective-permute-start | bytes 393224 | tf_op jit(solution)/shard_map/ppermute | solution.py:542
  62.5 8.3 %collective-permute-start.15 = (bf16[256,256]{1,0:T(8,128)(2,1)S(1)}, bf16[256,256]{1,0:T(8,128)(2,1)S(1)}, u32[]{:S(2)}, u32[]{:S(2)}) collective-permute-start(bf16[256,256]{1,0:T(8,128)(2,1)S(1)} %slice.57), channel_id=1, source_target_pairs={{0,12},{4,0},{8,4},{12,8},{1,13},{5,1},{9,5},{13,9},{2,14},{6,2},{... | collective-permute-start | bytes 393224 | tf_op jit(solution)/shard_map/ppermute | solution.py:542
  67.1 5.2 %collective-permute-start.18 = (bf16[256,256]{1,0:T(8,128)(2,1)S(1)}, bf16[256,256]{1,0:T(8,128)(2,1)S(1)}, u32[]{:S(2)}, u32[]{:S(2)}) collective-permute-start(bf16[256,256]{1,0:T(8,128)(2,1)S(1)} %slice.58), channel_id=1, source_target_pairs={{0,4},{4,8},{8,12},{12,0},{1,5},{5,9},{9,13},{13,1},{2,6},{6,10},{... | collective-permute-start | bytes 393224 | tf_op jit(solution)/shard_map/ppermute | solution.py:542
  69.5 6.3 %collective-permute-start.20 = (bf16[256,256]{1,0:T(8,128)(2,1)S(1)}, bf16[256,256]{1,0:T(8,128)(2,1)S(1)}, u32[]{:S(2)}, u32[]{:S(2)}) collective-permute-start(bf16[256,256]{1,0:T(8,128)(2,1)S(1)} %slice.59), channel_id=1, source_target_pairs={{0,12},{4,0},{8,4},{12,8},{1,13},{5,1},{9,5},{13,9},{2,14},{6,2},{... | collective-permute-start | bytes 393224 | tf_op jit(solution)/shard_map/ppermute | solution.py:542
  70.8 6.4 %copy-start.4 = (bf16[1536,256]{1,0:T(8,128)(2,1)S(1)}, bf16[1536,256]{1,0:T(8,128)(2,1)}, u32[]{:S(2)}) copy-start(bf16[1536,256]{1,0:T(8,128)(2,1)} %w_query.1) | copy-start | bytes 2359300
  70.8 6.4 %copy-start.5 = (bf16[1536,256]{1,0:T(8,128)(2,1)S(1)}, bf16[1536,256]{1,0:T(8,128)(2,1)}, u32[]{:S(2)}) copy-start(bf16[1536,256]{1,0:T(8,128)(2,1)} %w_key.1) | copy-start | bytes 2359300
  72.3 4.9 %copy-start.1 = (bf16[1536,768]{1,0:T(8,128)(2,1)S(1)}, bf16[1536,768]{1,0:T(8,128)(2,1)}, u32[]{:S(2)}) copy-start(bf16[1536,768]{1,0:T(8,128)(2,1)} %w_value.1) | copy-start | bytes 7077892
  72.3 4.9 %copy-start.7 = (bf16[128,1536]{1,0:T(8,128)(2,1)S(1)}, bf16[128,1536]{1,0:T(8,128)(2,1)}, u32[]{:S(2)}) copy-start(bf16[128,1536]{1,0:T(8,128)(2,1)} %get-tuple-element.173.z) | copy-start | bytes 1179652
  77.1 2.4 %collective-permute-start.21 = (bf16[4,192,512]{2,1,0:T(8,128)(2,1)S(1)}, bf16[4,192,512]{2,1,0:T(8,128)(2,1)S(1)}, u32[]{:S(2)}, u32[]{:S(2)}) collective-permute-start(bf16[4,192,512]{2,1,0:T(8,128)(2,1)S(1)} %get-tuple-element.152), channel_id=1, source_target_pairs={{0,1},{1,0},{2,3},{3,2},{4,5},{5,4},{6,7},{7,6},{8,9},{9,8},{10,11... | collective-permute-start | bytes 2359304 | tf_op jit(solution)/shard_map/ppermute | solution.py:554
  79.4 19.5 %copy-start.11 = (f32[2,3,1536]{2,0,1:T(2,128)S(1)}, f32[2,3,1536]{2,0,1:T(2,128)}, u32[]{:S(2)}) copy-start(f32[2,3,1536]{2,0,1:T(2,128)} %param.14) | copy-start | bytes 110596
  79.5 19.5 %copy-start.14 = (s32[2]{0:T(128)S(1)}, s32[2]{0:T(128)}, u32[]{:S(2)}) copy-start(s32[2]{0:T(128)} %dil.3) | copy-start | bytes 28
  80.3 13.5 %collective-permute-start.24 = (bf16[4,48,512]{2,1,0:T(8,128)(2,1)S(1)}, bf16[4,48,512]{2,1,0:T(8,128)(2,1)S(1)}, u32[]{:S(2)}, u32[]{:S(2)}) collective-permute-start(bf16[4,48,512]{2,1,0:T(8,128)(2,1)S(1)} %get-tuple-element.154), channel_id=1, source_target_pairs={{0,2},{2,0},{128,130},{130,128},{1,3},{3,1},{129,131},{131,129},{4... | collective-permute-start | bytes 589832 | tf_op jit(solution)/shard_map/ppermute | solution.py:716
  80.7 13.3 %collective-permute-start.25 = (bf16[4,48,512]{2,1,0:T(8,128)(2,1)S(1)}, bf16[4,48,512]{2,1,0:T(8,128)(2,1)S(1)}, u32[]{:S(2)}, u32[]{:S(2)}) collective-permute-start(bf16[4,48,512]{2,1,0:T(8,128)(2,1)S(1)} %get-tuple-element.155), channel_id=1, source_target_pairs={{0,128},{2,130},{128,0},{130,2},{1,129},{3,131},{129,1},{131,3},{4... | collective-permute-start | bytes 589832 | tf_op jit(solution)/shard_map/ppermute | solution.py:716
  84.1 12.2 %collective-permute-start.26 = (bf16[4,48,512]{2,1,0:T(8,128)(2,1)S(1)}, bf16[4,48,512]{2,1,0:T(8,128)(2,1)S(1)}, u32[]{:S(2)}, u32[]{:S(2)}) collective-permute-start(bf16[4,48,512]{2,1,0:T(8,128)(2,1)S(1)} %get-tuple-element.156), channel_id=1, source_target_pairs={{0,130},{2,128},{128,2},{130,0},{1,131},{3,129},{129,3},{131,1},{4... | collective-permute-start | bytes 589832 | tf_op jit(solution)/shard_map/ppermute | solution.py:716
  85.1 7.5 %collective-permute-start.22 = (bf16[32,1536]{1,0:T(8,128)(2,1)S(1)}, bf16[32,1536]{1,0:T(8,128)(2,1)S(1)}, u32[]{:S(2)}, u32[]{:S(2)}) collective-permute-start(bf16[32,1536]{1,0:T(8,128)(2,1)S(1)} %get-tuple-element.184), channel_id=1, source_target_pairs={{0,1},{1,2},{2,3},{3,4},{4,5},{5,6},{6,7},{7,8},{8,9},{9,10},{10,1... | collective-permute-start | bytes 294920 | tf_op jit(solution)/shard_map/ppermute | solution.py:559
  87.0 6.7 %collective-permute-start.23 = (bf16[32,1536]{1,0:T(8,128)(2,1)S(1)}, bf16[32,1536]{1,0:T(8,128)(2,1)S(1)}, u32[]{:S(2)}, u32[]{:S(2)}) collective-permute-start(bf16[32,1536]{1,0:T(8,128)(2,1)S(1)} %get-tuple-element.183), channel_id=1, source_target_pairs={{1,0},{2,1},{3,2},{4,3},{5,4},{6,5},{7,6},{8,7},{9,8},{10,9},{11,1... | collective-permute-start | bytes 294920 | tf_op jit(solution)/shard_map/ppermute | solution.py:560
  97.0 16.7 %copy-start = (bf16[768,1536]{1,0:T(8,128)(2,1)S(1)}, bf16[768,1536]{1,0:T(8,128)(2,1)}, u32[]{:S(2)}) copy-start(bf16[768,1536]{1,0:T(8,128)(2,1)} %w_out.1) | copy-start | bytes 7077892
  97.0 4.9 %collective-permute-start.27 = (bf16[4,24,512]{2,1,0:T(8,128)(2,1)S(1)}, bf16[4,24,512]{2,1,0:T(8,128)(2,1)S(1)}, u32[]{:S(2)}, u32[]{:S(2)}) collective-permute-start(bf16[4,24,512]{2,1,0:T(8,128)(2,1)S(1)} %get-tuple-element.165), channel_id=1, source_target_pairs={{0,16},{16,0},{32,48},{48,32},{64,80},{80,64},{96,112},{112,96},{1... | collective-permute-start | bytes 294920 | tf_op jit(solution)/shard_map/ppermute | solution.py:722
  102.5 13.1 %collective-permute-start.28 = (f32[4,6,512]{2,1,0:T(8,128)S(1)}, f32[4,6,512]{2,1,0:T(8,128)S(1)}, u32[]{:S(2)}, u32[]{:S(2)}) collective-permute-start(f32[4,6,512]{2,1,0:T(8,128)S(1)} %get-tuple-element.174), channel_id=1, source_target_pairs={{0,64},{16,80},{32,96},{48,112},{64,0},{80,16},{96,32},{112,48},{1... | collective-permute-start | bytes 147464 | tf_op jit(solution)/shard_map/ppermute | solution.py:542
  109.6 6.5 %collective-permute-start.29 = (f32[4,6,512]{2,1,0:T(8,128)S(1)}, f32[4,6,512]{2,1,0:T(8,128)S(1)}, u32[]{:S(2)}, u32[]{:S(2)}) collective-permute-start(f32[4,6,512]{2,1,0:T(8,128)S(1)} %get-tuple-element.175), channel_id=1, source_target_pairs={{0,32},{16,48},{32,64},{48,80},{64,96},{80,112},{96,0},{112,16},{1... | collective-permute-start | bytes 147464 | tf_op jit(solution)/shard_map/ppermute | solution.py:542
  111.0 5.6 %collective-permute-start.30 = (f32[4,6,512]{2,1,0:T(8,128)S(1)}, f32[4,6,512]{2,1,0:T(8,128)S(1)}, u32[]{:S(2)}, u32[]{:S(2)}) collective-permute-start(f32[4,6,512]{2,1,0:T(8,128)S(1)} %get-tuple-element.176), channel_id=1, source_target_pairs={{0,96},{16,112},{32,0},{48,16},{64,32},{80,48},{96,64},{112,80},{1... | collective-permute-start | bytes 147464 | tf_op jit(solution)/shard_map/ppermute | solution.py:542

commit v3 on v2

--- a/solution.py
+++ b/solution.py
@@ -274,9 +274,10 @@
     top = None
     for j, block in enumerate(blocks):
         other = jnp.bitwise_xor(c, j)
+        product = contract(block[...], queries, 1, 1)
         for i in range(HEADS):
             at = j * many + i * tok
-            part = contract(block[i * tok : (i + 1) * tok, :], queries, 1, 1)
+            part = product[i * tok : (i + 1) * tok, :]
             bias = jnp.concatenate(
                 [
                     master[:, pl.ds(pl.multiple_of((4 * (q - bands[i]) + c - other + 15) * tok, tok), tok)]
@@ -296,12 +297,13 @@
     scale = 1.0 / total
     delta = jnp.zeros_like(top)
     for j, block in enumerate(blocks):
+        product = contract(block[...], d_att, 1, 1)
         for i in range(HEADS):
             at = j * many + i * tok
             probs = score[at : at + tok, :] * scale
             score[at : at + tok, :] = probs
             soft[at : at + tok, :] = probs.astype(BF16)
-            part = contract(block[i * tok : (i + 1) * tok, :], d_att, 1, 1)
+            part = product[i * tok : (i + 1) * tok, :]
             pull[at : at + tok, :] = part
             delta = delta + jnp.sum(part * probs, axis=0, keepdims=True)
     for at in range(0, 4 * many, tok):

time: 118 us -> 117 us (level)
  waiting for transfers between devices: 29 us -> 30.3 us
  Pallas kernels: 35.3 us -> 34.1 us
    ppermute x17, waiting for transfers between devices: 18.2 us -> 19.7 us  [shift(): lax.ppermute(array, axis, [(i, (i + step) % count) for i in range(count)])]
    pallas_call x18, Pallas kernels: 35.3 us -> 34.1 us  [call(): pl.pallas_call(body, out_shape=tuple((jax.ShapeDtypeStruct(s, d) for s, d...]
  transfers between devices with their start and end apart: 31 -> 31, of which waited for: 18 -> 20; matrix products, arithmetic and copies ran while one was open for 0% -> 0% of each run, Pallas kernels for 21% -> 20%
where the time goes in v3:
time: 117 us
  starting transfers between devices  48.1 us (41%)
  Pallas kernels  34.1 us (29%)
  waiting for transfers between devices  30.3 us (26%)
  local copies, waits for them, and re-layouts  3.66 us (3%)
    pallas_call x18, Pallas kernels, call(): pl.pallas_call(body, out_shape=tuple((jax.ShapeDtypeStruct(s, d) for s, d...  34.1 us
    ppermute x17, starting transfers between devices, shift(): lax.ppermute(array, axis, [(i, (i + step) % count) for i in range(count)])  26 us
    ppermute x17, waiting for transfers between devices, shift(): lax.ppermute(array, axis, [(i, (i + step) % count) for i in range(count)])  19.7 us
    ppermute x2, starting transfers between devices, halo(): lax.ppermute(rows[:width], SEQ, [(i + 1, i) for i in range(nseq - 1)])  9.08 us
    ppermute x6, waiting for transfers between devices, flip(): return lax.ppermute(array, axis, [(0, 1), (1, 0)])  6.11 us
    ppermute x3, starting transfers between devices, local(): got.append(lax.ppermute(send, ('xh', 'xl'), way))  4.79 us
    ppermute x2, starting transfers between devices, halo(): lax.ppermute(rows[-width:], SEQ, [(i, i + 1) for i in range(nseq - 1)])  3.84 us
    ppermute x6, starting transfers between devices, flip(): return lax.ppermute(array, axis, [(0, 1), (1, 0)])  2.4 us
  transfers between devices with their start and end apart: 31, of which 20 were waited for; matrix products, arithmetic and copies ran while one was open for 0% of the time, Pallas kernels for 20%

profile of v3, /device:TPU:24, one launch (start us, length us, event | category | flops | bytes accessed | tf_op | source)
XLA Modules:
  0.0 117.1 jit_solution(8806544945311460115)
XLA Ops:
  0.6 1.0 slice_bitcast_fusion
  1.6 1.9 %collective-permute-start = (bf16[32,1536]{1,0:T(8,128)(2,1)S(1)}, bf16[32,1536]{1,0:T(8,128)(2,1)S(1)}, u32[]{:S(2)}, u32[]{:S(2)}) collective-permute-start(bf16[32,1536]{1,0:T(8,128)(2,1)S(1)} %get-tuple-element.186), channel_id=1, source_target_pairs={{0,1},{1,2},{2,3},{3,4},{4,5},{5,6},{6,7},{7,8},{8,9},{9,10},{10,1... | collective-permute-start | bytes 294920 | tf_op jit(solution)/shard_map/ppermute | solution.py:561
  3.5 4.5 %collective-permute-start.1 = (bf16[32,1536]{1,0:T(8,128)(2,1)S(1)}, bf16[32,1536]{1,0:T(8,128)(2,1)S(1)}, u32[]{:S(2)}, u32[]{:S(2)}) collective-permute-start(bf16[32,1536]{1,0:T(8,128)(2,1)S(1)} %get-tuple-element.185), channel_id=1, source_target_pairs={{1,0},{2,1},{3,2},{4,3},{5,4},{6,5},{7,6},{8,7},{9,8},{10,9},{11,1... | collective-permute-start | bytes 294920 | tf_op jit(solution)/shard_map/ppermute | solution.py:562
  8.1 4.2 %prelude.1 = (bf16[128,1536]{1,0:T(8,128)(2,1)}, bf16[128,768]{1,0:T(8,128)(2,1)}) custom-call(bf16[128,1536]{1,0:T(8,128)(2,1)} %bitcast.19, f32[3,1536]{1,0:T(4,128)} %gains.7, bf16[128,1536]{1,0:T(8,128)(2,1)} %bitcast.23, bf16[768,1536]{1,0:T(8,128)(2,1)} %w_out.1), custom_call_target="tpu_custom_call" | custom-call | flops 1000 | bytes 10800000 | tf_op jit(solution)/shard_map/prelude/pallas_call | solution.py:43
  12.4 0.6 copy-done.16
  13.0 5.3 %forward.1 = (bf16[128,512]{1,0:T(8,128)(2,1)}, bf16[128,512]{1,0:T(8,128)(2,1)}, bf16[128,512]{1,0:T(8,128)(2,1)}, bf16[128,512]{1,0:T(8,128)(2,1)}, bf16[128,1...) custom-call(s32[2]{0:T(128)} %dil.3, bf16[32,1536]{1,0:T(8,128)(2,1)} %copy-done.16, ...), custom_call_target="tpu_custom_call" | custom-call | flops 1000 | bytes 18000000 | tf_op jit(solution)/shard_map/forward/pallas_call | solution.py:43
  18.5 2.8 %collective-permute-start.3 = (bf16[128,512]{1,0:T(8,128)(2,1)}, bf16[128,512]{1,0:T(8,128)(2,1)S(1)}, u32[]{:S(2)}, u32[]{:S(2)}) collective-permute-start(bf16[128,512]{1,0:T(8,128)(2,1)} %get-tuple-element.97), channel_id=1, source_target_pairs={{0,8},{4,12},{8,0},{12,4},{1,9},{5,13},{9,1},{13,5},{2,10},{6,14},... | collective-permute-start | bytes 393224 | tf_op jit(solution)/shard_map/ppermute | solution.py:544
  21.4 1.0 copy-done.8
  22.4 1.6 %shuffle.1 = (bf16[128,768]{1,0:T(8,128)(2,1)S(1)}, bf16[128,768]{1,0:T(8,128)(2,1)S(1)}, bf16[128,768]{1,0:T(8,128)(2,1)S(1)}, bf16[128,768]{1,0:T(8,128)(2,1)S(1)}) custom-call(s32[10]{0:T(128)S(1)} %stack.35.where, s32[1,768]{1,0:T(1,128)S(1)} %copy-done.13, bf16[128,1536]{1,0:T(8,128)(2,1)S(1)} %copy-done.8, bf16[128,1536]{1,0:T(8,128)(2,1)S(1)} %bitcast.24), custom_call_target="tpu_custom_call" | custom-call | flops 1000 | bytes 5760000 | tf_op jit(solution)/shard_map/shuffle/pallas_call | solution.py:43
  23.9 0.5 collective-permute-done.2.m1
  24.4 2.3 %collective-permute-done.3.m2 = bf16[128,512]{1,0:T(8,128)(2,1)S(1)} collective-permute-done((bf16[128,512]{1,0:T(8,128)(2,1)}, bf16[128,512]{1,0:T(8,128)(2,1)S(1)}, u32[]{:S(2)}, u32[]{:S(2)}) %collective-permute-start.3) | collective-permute-done | bytes 131104 | tf_op jit(solution)/shard_map/ppermute | solution.py:544
  26.7 1.2 %collective-permute-done.4.m3 = bf16[128,512]{1,0:T(8,128)(2,1)S(1)} collective-permute-done((bf16[128,512]{1,0:T(8,128)(2,1)}, bf16[128,512]{1,0:T(8,128)(2,1)S(1)}, u32[]{:S(2)}, u32[]{:S(2)}) %collective-permute-start.4) | collective-permute-done | bytes 131104 | tf_op jit(solution)/shard_map/ppermute | solution.py:544
  27.9 0.8 slice.46
  28.8 1.6 %collective-permute-start.6 = (bf16[512,256]{1,0:T(8,128)(2,1)S(1)}, bf16[512,256]{1,0:T(8,128)(2,1)S(1)}, u32[]{:S(2)}, u32[]{:S(2)}) collective-permute-start(bf16[512,256]{1,0:T(8,128)(2,1)S(1)} %pad_maximum_fusion), channel_id=1, source_target_pairs={{0,2},{2,0},{1,3},{3,1},{4,6},{6,4},{5,7},{7,5},{8,10},{10,8},{9,1... | collective-permute-start | bytes 786440 | tf_op jit(solution)/shard_map/ppermute | solution.py:556
  30.4 0.6 collective-permute-start.7
  31.0 1.5 %collective-permute-start.8 = (bf16[128,768]{1,0:T(8,128)(2,1)S(1)}, bf16[128,768]{1,0:T(8,128)(2,1)S(1)}, u32[]{:S(2)}, u32[]{:S(2)}) collective-permute-start(bf16[128,768]{1,0:T(8,128)(2,1)S(1)} %get-tuple-element.109), channel_id=1, source_target_pairs={{0,12},{4,0},{8,4},{12,8},{1,13},{5,1},{9,5},{13,9},{2,14},{6,2},{... | collective-permute-start | bytes 589832 | tf_op jit(solution)/shard_map/ppermute | solution.py:544
  32.5 1.5 %expand.1.master = f32[128,4096]{1,0:T(8,128)S(1)} custom-call(s32[10]{0:T(128)S(1)} %stack.35.where, f32[4,64]{1,0:T(4,128)S(1)} %bitcast.29, s32[1,4095]{1,0:T(1,128)S(1)} %bitcast.28), custom_call_target="tpu_custom_call" | custom-call | flops 1000 | bytes 5400000 | tf_op jit(solution)/shard_map/expand/pallas_call | solution.py:43
  34.0 2.6 %collective-permute-done.7.f1 = bf16[128,768]{1,0:T(8,128)(2,1)S(1)} collective-permute-done((bf16[128,768]{1,0:T(8,128)(2,1)S(1)}, bf16[128,768]{1,0:T(8,128)(2,1)S(1)}, u32[]{:S(2)}, u32[]{:S(2)}) %collective-permute-start.7) | collective-permute-done | bytes 196640 | tf_op jit(solution)/shard_map/ppermute | solution.py:544
  36.6 1.3 %collective-permute-done.8.f3 = bf16[128,768]{1,0:T(8,128)(2,1)S(1)} collective-permute-done((bf16[128,768]{1,0:T(8,128)(2,1)S(1)}, bf16[128,768]{1,0:T(8,128)(2,1)S(1)}, u32[]{:S(2)}, u32[]{:S(2)}) %collective-permute-start.8) | collective-permute-done | bytes 196640 | tf_op jit(solution)/shard_map/ppermute | solution.py:544
  37.9 1.1 collective-permute-start.10
  39.0 0.4 collective-permute-done.9.kv3
  39.4 5.6 %attend.1 = (bf16[512,256]{1,0:T(8,128)(2,1)S(1)}, f32[512,256]{1,0:T(8,128)S(1)}, f32[512,256]{1,0:T(8,128)S(1)}, bf16[1024,256]{1,0:T(8,128)(2,1)S(1)}) custom-call(s32[10]{0:T(128)S(1)} %stack.35.where, bf16[128,512]{1,0:T(8,128)(2,1)S(1)} %copy-done.10, bf16[128,512]{1,0:T(8,128)(2,1)S(1)} %collective-permute-done.2.m1, ...), custom_call_target="tpu_custom_call" | custom-call | flops 1000 | bytes 25200000 | tf_op jit(solution)/shard_map/attend/pallas_call | solution.py:43
  45.0 1.7 %collective-permute-done.10.f2 = bf16[128,768]{1,0:T(8,128)(2,1)S(1)} collective-permute-done((bf16[128,768]{1,0:T(8,128)(2,1)S(1)}, bf16[128,768]{1,0:T(8,128)(2,1)S(1)}, u32[]{:S(2)}, u32[]{:S(2)}) %collective-permute-start.10) | collective-permute-done | bytes 196640 | tf_op jit(solution)/shard_map/ppermute | solution.py:544
  46.7 1.9 %collective-permute-done.11.got = bf16[1024,256]{1,0:T(8,128)(2,1)S(1)} collective-permute-done((bf16[1024,256]{1,0:T(8,128)(2,1)S(1)}, bf16[1024,256]{1,0:T(8,128)(2,1)S(1)}, u32[]{:S(2)}, u32[]{:S(2)}) %collective-permute-start.11) | collective-permute-done | bytes 524320 | tf_op jit(solution)/shard_map/ppermute | solution.py:556
  48.7 0.7 collective-permute-start.16
  49.4 0.3 collective-permute-start.12
  49.8 1.7 %collective-permute-start.14 = (bf16[512,256]{1,0:T(8,128)(2,1)S(1)}, bf16[512,256]{1,0:T(8,128)(2,1)S(1)}, u32[]{:S(2)}, u32[]{:S(2)}) collective-permute-start(bf16[512,256]{1,0:T(8,128)(2,1)S(1)} %get-tuple-element.168.t0), channel_id=1, source_target_pairs={{0,12},{4,0},{8,4},{12,8},{1,13},{5,1},{9,5},{13,9},{2,14},{6,2},{... | collective-permute-start | bytes 786440 | tf_op jit(solution)/shard_map/ppermute | solution.py:544
  51.5 1.0 slopes.1
  52.5 0.9 turn.1
  53.4 3.8 %collective-permute-done.16.got = bf16[512,256]{1,0:T(8,128)(2,1)S(1)} collective-permute-done((bf16[512,256]{1,0:T(8,128)(2,1)S(1)}, bf16[512,256]{1,0:T(8,128)(2,1)S(1)}, u32[]{:S(2)}, u32[]{:S(2)}) %collective-permute-start.16) | collective-permute-done | bytes 262176 | tf_op jit(solution)/shard_map/ppermute | solution.py:556
  57.2 0.6 second_sum.1.d0
  57.8 0.6 collective-permute-start.17
  58.4 1.5 %collective-permute-start.19 = (bf16[512,256]{1,0:T(8,128)(2,1)S(1)}, bf16[512,256]{1,0:T(8,128)(2,1)S(1)}, u32[]{:S(2)}, u32[]{:S(2)}) collective-permute-start(bf16[512,256]{1,0:T(8,128)(2,1)S(1)} %second_sum.1.d0), channel_id=1, source_target_pairs={{0,12},{4,0},{8,4},{12,8},{1,13},{5,1},{9,5},{13,9},{2,14},{6,2},{... | collective-permute-start | bytes 786440 | tf_op jit(solution)/shard_map/ppermute | solution.py:544
  59.9 1.9 %collective-permute-start.13 = (bf16[256,256]{1,0:T(8,128)(2,1)S(1)}, bf16[256,256]{1,0:T(8,128)(2,1)S(1)}, u32[]{:S(2)}, u32[]{:S(2)}) collective-permute-start(bf16[256,256]{1,0:T(8,128)(2,1)S(1)} %slice.56), channel_id=1, source_target_pairs={{0,4},{4,8},{8,12},{12,0},{1,5},{5,9},{9,13},{13,1},{2,6},{6,10},{... | collective-permute-start | bytes 393224 | tf_op jit(solution)/shard_map/ppermute | solution.py:544
  61.8 0.3 collective-permute-start.15
  62.1 4.7 %collective-permute-done.17.d1 = bf16[512,256]{1,0:T(8,128)(2,1)S(1)} collective-permute-done((bf16[512,256]{1,0:T(8,128)(2,1)S(1)}, bf16[512,256]{1,0:T(8,128)(2,1)S(1)}, u32[]{:S(2)}, u32[]{:S(2)}) %collective-permute-start.17) | collective-permute-done | bytes 262176 | tf_op jit(solution)/shard_map/ppermute | solution.py:544
  66.8 2.0 %collective-permute-start.18 = (bf16[256,256]{1,0:T(8,128)(2,1)S(1)}, bf16[256,256]{1,0:T(8,128)(2,1)S(1)}, u32[]{:S(2)}, u32[]{:S(2)}) collective-permute-start(bf16[256,256]{1,0:T(8,128)(2,1)S(1)} %slice.58), channel_id=1, source_target_pairs={{0,4},{4,8},{8,12},{12,0},{1,5},{5,9},{9,13},{13,1},{2,6},{6,10},{... | collective-permute-start | bytes 393224 | tf_op jit(solution)/shard_map/ppermute | solution.py:544
  68.9 0.4 collective-permute-start.20
  69.2 0.3 collective-permute-done.13.t2
  69.8 1.5 %weigh_first.1.before = f32[2,4,192,256]{3,2,1,0:T(8,128)S(1)} custom-call(s32[10]{0:T(128)S(1)} %stack.35.where, bf16[384,512]{1,0:T(8,128)(2,1)S(1)} %get-tuple-element.141.n_turned, bf16[384,512]{1,0:T(8,128)(2,1)S(1)} %get-tuple-element.144.u_turned, bf16[512,256]{1,0:T(8,128)(2,1)S(1)} %get-tuple-element.168.t0, ...), custom_call_target="tpu_custom_call" | custom-call | flops 1000 | bytes 7200000 | tf_op jit(solution)/shard_map/weigh_first/pallas_call | solution.py:43
  71.3 0.7 collective-permute-done.18.d2
  72.1 3.0 %collective-permute-done.20.d3 = bf16[256,256]{1,0:T(8,128)(2,1)S(1)} collective-permute-done((bf16[256,256]{1,0:T(8,128)(2,1)S(1)}, bf16[256,256]{1,0:T(8,128)(2,1)S(1)}, u32[]{:S(2)}, u32[]{:S(2)}) %collective-permute-start.20) | collective-permute-done | bytes 131104 | tf_op jit(solution)/shard_map/ppermute | solution.py:544
  75.1 1.3 %weigh_second.1 = (f32[4,192,512]{2,1,0:T(8,128)S(1)}, bf16[4,192,512]{2,1,0:T(8,128)(2,1)S(1)}) custom-call(s32[10]{0:T(128)S(1)} %stack.35.where, bf16[384,512]{1,0:T(8,128)(2,1)S(1)} %get-tuple-element.141.n_turned, bf16[512,256]{1,0:T(8,128)(2,1)S(1)} %second_sum.1.d0, bf16[512,256]{1,0:T(8,128)(2,1)S(1)} %collective-permute-done.17.d1, ...), custom_call_target="tpu_custom_call" | custom-call | flops 1000 | bytes 5400000 | tf_op jit(solution)/shard_map/weigh_second/pallas_call | solution.py:43
  76.6 2.2 %grad_top.1.grad = bf16[128,1536]{1,0:T(8,128)(2,1)S(1)} custom-call(s32[10]{0:T(128)S(1)} %stack.35.where, bf16[512,256]{1,0:T(8,128)(2,1)S(1)} %get-tuple-element.168.t0, bf16[512,256]{1,0:T(8,128)(2,1)S(1)} %collective-permute-done.12.t1, bf16[256,256]{1,0:T(8,128)(2,1)S(1)} %collective-permute-done.13.t2, ...), custom_call_target="tpu_custom_call" | custom-call | flops 1000 | bytes 10800000 | tf_op jit(solution)/shard_map/grad_top/pallas_call | solution.py:43
  78.8 0.8 fold.2
  79.7 0.5 collective-permute-start.24
  80.1 3.2 %collective-permute-start.25 = (bf16[4,48,512]{2,1,0:T(8,128)(2,1)S(1)}, bf16[4,48,512]{2,1,0:T(8,128)(2,1)S(1)}, u32[]{:S(2)}, u32[]{:S(2)}) collective-permute-start(bf16[4,48,512]{2,1,0:T(8,128)(2,1)S(1)} %get-tuple-element.155), channel_id=1, source_target_pairs={{0,128},{2,130},{128,0},{130,2},{1,129},{3,131},{129,1},{131,3},{4... | collective-permute-start | bytes 589832 | tf_op jit(solution)/shard_map/ppermute | solution.py:718
  83.3 1.2 collective-permute-start.26
  84.5 1.9 %collective-permute-start.22 = (bf16[32,1536]{1,0:T(8,128)(2,1)S(1)}, bf16[32,1536]{1,0:T(8,128)(2,1)S(1)}, u32[]{:S(2)}, u32[]{:S(2)}) collective-permute-start(bf16[32,1536]{1,0:T(8,128)(2,1)S(1)} %get-tuple-element.184), channel_id=1, source_target_pairs={{0,1},{1,2},{2,3},{3,4},{4,5},{5,6},{6,7},{7,8},{8,9},{9,10},{10,1... | collective-permute-start | bytes 294920 | tf_op jit(solution)/shard_map/ppermute | solution.py:561
  86.4 4.5 %collective-permute-start.23 = (bf16[32,1536]{1,0:T(8,128)(2,1)S(1)}, bf16[32,1536]{1,0:T(8,128)(2,1)S(1)}, u32[]{:S(2)}, u32[]{:S(2)}) collective-permute-start(bf16[32,1536]{1,0:T(8,128)(2,1)S(1)} %get-tuple-element.183), channel_id=1, source_target_pairs={{1,0},{2,1},{3,2},{4,3},{5,4},{6,5},{7,6},{8,7},{9,8},{10,9},{11,1... | collective-permute-start | bytes 294920 | tf_op jit(solution)/shard_map/ppermute | solution.py:562
  90.9 1.3 %collective-permute-done.22.left = bf16[32,1536]{1,0:T(8,128)(2,1)S(1)} collective-permute-done((bf16[32,1536]{1,0:T(8,128)(2,1)S(1)}, bf16[32,1536]{1,0:T(8,128)(2,1)S(1)}, u32[]{:S(2)}, u32[]{:S(2)}) %collective-permute-start.22) | collective-permute-done | bytes 98336 | tf_op jit(solution)/shard_map/ppermute | solution.py:561
  92.3 0.9 collective-permute-done.23.right
  93.2 2.2 %collective-permute-done.26.refs_2_ = bf16[4,48,512]{2,1,0:T(8,128)(2,1)S(1)} collective-permute-done((bf16[4,48,512]{2,1,0:T(8,128)(2,1)S(1)}, bf16[4,48,512]{2,1,0:T(8,128)(2,1)S(1)}, u32[]{:S(2)}, u32[]{:S(2)}) %collective-permute-start.26) | collective-permute-done | bytes 196640 | tf_op jit(solution)/shard_map/ppermute | solution.py:718
  95.4 0.7 fold.3
  96.1 2.0 %collective-permute-start.27 = (bf16[4,24,512]{2,1,0:T(8,128)(2,1)S(1)}, bf16[4,24,512]{2,1,0:T(8,128)(2,1)S(1)}, u32[]{:S(2)}, u32[]{:S(2)}) collective-permute-start(bf16[4,24,512]{2,1,0:T(8,128)(2,1)S(1)} %get-tuple-element.165), channel_id=1, source_target_pairs={{0,16},{16,0},{32,48},{48,32},{64,80},{80,64},{96,112},{112,96},{1... | collective-permute-start | bytes 294920 | tf_op jit(solution)/shard_map/ppermute | solution.py:724
  98.1 2.9 %backward.1 = bf16[128,1536]{1,0:T(8,128)(2,1)} custom-call(s32[10]{0:T(128)S(1)} %stack.35.where, s32[2]{0:T(128)S(1)} %copy-done.14, bf16[32,1536]{1,0:T(8,128)(2,1)S(1)} %collective-permute-done.22.left, bf16[32,1536]{1,0:T(8,128)(2,1)S(1)} %collective-permute-done.23.right, bf16[128,1536]{1,0:T(8,128)(2,1)S(1)} %grad_top.1.grad, ...), custom_call_target="tpu_custom_call" | custom-call | flops 1000 | bytes 16559999 | tf_op jit(solution)/shard_map/backward/pallas_call | solution.py:43
  101.0 0.6 last_fold.1
  101.6 7.1 %collective-permute-start.28 = (f32[4,6,512]{2,1,0:T(8,128)S(1)}, f32[4,6,512]{2,1,0:T(8,128)S(1)}, u32[]{:S(2)}, u32[]{:S(2)}) collective-permute-start(f32[4,6,512]{2,1,0:T(8,128)S(1)} %get-tuple-element.174), channel_id=1, source_target_pairs={{0,64},{16,80},{32,96},{48,112},{64,0},{80,16},{96,32},{112,48},{1... | collective-permute-start | bytes 147464 | tf_op jit(solution)/shard_map/ppermute | solution.py:544
  108.7 1.5 %collective-permute-start.29 = (f32[4,6,512]{2,1,0:T(8,128)S(1)}, f32[4,6,512]{2,1,0:T(8,128)S(1)}, u32[]{:S(2)}, u32[]{:S(2)}) collective-permute-start(f32[4,6,512]{2,1,0:T(8,128)S(1)} %get-tuple-element.175), channel_id=1, source_target_pairs={{0,32},{16,48},{32,64},{48,80},{64,96},{80,112},{96,0},{112,16},{1... | collective-permute-start | bytes 147464 | tf_op jit(solution)/shard_map/ppermute | solution.py:544
  110.2 2.7 %collective-permute-start.30 = (f32[4,6,512]{2,1,0:T(8,128)S(1)}, f32[4,6,512]{2,1,0:T(8,128)S(1)}, u32[]{:S(2)}, u32[]{:S(2)}) collective-permute-start(f32[4,6,512]{2,1,0:T(8,128)S(1)} %get-tuple-element.176), channel_id=1, source_target_pairs={{0,96},{16,112},{32,0},{48,16},{64,32},{80,48},{96,64},{112,80},{1... | collective-permute-start | bytes 147464 | tf_op jit(solution)/shard_map/ppermute | solution.py:544
  112.8 1.9 %project.1 = bf16[128,1536]{1,0:T(8,128)(2,1)} custom-call(s32[10]{0:T(128)S(1)} %stack.35.where, bf16[512,256]{1,0:T(8,128)(2,1)S(1)} %get-tuple-element.168.t0, bf16[512,256]{1,0:T(8,128)(2,1)S(1)} %collective-permute-done.12.t1, bf16[256,256]{1,0:T(8,128)(2,1)S(1)} %collective-permute-done.13.t2, bf16[256,256]{1,0:T(8,128)(2,1)S(1)} %collective-permute-done.15.t3, ...), custom_call_target="tpu_custom_call" | custom-call | flops 1000 | bytes 36000 | tf_op jit(solution)/shard_map/project/pallas_call | solution.py:43
  114.7 0.5 collective-permute-done.29.refs_2_
  115.2 0.6 collective-permute-done.30.refs_3_
  115.8 1.3 %arrange.1 = f32[6,2048]{1,0:T(8,128)} custom-call(s32[10]{0:T(128)S(1)} %stack.35.where, f32[4,6,512]{2,1,0:T(8,128)S(1)} %get-tuple-element.179.refs_0_, f32[4,6,512]{2,1,0:T(8,128)S(1)} %collective-permute-done.28.refs_1_, f32[4,6,512]{2,1,0:T(8,128)S(1)} %collective-permute-done.29.refs_2_, f32[4,6,512]{2,1,0:T(8,128)S(1)} %collective-permute-done.30.refs_3_), custom_call_target="tpu_custom_call" | custom-call | flops 1000 | bytes 3600000 | tf_op jit(solution)/shard_map/arrange/pallas_call | solution.py:43
  (64 shorter events, 0.9 us)
Async XLA Ops:
  1.6 10.7 %collective-permute-start = (bf16[32,1536]{1,0:T(8,128)(2,1)S(1)}, bf16[32,1536]{1,0:T(8,128)(2,1)S(1)}, u32[]{:S(2)}, u32[]{:S(2)}) collective-permute-start(bf16[32,1536]{1,0:T(8,128)(2,1)S(1)} %get-tuple-element.186), channel_id=1, source_target_pairs={{0,1},{1,2},{2,3},{3,4},{4,5},{5,6},{6,7},{7,8},{8,9},{9,10},{10,1... | collective-permute-start | bytes 294920 | tf_op jit(solution)/shard_map/ppermute | solution.py:561
  3.5 8.8 %collective-permute-start.1 = (bf16[32,1536]{1,0:T(8,128)(2,1)S(1)}, bf16[32,1536]{1,0:T(8,128)(2,1)S(1)}, u32[]{:S(2)}, u32[]{:S(2)}) collective-permute-start(bf16[32,1536]{1,0:T(8,128)(2,1)S(1)} %get-tuple-element.185), channel_id=1, source_target_pairs={{1,0},{2,1},{3,2},{4,3},{5,4},{6,5},{7,6},{8,7},{9,8},{10,9},{11,1... | collective-permute-start | bytes 294920 | tf_op jit(solution)/shard_map/ppermute | solution.py:562
  12.3 0.6 copy-start.16
  12.3 0.6 copy-start.17
  13.0 8.3 %copy-start.3 = (bf16[1,128,1536]{2,1,0:T(8,128)(2,1)S(1)}, bf16[1,128,1536]{2,1,0:T(8,128)(2,1)}, u32[]{:S(2)}) copy-start(bf16[1,128,1536]{2,1,0:T(8,128)(2,1)} %param.22) | copy-start | bytes 1179652
  13.0 8.3 %copy-start.13 = (s32[1,768]{1,0:T(1,128)S(1)}, s32[1,768]{1,0:T(1,128)}, u32[]{:S(2)}) copy-start(s32[1,768]{1,0:T(1,128)} %constant.50.clone.order) | copy-start | bytes 9220
  13.0 19.4 %copy-start.12 = (s32[4095]{0:T(1024)S(1)}, s32[4095]{0:T(1024)}, u32[]{:S(2)}) copy-start(s32[4095]{0:T(1024)} %param.17) | copy-start | bytes 49144
  13.0 19.4 %copy-start.15 = (f32[64,4]{0,1:T(4,128)S(1)}, f32[64,4]{0,1:T(4,128)}, u32[]{:S(2)}) copy-start(f32[64,4]{0,1:T(4,128)} %param.16) | copy-start | bytes 3076
  18.4 6.1 %collective-permute-start.2 = (bf16[128,512]{1,0:T(8,128)(2,1)}, bf16[128,512]{1,0:T(8,128)(2,1)S(1)}, u32[]{:S(2)}, u32[]{:S(2)}) collective-permute-start(bf16[128,512]{1,0:T(8,128)(2,1)} %get-tuple-element.96), channel_id=1, source_target_pairs={{0,4},{4,8},{8,12},{12,0},{1,5},{5,9},{9,13},{13,1},{2,6},{6,10},{... | collective-permute-start | bytes 393224 | tf_op jit(solution)/shard_map/ppermute | solution.py:544
  18.5 8.3 %collective-permute-start.3 = (bf16[128,512]{1,0:T(8,128)(2,1)}, bf16[128,512]{1,0:T(8,128)(2,1)S(1)}, u32[]{:S(2)}, u32[]{:S(2)}) collective-permute-start(bf16[128,512]{1,0:T(8,128)(2,1)} %get-tuple-element.97), channel_id=1, source_target_pairs={{0,8},{4,12},{8,0},{12,4},{1,9},{5,13},{9,1},{13,5},{2,10},{6,14},... | collective-permute-start | bytes 393224 | tf_op jit(solution)/shard_map/ppermute | solution.py:544
  21.3 6.6 %collective-permute-start.4 = (bf16[128,512]{1,0:T(8,128)(2,1)}, bf16[128,512]{1,0:T(8,128)(2,1)S(1)}, u32[]{:S(2)}, u32[]{:S(2)}) collective-permute-start(bf16[128,512]{1,0:T(8,128)(2,1)} %get-tuple-element.98), channel_id=1, source_target_pairs={{0,12},{4,0},{8,4},{12,8},{1,13},{5,1},{9,5},{13,9},{2,14},{6,2},{... | collective-permute-start | bytes 393224 | tf_op jit(solution)/shard_map/ppermute | solution.py:544
  21.4 1.0 copy-start.8
  22.4 17.1 %copy-start.10 = (bf16[128,512]{1,0:T(8,128)(2,1)S(1)}, bf16[128,512]{1,0:T(8,128)(2,1)}, u32[]{:S(2)}) copy-start(bf16[128,512]{1,0:T(8,128)(2,1)} %get-tuple-element.104.m0) | copy-start | bytes 393220
  28.8 9.1 %collective-permute-start.6 = (bf16[512,256]{1,0:T(8,128)(2,1)S(1)}, bf16[512,256]{1,0:T(8,128)(2,1)S(1)}, u32[]{:S(2)}, u32[]{:S(2)}) collective-permute-start(bf16[512,256]{1,0:T(8,128)(2,1)S(1)} %pad_maximum_fusion), channel_id=1, source_target_pairs={{0,2},{2,0},{1,3},{3,1},{4,6},{6,4},{5,7},{7,5},{8,10},{10,8},{9,1... | collective-permute-start | bytes 786440 | tf_op jit(solution)/shard_map/ppermute | solution.py:556
  30.4 6.2 %collective-permute-start.7 = (bf16[128,768]{1,0:T(8,128)(2,1)S(1)}, bf16[128,768]{1,0:T(8,128)(2,1)S(1)}, u32[]{:S(2)}, u32[]{:S(2)}) collective-permute-start(bf16[128,768]{1,0:T(8,128)(2,1)S(1)} %get-tuple-element.108), channel_id=1, source_target_pairs={{0,4},{4,8},{8,12},{12,0},{1,5},{5,9},{9,13},{13,1},{2,6},{6,10},{... | collective-permute-start | bytes 589832 | tf_op jit(solution)/shard_map/ppermute | solution.py:544
  31.0 6.9 %collective-permute-start.8 = (bf16[128,768]{1,0:T(8,128)(2,1)S(1)}, bf16[128,768]{1,0:T(8,128)(2,1)S(1)}, u32[]{:S(2)}, u32[]{:S(2)}) collective-permute-start(bf16[128,768]{1,0:T(8,128)(2,1)S(1)} %get-tuple-element.109), channel_id=1, source_target_pairs={{0,12},{4,0},{8,4},{12,8},{1,13},{5,1},{9,5},{13,9},{2,14},{6,2},{... | collective-permute-start | bytes 589832 | tf_op jit(solution)/shard_map/ppermute | solution.py:544
  32.4 6.6 %collective-permute-start.5 = (bf16[512,256]{1,0:T(8,128)(2,1)S(1)}, bf16[512,256]{1,0:T(8,128)(2,1)S(1)}, u32[]{:S(2)}, u32[]{:S(2)}) collective-permute-start(bf16[512,256]{1,0:T(8,128)(2,1)S(1)} %pad_maximum_fusion), channel_id=1, source_target_pairs={{0,1},{1,0},{2,3},{3,2},{4,5},{5,4},{6,7},{7,6},{8,9},{9,8},{10,11... | collective-permute-start | bytes 786440 | tf_op jit(solution)/shard_map/ppermute | solution.py:556
  34.0 17.5 %copy-start.2 = (bf16[1,128,1536]{2,1,0:T(8,128)(2,1)S(1)}, bf16[1,128,1536]{2,1,0:T(8,128)(2,1)}, u32[]{:S(2)}) copy-start(bf16[1,128,1536]{2,1,0:T(8,128)(2,1)} %param.12) | copy-start | bytes 1179652
  34.0 17.5 %copy-start.6 = (bf16[160,1536]{1,0:T(8,128)(2,1)S(1)}, bf16[160,1536]{1,0:T(8,128)(2,1)}, u32[]{:S(2)}) copy-start(bf16[160,1536]{1,0:T(8,128)(2,1)} %get-tuple-element.132.near) | copy-start | bytes 1474564
  34.0 17.5 %copy-start.9 = (f32[3,1536]{1,0:T(4,128)S(1)}, f32[3,1536]{1,0:T(4,128)}, u32[]{:S(2)}) copy-start(f32[3,1536]{1,0:T(4,128)} %gains.7) | copy-start | bytes 55300
  37.9 1.5 %collective-permute-start.9 = (bf16[512,256]{1,0:T(8,128)(2,1)S(1)}, bf16[512,256]{1,0:T(8,128)(2,1)S(1)}, u32[]{:S(2)}, u32[]{:S(2)}) collective-permute-start(bf16[512,256]{1,0:T(8,128)(2,1)S(1)} %collective-permute-done.6.kv2), channel_id=1, source_target_pairs={{0,1},{1,0},{2,3},{3,2},{4,5},{5,4},{6,7},{7,6},{8,9},{9,8},{10,11... | collective-permute-start | bytes 786440 | tf_op jit(solution)/shard_map/ppermute | solution.py:556
  37.9 8.8 %collective-permute-start.10 = (bf16[128,768]{1,0:T(8,128)(2,1)S(1)}, bf16[128,768]{1,0:T(8,128)(2,1)S(1)}, u32[]{:S(2)}, u32[]{:S(2)}) collective-permute-start(bf16[128,768]{1,0:T(8,128)(2,1)S(1)} %get-tuple-element.118), channel_id=1, source_target_pairs={{0,8},{4,12},{8,0},{12,4},{1,9},{5,13},{9,1},{13,5},{2,10},{6,14},... | collective-permute-start | bytes 589832 | tf_op jit(solution)/shard_map/ppermute | solution.py:544
  46.7 1.9 %collective-permute-start.11 = (bf16[1024,256]{1,0:T(8,128)(2,1)S(1)}, bf16[1024,256]{1,0:T(8,128)(2,1)S(1)}, u32[]{:S(2)}, u32[]{:S(2)}) collective-permute-start(bf16[1024,256]{1,0:T(8,128)(2,1)S(1)} %get-tuple-element.120), channel_id=1, source_target_pairs={{0,1},{1,0},{2,3},{3,2},{4,5},{5,4},{6,7},{7,6},{8,9},{9,8},{10,11... | collective-permute-start | bytes 1572872 | tf_op jit(solution)/shard_map/ppermute | solution.py:556
  48.7 8.4 %collective-permute-start.16 = (bf16[512,256]{1,0:T(8,128)(2,1)S(1)}, bf16[512,256]{1,0:T(8,128)(2,1)S(1)}, u32[]{:S(2)}, u32[]{:S(2)}) collective-permute-start(bf16[512,256]{1,0:T(8,128)(2,1)S(1)} %get-tuple-element.130), channel_id=1, source_target_pairs={{0,2},{2,0},{1,3},{3,1},{4,6},{6,4},{5,7},{7,5},{8,10},{10,8},{9,1... | collective-permute-start | bytes 786440 | tf_op jit(solution)/shard_map/ppermute | solution.py:556
  49.4 10.5 %collective-permute-start.12 = (bf16[512,256]{1,0:T(8,128)(2,1)S(1)}, bf16[512,256]{1,0:T(8,128)(2,1)S(1)}, u32[]{:S(2)}, u32[]{:S(2)}) collective-permute-start(bf16[512,256]{1,0:T(8,128)(2,1)S(1)} %get-tuple-element.168.t0), channel_id=1, source_target_pairs={{0,4},{4,8},{8,12},{12,0},{1,5},{5,9},{9,13},{13,1},{2,6},{6,10},{... | collective-permute-start | bytes 786440 | tf_op jit(solution)/shard_map/ppermute | solution.py:544
  49.8 12.0 %collective-permute-start.14 = (bf16[512,256]{1,0:T(8,128)(2,1)S(1)}, bf16[512,256]{1,0:T(8,128)(2,1)S(1)}, u32[]{:S(2)}, u32[]{:S(2)}) collective-permute-start(bf16[512,256]{1,0:T(8,128)(2,1)S(1)} %get-tuple-element.168.t0), channel_id=1, source_target_pairs={{0,12},{4,0},{8,4},{12,8},{1,13},{5,1},{9,5},{13,9},{2,14},{6,2},{... | collective-permute-start | bytes 786440 | tf_op jit(solution)/shard_map/ppermute | solution.py:544
  57.8 9.0 %collective-permute-start.17 = (bf16[512,256]{1,0:T(8,128)(2,1)S(1)}, bf16[512,256]{1,0:T(8,128)(2,1)S(1)}, u32[]{:S(2)}, u32[]{:S(2)}) collective-permute-start(bf16[512,256]{1,0:T(8,128)(2,1)S(1)} %second_sum.1.d0), channel_id=1, source_target_pairs={{0,4},{4,8},{8,12},{12,0},{1,5},{5,9},{9,13},{13,1},{2,6},{6,10},{... | collective-permute-start | bytes 786440 | tf_op jit(solution)/shard_map/ppermute | solution.py:544
  58.4 10.4 %collective-permute-start.19 = (bf16[512,256]{1,0:T(8,128)(2,1)S(1)}, bf16[512,256]{1,0:T(8,128)(2,1)S(1)}, u32[]{:S(2)}, u32[]{:S(2)}) collective-permute-start(bf16[512,256]{1,0:T(8,128)(2,1)S(1)} %second_sum.1.d0), channel_id=1, source_target_pairs={{0,12},{4,0},{8,4},{12,8},{1,13},{5,1},{9,5},{13,9},{2,14},{6,2},{... | collective-permute-start | bytes 786440 | tf_op jit(solution)/shard_map/ppermute | solution.py:544
  59.9 9.7 %collective-permute-start.13 = (bf16[256,256]{1,0:T(8,128)(2,1)S(1)}, bf16[256,256]{1,0:T(8,128)(2,1)S(1)}, u32[]{:S(2)}, u32[]{:S(2)}) collective-permute-start(bf16[256,256]{1,0:T(8,128)(2,1)S(1)} %slice.56), channel_id=1, source_target_pairs={{0,4},{4,8},{8,12},{12,0},{1,5},{5,9},{9,13},{13,1},{2,6},{6,10},{... | collective-permute-start | bytes 393224 | tf_op jit(solution)/shard_map/ppermute | solution.py:544
  61.8 8.1 %collective-permute-start.15 = (bf16[256,256]{1,0:T(8,128)(2,1)S(1)}, bf16[256,256]{1,0:T(8,128)(2,1)S(1)}, u32[]{:S(2)}, u32[]{:S(2)}) collective-permute-start(bf16[256,256]{1,0:T(8,128)(2,1)S(1)} %slice.57), channel_id=1, source_target_pairs={{0,12},{4,0},{8,4},{12,8},{1,13},{5,1},{9,5},{13,9},{2,14},{6,2},{... | collective-permute-start | bytes 393224 | tf_op jit(solution)/shard_map/ppermute | solution.py:544
  66.8 5.3 %collective-permute-start.18 = (bf16[256,256]{1,0:T(8,128)(2,1)S(1)}, bf16[256,256]{1,0:T(8,128)(2,1)S(1)}, u32[]{:S(2)}, u32[]{:S(2)}) collective-permute-start(bf16[256,256]{1,0:T(8,128)(2,1)S(1)} %slice.58), channel_id=1, source_target_pairs={{0,4},{4,8},{8,12},{12,0},{1,5},{5,9},{9,13},{13,1},{2,6},{6,10},{... | collective-permute-start | bytes 393224 | tf_op jit(solution)/shard_map/ppermute | solution.py:544
  68.9 6.3 %collective-permute-start.20 = (bf16[256,256]{1,0:T(8,128)(2,1)S(1)}, bf16[256,256]{1,0:T(8,128)(2,1)S(1)}, u32[]{:S(2)}, u32[]{:S(2)}) collective-permute-start(bf16[256,256]{1,0:T(8,128)(2,1)S(1)} %slice.59), channel_id=1, source_target_pairs={{0,12},{4,0},{8,4},{12,8},{1,13},{5,1},{9,5},{13,9},{2,14},{6,2},{... | collective-permute-start | bytes 393224 | tf_op jit(solution)/shard_map/ppermute | solution.py:544
  69.8 6.7 %copy-start.4 = (bf16[1536,256]{1,0:T(8,128)(2,1)S(1)}, bf16[1536,256]{1,0:T(8,128)(2,1)}, u32[]{:S(2)}) copy-start(bf16[1536,256]{1,0:T(8,128)(2,1)} %w_query.1) | copy-start | bytes 2359300
  69.8 6.8 %copy-start.5 = (bf16[1536,256]{1,0:T(8,128)(2,1)S(1)}, bf16[1536,256]{1,0:T(8,128)(2,1)}, u32[]{:S(2)}) copy-start(bf16[1536,256]{1,0:T(8,128)(2,1)} %w_key.1) | copy-start | bytes 2359300
  71.3 5.2 %copy-start.1 = (bf16[1536,768]{1,0:T(8,128)(2,1)S(1)}, bf16[1536,768]{1,0:T(8,128)(2,1)}, u32[]{:S(2)}) copy-start(bf16[1536,768]{1,0:T(8,128)(2,1)} %w_value.1) | copy-start | bytes 7077892
  71.3 5.2 %copy-start.7 = (bf16[128,1536]{1,0:T(8,128)(2,1)S(1)}, bf16[128,1536]{1,0:T(8,128)(2,1)}, u32[]{:S(2)}) copy-start(bf16[128,1536]{1,0:T(8,128)(2,1)} %get-tuple-element.173.z) | copy-start | bytes 1179652
  76.4 2.4 %collective-permute-start.21 = (bf16[4,192,512]{2,1,0:T(8,128)(2,1)S(1)}, bf16[4,192,512]{2,1,0:T(8,128)(2,1)S(1)}, u32[]{:S(2)}, u32[]{:S(2)}) collective-permute-start(bf16[4,192,512]{2,1,0:T(8,128)(2,1)S(1)} %get-tuple-element.152), channel_id=1, source_target_pairs={{0,1},{1,0},{2,3},{3,2},{4,5},{5,4},{6,7},{7,6},{8,9},{9,8},{10,11... | collective-permute-start | bytes 2359304 | tf_op jit(solution)/shard_map/ppermute | solution.py:556
  78.8 19.3 %copy-start.11 = (f32[2,3,1536]{2,0,1:T(2,128)S(1)}, f32[2,3,1536]{2,0,1:T(2,128)}, u32[]{:S(2)}) copy-start(f32[2,3,1536]{2,0,1:T(2,128)} %param.14) | copy-start | bytes 110596
  78.8 19.3 %copy-start.14 = (s32[2]{0:T(128)S(1)}, s32[2]{0:T(128)}, u32[]{:S(2)}) copy-start(s32[2]{0:T(128)} %dil.3) | copy-start | bytes 28
  79.7 13.5 %collective-permute-start.24 = (bf16[4,48,512]{2,1,0:T(8,128)(2,1)S(1)}, bf16[4,48,512]{2,1,0:T(8,128)(2,1)S(1)}, u32[]{:S(2)}, u32[]{:S(2)}) collective-permute-start(bf16[4,48,512]{2,1,0:T(8,128)(2,1)S(1)} %get-tuple-element.154), channel_id=1, source_target_pairs={{0,2},{2,0},{128,130},{130,128},{1,3},{3,1},{129,131},{131,129},{4... | collective-permute-start | bytes 589832 | tf_op jit(solution)/shard_map/ppermute | solution.py:718
  80.1 13.1 %collective-permute-start.25 = (bf16[4,48,512]{2,1,0:T(8,128)(2,1)S(1)}, bf16[4,48,512]{2,1,0:T(8,128)(2,1)S(1)}, u32[]{:S(2)}, u32[]{:S(2)}) collective-permute-start(bf16[4,48,512]{2,1,0:T(8,128)(2,1)S(1)} %get-tuple-element.155), channel_id=1, source_target_pairs={{0,128},{2,130},{128,0},{130,2},{1,129},{3,131},{129,1},{131,3},{4... | collective-permute-start | bytes 589832 | tf_op jit(solution)/shard_map/ppermute | solution.py:718
  83.3 12.1 %collective-permute-start.26 = (bf16[4,48,512]{2,1,0:T(8,128)(2,1)S(1)}, bf16[4,48,512]{2,1,0:T(8,128)(2,1)S(1)}, u32[]{:S(2)}, u32[]{:S(2)}) collective-permute-start(bf16[4,48,512]{2,1,0:T(8,128)(2,1)S(1)} %get-tuple-element.156), channel_id=1, source_target_pairs={{0,130},{2,128},{128,2},{130,0},{1,131},{3,129},{129,3},{131,1},{4... | collective-permute-start | bytes 589832 | tf_op jit(solution)/shard_map/ppermute | solution.py:718
  84.5 7.8 %collective-permute-start.22 = (bf16[32,1536]{1,0:T(8,128)(2,1)S(1)}, bf16[32,1536]{1,0:T(8,128)(2,1)S(1)}, u32[]{:S(2)}, u32[]{:S(2)}) collective-permute-start(bf16[32,1536]{1,0:T(8,128)(2,1)S(1)} %get-tuple-element.184), channel_id=1, source_target_pairs={{0,1},{1,2},{2,3},{3,4},{4,5},{5,6},{6,7},{7,8},{8,9},{9,10},{10,1... | collective-permute-start | bytes 294920 | tf_op jit(solution)/shard_map/ppermute | solution.py:561
  86.4 6.7 %collective-permute-start.23 = (bf16[32,1536]{1,0:T(8,128)(2,1)S(1)}, bf16[32,1536]{1,0:T(8,128)(2,1)S(1)}, u32[]{:S(2)}, u32[]{:S(2)}) collective-permute-start(bf16[32,1536]{1,0:T(8,128)(2,1)S(1)} %get-tuple-element.183), channel_id=1, source_target_pairs={{1,0},{2,1},{3,2},{4,3},{5,4},{6,5},{7,6},{8,7},{9,8},{10,9},{11,1... | collective-permute-start | bytes 294920 | tf_op jit(solution)/shard_map/ppermute | solution.py:562
  96.1 16.7 %copy-start = (bf16[768,1536]{1,0:T(8,128)(2,1)S(1)}, bf16[768,1536]{1,0:T(8,128)(2,1)}, u32[]{:S(2)}) copy-start(bf16[768,1536]{1,0:T(8,128)(2,1)} %w_out.1) | copy-start | bytes 7077892
  96.1 4.9 %collective-permute-start.27 = (bf16[4,24,512]{2,1,0:T(8,128)(2,1)S(1)}, bf16[4,24,512]{2,1,0:T(8,128)(2,1)S(1)}, u32[]{:S(2)}, u32[]{:S(2)}) collective-permute-start(bf16[4,24,512]{2,1,0:T(8,128)(2,1)S(1)} %get-tuple-element.165), channel_id=1, source_target_pairs={{0,16},{16,0},{32,48},{48,32},{64,80},{80,64},{96,112},{112,96},{1... | collective-permute-start | bytes 294920 | tf_op jit(solution)/shard_map/ppermute | solution.py:724
  101.6 13.1 %collective-permute-start.28 = (f32[4,6,512]{2,1,0:T(8,128)S(1)}, f32[4,6,512]{2,1,0:T(8,128)S(1)}, u32[]{:S(2)}, u32[]{:S(2)}) collective-permute-start(f32[4,6,512]{2,1,0:T(8,128)S(1)} %get-tuple-element.174), channel_id=1, source_target_pairs={{0,64},{16,80},{32,96},{48,112},{64,0},{80,16},{96,32},{112,48},{1... | collective-permute-start | bytes 147464 | tf_op jit(solution)/shard_map/ppermute | solution.py:544
  108.7 6.5 %collective-permute-start.29 = (f32[4,6,512]{2,1,0:T(8,128)S(1)}, f32[4,6,512]{2,1,0:T(8,128)S(1)}, u32[]{:S(2)}, u32[]{:S(2)}) collective-permute-start(f32[4,6,512]{2,1,0:T(8,128)S(1)} %get-tuple-element.175), channel_id=1, source_target_pairs={{0,32},{16,48},{32,64},{48,80},{64,96},{80,112},{96,0},{112,16},{1... | collective-permute-start | bytes 147464 | tf_op jit(solution)/shard_map/ppermute | solution.py:544
  110.2 5.6 %collective-permute-start.30 = (f32[4,6,512]{2,1,0:T(8,128)S(1)}, f32[4,6,512]{2,1,0:T(8,128)S(1)}, u32[]{:S(2)}, u32[]{:S(2)}) collective-permute-start(f32[4,6,512]{2,1,0:T(8,128)S(1)} %get-tuple-element.176), channel_id=1, source_target_pairs={{0,96},{16,112},{32,0},{48,16},{64,32},{80,48},{96,64},{112,80},{1... | collective-permute-start | bytes 147464 | tf_op jit(solution)/shard_map/ppermute | solution.py:544

commit v4 on v3

--- a/solution.py
+++ b/solution.py
@@ -612,7 +612,8 @@
         us=5.0,
         limit=LARGE,
     )
-    ms = [ms[0]] + [shift(ms[k], "y", ny, k) for k in (1, 2, 3)]
+    sent = {k: shift(ms[k], "y", ny, k) for k in (2, 1, 3)}
+    ms = [ms[0], sent[1], sent[2], sent[3]]
     unit = order.shape[1]
     fs = call(
         shuffle,
@@ -705,7 +706,7 @@
     )
     left, right = halo(grad, nseq)
 
-    pairs = [(a, b) for b in range(nxh) for a in range(2)]
+    pairs = [(a, b) for a in range(2) for b in range(nxh)]
 
     def ring_part(where, i):
         a, b = pairs[i]

time: 117 us -> 117 us (level); the launches traced: 117 us -> 116 us
    ppermute x3, waiting for transfers between devices: 2.29 us -> 0.01 us  [local(): got.append(lax.ppermute(send, ('xh', 'xl'), way))]
  transfers between devices with their start and end apart: 31 -> 31, of which waited for: 20 -> 18; matrix products, arithmetic and copies ran while one was open for 0% -> 0% of each run, Pallas kernels for 20% -> 21%
where the time goes in v4:
time: 117 us; the launch traced here: 116 us
  starting transfers between devices  47.4 us (41%)
  Pallas kernels  34.1 us (29%)
  waiting for transfers between devices  29.4 us (25%)
  local copies, waits for them, and re-layouts  3.66 us (3%)
    pallas_call x18, Pallas kernels, call(): pl.pallas_call(body, out_shape=tuple((jax.ShapeDtypeStruct(s, d) for s, d...  34.1 us
    ppermute x17, starting transfers between devices, shift(): lax.ppermute(array, axis, [(i, (i + step) % count) for i in range(count)])  26 us
    ppermute x17, waiting for transfers between devices, shift(): lax.ppermute(array, axis, [(i, (i + step) % count) for i in range(count)])  19.7 us
    ppermute x2, starting transfers between devices, halo(): lax.ppermute(rows[:width], SEQ, [(i + 1, i) for i in range(nseq - 1)])  9.08 us
    ppermute x6, waiting for transfers between devices, flip(): return lax.ppermute(array, axis, [(0, 1), (1, 0)])  6.11 us
    ppermute x3, starting transfers between devices, local(): got.append(lax.ppermute(send, ('xh', 'xl'), way))  4.18 us
    ppermute x2, starting transfers between devices, halo(): lax.ppermute(rows[-width:], SEQ, [(i, i + 1) for i in range(nseq - 1)])  3.84 us
    ppermute x6, starting transfers between devices, flip(): return lax.ppermute(array, axis, [(0, 1), (1, 0)])  2.4 us
  transfers between devices with their start and end apart: 31, of which 18 were waited for; matrix products, arithmetic and copies ran while one was open for 0% of the time, Pallas kernels for 21%

profile of v4, /device:TPU:24, one launch (start us, length us, event | category | flops | bytes accessed | tf_op | source)
XLA Modules:
  0.0 115.6 jit_solution(3945153685875707732)
XLA Ops:
  0.6 1.0 slice_bitcast_fusion
  1.6 1.9 %collective-permute-start = (bf16[32,1536]{1,0:T(8,128)(2,1)S(1)}, bf16[32,1536]{1,0:T(8,128)(2,1)S(1)}, u32[]{:S(2)}, u32[]{:S(2)}) collective-permute-start(bf16[32,1536]{1,0:T(8,128)(2,1)S(1)} %get-tuple-element.186), channel_id=1, source_target_pairs={{0,1},{1,2},{2,3},{3,4},{4,5},{5,6},{6,7},{7,8},{8,9},{9,10},{10,1... | collective-permute-start | bytes 294920 | tf_op jit(solution)/shard_map/ppermute | solution.py:561
  3.5 4.5 %collective-permute-start.1 = (bf16[32,1536]{1,0:T(8,128)(2,1)S(1)}, bf16[32,1536]{1,0:T(8,128)(2,1)S(1)}, u32[]{:S(2)}, u32[]{:S(2)}) collective-permute-start(bf16[32,1536]{1,0:T(8,128)(2,1)S(1)} %get-tuple-element.185), channel_id=1, source_target_pairs={{1,0},{2,1},{3,2},{4,3},{5,4},{6,5},{7,6},{8,7},{9,8},{10,9},{11,1... | collective-permute-start | bytes 294920 | tf_op jit(solution)/shard_map/ppermute | solution.py:562
  8.1 4.2 %prelude.1 = (bf16[128,1536]{1,0:T(8,128)(2,1)}, bf16[128,768]{1,0:T(8,128)(2,1)}) custom-call(bf16[128,1536]{1,0:T(8,128)(2,1)} %bitcast.19, f32[3,1536]{1,0:T(4,128)} %gains.7, bf16[128,1536]{1,0:T(8,128)(2,1)} %bitcast.23, bf16[768,1536]{1,0:T(8,128)(2,1)} %w_out.1), custom_call_target="tpu_custom_call" | custom-call | flops 1000 | bytes 10800000 | tf_op jit(solution)/shard_map/prelude/pallas_call | solution.py:43
  12.4 0.6 copy-done.16
  13.0 5.3 %forward.1 = (bf16[128,512]{1,0:T(8,128)(2,1)}, bf16[128,512]{1,0:T(8,128)(2,1)}, bf16[128,512]{1,0:T(8,128)(2,1)}, bf16[128,512]{1,0:T(8,128)(2,1)}, bf16[128,1...) custom-call(s32[2]{0:T(128)} %dil.3, bf16[32,1536]{1,0:T(8,128)(2,1)} %copy-done.16, ...), custom_call_target="tpu_custom_call" | custom-call | flops 1000 | bytes 18000000 | tf_op jit(solution)/shard_map/forward/pallas_call | solution.py:43
  18.5 2.8 %collective-permute-start.3 = (bf16[128,512]{1,0:T(8,128)(2,1)}, bf16[128,512]{1,0:T(8,128)(2,1)S(1)}, u32[]{:S(2)}, u32[]{:S(2)}) collective-permute-start(bf16[128,512]{1,0:T(8,128)(2,1)} %get-tuple-element.97), channel_id=1, source_target_pairs={{0,8},{4,12},{8,0},{12,4},{1,9},{5,13},{9,1},{13,5},{2,10},{6,14},... | collective-permute-start | bytes 393224 | tf_op jit(solution)/shard_map/ppermute | solution.py:544
  21.4 1.0 copy-done.8
  22.4 1.6 %shuffle.1 = (bf16[128,768]{1,0:T(8,128)(2,1)S(1)}, bf16[128,768]{1,0:T(8,128)(2,1)S(1)}, bf16[128,768]{1,0:T(8,128)(2,1)S(1)}, bf16[128,768]{1,0:T(8,128)(2,1)S(1)}) custom-call(s32[10]{0:T(128)S(1)} %stack.35.where, s32[1,768]{1,0:T(1,128)S(1)} %copy-done.13, bf16[128,1536]{1,0:T(8,128)(2,1)S(1)} %copy-done.8, bf16[128,1536]{1,0:T(8,128)(2,1)S(1)} %bitcast.24), custom_call_target="tpu_custom_call" | custom-call | flops 1000 | bytes 5760000 | tf_op jit(solution)/shard_map/shuffle/pallas_call | solution.py:43
  23.9 0.5 collective-permute-done.2.m1
  24.4 2.3 %collective-permute-done.3.m2 = bf16[128,512]{1,0:T(8,128)(2,1)S(1)} collective-permute-done((bf16[128,512]{1,0:T(8,128)(2,1)}, bf16[128,512]{1,0:T(8,128)(2,1)S(1)}, u32[]{:S(2)}, u32[]{:S(2)}) %collective-permute-start.3) | collective-permute-done | bytes 131104 | tf_op jit(solution)/shard_map/ppermute | solution.py:544
  26.7 1.2 %collective-permute-done.4.m3 = bf16[128,512]{1,0:T(8,128)(2,1)S(1)} collective-permute-done((bf16[128,512]{1,0:T(8,128)(2,1)}, bf16[128,512]{1,0:T(8,128)(2,1)S(1)}, u32[]{:S(2)}, u32[]{:S(2)}) %collective-permute-start.4) | collective-permute-done | bytes 131104 | tf_op jit(solution)/shard_map/ppermute | solution.py:544
  27.9 0.8 slice.46
  28.8 1.6 %collective-permute-start.6 = (bf16[512,256]{1,0:T(8,128)(2,1)S(1)}, bf16[512,256]{1,0:T(8,128)(2,1)S(1)}, u32[]{:S(2)}, u32[]{:S(2)}) collective-permute-start(bf16[512,256]{1,0:T(8,128)(2,1)S(1)} %pad_maximum_fusion), channel_id=1, source_target_pairs={{0,2},{2,0},{1,3},{3,1},{4,6},{6,4},{5,7},{7,5},{8,10},{10,8},{9,1... | collective-permute-start | bytes 786440 | tf_op jit(solution)/shard_map/ppermute | solution.py:556
  30.4 0.6 collective-permute-start.7
  31.0 1.5 %collective-permute-start.8 = (bf16[128,768]{1,0:T(8,128)(2,1)S(1)}, bf16[128,768]{1,0:T(8,128)(2,1)S(1)}, u32[]{:S(2)}, u32[]{:S(2)}) collective-permute-start(bf16[128,768]{1,0:T(8,128)(2,1)S(1)} %get-tuple-element.109), channel_id=1, source_target_pairs={{0,12},{4,0},{8,4},{12,8},{1,13},{5,1},{9,5},{13,9},{2,14},{6,2},{... | collective-permute-start | bytes 589832 | tf_op jit(solution)/shard_map/ppermute | solution.py:544
  32.5 1.5 %expand.1.master = f32[128,4096]{1,0:T(8,128)S(1)} custom-call(s32[10]{0:T(128)S(1)} %stack.35.where, f32[4,64]{1,0:T(4,128)S(1)} %bitcast.29, s32[1,4095]{1,0:T(1,128)S(1)} %bitcast.28), custom_call_target="tpu_custom_call" | custom-call | flops 1000 | bytes 5400000 | tf_op jit(solution)/shard_map/expand/pallas_call | solution.py:43
  34.0 2.6 %collective-permute-done.7.f1 = bf16[128,768]{1,0:T(8,128)(2,1)S(1)} collective-permute-done((bf16[128,768]{1,0:T(8,128)(2,1)S(1)}, bf16[128,768]{1,0:T(8,128)(2,1)S(1)}, u32[]{:S(2)}, u32[]{:S(2)}) %collective-permute-start.7) | collective-permute-done | bytes 196640 | tf_op jit(solution)/shard_map/ppermute | solution.py:544
  36.6 1.3 %collective-permute-done.8.f3 = bf16[128,768]{1,0:T(8,128)(2,1)S(1)} collective-permute-done((bf16[128,768]{1,0:T(8,128)(2,1)S(1)}, bf16[128,768]{1,0:T(8,128)(2,1)S(1)}, u32[]{:S(2)}, u32[]{:S(2)}) %collective-permute-start.8) | collective-permute-done | bytes 196640 | tf_op jit(solution)/shard_map/ppermute | solution.py:544
  37.9 1.1 collective-permute-start.10
  39.0 0.4 collective-permute-done.9.kv3
  39.4 5.6 %attend.1 = (bf16[512,256]{1,0:T(8,128)(2,1)S(1)}, f32[512,256]{1,0:T(8,128)S(1)}, f32[512,256]{1,0:T(8,128)S(1)}, bf16[1024,256]{1,0:T(8,128)(2,1)S(1)}) custom-call(s32[10]{0:T(128)S(1)} %stack.35.where, bf16[128,512]{1,0:T(8,128)(2,1)S(1)} %copy-done.10, bf16[128,512]{1,0:T(8,128)(2,1)S(1)} %collective-permute-done.2.m1, ...), custom_call_target="tpu_custom_call" | custom-call | flops 1000 | bytes 25200000 | tf_op jit(solution)/shard_map/attend/pallas_call | solution.py:43
  45.0 1.7 %collective-permute-done.10.f2 = bf16[128,768]{1,0:T(8,128)(2,1)S(1)} collective-permute-done((bf16[128,768]{1,0:T(8,128)(2,1)S(1)}, bf16[128,768]{1,0:T(8,128)(2,1)S(1)}, u32[]{:S(2)}, u32[]{:S(2)}) %collective-permute-start.10) | collective-permute-done | bytes 196640 | tf_op jit(solution)/shard_map/ppermute | solution.py:544
  46.7 1.9 %collective-permute-done.11.got = bf16[1024,256]{1,0:T(8,128)(2,1)S(1)} collective-permute-done((bf16[1024,256]{1,0:T(8,128)(2,1)S(1)}, bf16[1024,256]{1,0:T(8,128)(2,1)S(1)}, u32[]{:S(2)}, u32[]{:S(2)}) %collective-permute-start.11) | collective-permute-done | bytes 524320 | tf_op jit(solution)/shard_map/ppermute | solution.py:556
  48.6 0.1 first_sum.1
  48.7 0.7 collective-permute-start.16
  49.4 0.3 collective-permute-start.12
  49.8 1.7 %collective-permute-start.14 = (bf16[512,256]{1,0:T(8,128)(2,1)S(1)}, bf16[512,256]{1,0:T(8,128)(2,1)S(1)}, u32[]{:S(2)}, u32[]{:S(2)}) collective-permute-start(bf16[512,256]{1,0:T(8,128)(2,1)S(1)} %get-tuple-element.168.t0), channel_id=1, source_target_pairs={{0,12},{4,0},{8,4},{12,8},{1,13},{5,1},{9,5},{13,9},{2,14},{6,2},{... | collective-permute-start | bytes 786440 | tf_op jit(solution)/shard_map/ppermute | solution.py:544
  51.5 1.0 slopes.1
  52.5 0.9 turn.1
  53.4 3.8 %collective-permute-done.16.got = bf16[512,256]{1,0:T(8,128)(2,1)S(1)} collective-permute-done((bf16[512,256]{1,0:T(8,128)(2,1)S(1)}, bf16[512,256]{1,0:T(8,128)(2,1)S(1)}, u32[]{:S(2)}, u32[]{:S(2)}) %collective-permute-start.16) | collective-permute-done | bytes 262176 | tf_op jit(solution)/shard_map/ppermute | solution.py:556
  57.2 0.6 second_sum.1.d0
  57.8 0.6 collective-permute-start.17
  58.4 1.5 %collective-permute-start.19 = (bf16[512,256]{1,0:T(8,128)(2,1)S(1)}, bf16[512,256]{1,0:T(8,128)(2,1)S(1)}, u32[]{:S(2)}, u32[]{:S(2)}) collective-permute-start(bf16[512,256]{1,0:T(8,128)(2,1)S(1)} %second_sum.1.d0), channel_id=1, source_target_pairs={{0,12},{4,0},{8,4},{12,8},{1,13},{5,1},{9,5},{13,9},{2,14},{6,2},{... | collective-permute-start | bytes 786440 | tf_op jit(solution)/shard_map/ppermute | solution.py:544
  59.9 1.9 %collective-permute-start.13 = (bf16[256,256]{1,0:T(8,128)(2,1)S(1)}, bf16[256,256]{1,0:T(8,128)(2,1)S(1)}, u32[]{:S(2)}, u32[]{:S(2)}) collective-permute-start(bf16[256,256]{1,0:T(8,128)(2,1)S(1)} %slice.56), channel_id=1, source_target_pairs={{0,4},{4,8},{8,12},{12,0},{1,5},{5,9},{9,13},{13,1},{2,6},{6,10},{... | collective-permute-start | bytes 393224 | tf_op jit(solution)/shard_map/ppermute | solution.py:544
  61.8 0.3 collective-permute-start.15
  62.1 4.7 %collective-permute-done.17.d1 = bf16[512,256]{1,0:T(8,128)(2,1)S(1)} collective-permute-done((bf16[512,256]{1,0:T(8,128)(2,1)S(1)}, bf16[512,256]{1,0:T(8,128)(2,1)S(1)}, u32[]{:S(2)}, u32[]{:S(2)}) %collective-permute-start.17) | collective-permute-done | bytes 262176 | tf_op jit(solution)/shard_map/ppermute | solution.py:544
  66.8 2.0 %collective-permute-start.18 = (bf16[256,256]{1,0:T(8,128)(2,1)S(1)}, bf16[256,256]{1,0:T(8,128)(2,1)S(1)}, u32[]{:S(2)}, u32[]{:S(2)}) collective-permute-start(bf16[256,256]{1,0:T(8,128)(2,1)S(1)} %slice.58), channel_id=1, source_target_pairs={{0,4},{4,8},{8,12},{12,0},{1,5},{5,9},{9,13},{13,1},{2,6},{6,10},{... | collective-permute-start | bytes 393224 | tf_op jit(solution)/shard_map/ppermute | solution.py:544
  68.9 0.4 collective-permute-start.20
  69.2 0.3 collective-permute-done.13.t2
  69.6 0.2 collective-permute-done.15.t3
  69.8 1.5 %weigh_first.1.before = f32[2,4,192,256]{3,2,1,0:T(8,128)S(1)} custom-call(s32[10]{0:T(128)S(1)} %stack.35.where, bf16[384,512]{1,0:T(8,128)(2,1)S(1)} %get-tuple-element.141.n_turned, bf16[384,512]{1,0:T(8,128)(2,1)S(1)} %get-tuple-element.144.u_turned, bf16[512,256]{1,0:T(8,128)(2,1)S(1)} %get-tuple-element.168.t0, ...), custom_call_target="tpu_custom_call" | custom-call | flops 1000 | bytes 7200000 | tf_op jit(solution)/shard_map/weigh_first/pallas_call | solution.py:43
  71.3 0.7 collective-permute-done.18.d2
  72.1 3.0 %collective-permute-done.20.d3 = bf16[256,256]{1,0:T(8,128)(2,1)S(1)} collective-permute-done((bf16[256,256]{1,0:T(8,128)(2,1)S(1)}, bf16[256,256]{1,0:T(8,128)(2,1)S(1)}, u32[]{:S(2)}, u32[]{:S(2)}) %collective-permute-start.20) | collective-permute-done | bytes 131104 | tf_op jit(solution)/shard_map/ppermute | solution.py:544
  75.1 1.3 %weigh_second.1 = (f32[4,192,512]{2,1,0:T(8,128)S(1)}, bf16[4,192,512]{2,1,0:T(8,128)(2,1)S(1)}) custom-call(s32[10]{0:T(128)S(1)} %stack.35.where, bf16[384,512]{1,0:T(8,128)(2,1)S(1)} %get-tuple-element.141.n_turned, bf16[512,256]{1,0:T(8,128)(2,1)S(1)} %second_sum.1.d0, bf16[512,256]{1,0:T(8,128)(2,1)S(1)} %collective-permute-done.17.d1, ...), custom_call_target="tpu_custom_call" | custom-call | flops 1000 | bytes 5400000 | tf_op jit(solution)/shard_map/weigh_second/pallas_call | solution.py:43
  76.6 2.2 %grad_top.1.grad = bf16[128,1536]{1,0:T(8,128)(2,1)S(1)} custom-call(s32[10]{0:T(128)S(1)} %stack.35.where, bf16[512,256]{1,0:T(8,128)(2,1)S(1)} %get-tuple-element.168.t0, bf16[512,256]{1,0:T(8,128)(2,1)S(1)} %collective-permute-done.12.t1, bf16[256,256]{1,0:T(8,128)(2,1)S(1)} %collective-permute-done.13.t2, ...), custom_call_target="tpu_custom_call" | custom-call | flops 1000 | bytes 10800000 | tf_op jit(solution)/shard_map/grad_top/pallas_call | solution.py:43
  78.8 0.8 fold.2
  79.7 3.2 %collective-permute-start.24 = (bf16[4,48,512]{2,1,0:T(8,128)(2,1)S(1)}, bf16[4,48,512]{2,1,0:T(8,128)(2,1)S(1)}, u32[]{:S(2)}, u32[]{:S(2)}) collective-permute-start(bf16[4,48,512]{2,1,0:T(8,128)(2,1)S(1)} %get-tuple-element.154), channel_id=1, source_target_pairs={{0,128},{2,130},{128,0},{130,2},{1,129},{3,131},{129,1},{131,3},{4... | collective-permute-start | bytes 589832 | tf_op jit(solution)/shard_map/ppermute | solution.py:719
  82.8 1.0 collective-permute-start.26
  83.9 1.9 %collective-permute-start.22 = (bf16[32,1536]{1,0:T(8,128)(2,1)S(1)}, bf16[32,1536]{1,0:T(8,128)(2,1)S(1)}, u32[]{:S(2)}, u32[]{:S(2)}) collective-permute-start(bf16[32,1536]{1,0:T(8,128)(2,1)S(1)} %get-tuple-element.184), channel_id=1, source_target_pairs={{0,1},{1,2},{2,3},{3,4},{4,5},{5,6},{6,7},{7,8},{8,9},{9,10},{10,1... | collective-permute-start | bytes 294920 | tf_op jit(solution)/shard_map/ppermute | solution.py:561
  85.8 4.5 %collective-permute-start.23 = (bf16[32,1536]{1,0:T(8,128)(2,1)S(1)}, bf16[32,1536]{1,0:T(8,128)(2,1)S(1)}, u32[]{:S(2)}, u32[]{:S(2)}) collective-permute-start(bf16[32,1536]{1,0:T(8,128)(2,1)S(1)} %get-tuple-element.183), channel_id=1, source_target_pairs={{1,0},{2,1},{3,2},{4,3},{5,4},{6,5},{7,6},{8,7},{9,8},{10,9},{11,1... | collective-permute-start | bytes 294920 | tf_op jit(solution)/shard_map/ppermute | solution.py:562
  90.3 2.3 %collective-permute-done.22.left = bf16[32,1536]{1,0:T(8,128)(2,1)S(1)} collective-permute-done((bf16[32,1536]{1,0:T(8,128)(2,1)S(1)}, bf16[32,1536]{1,0:T(8,128)(2,1)S(1)}, u32[]{:S(2)}, u32[]{:S(2)}) %collective-permute-start.22) | collective-permute-done | bytes 98336 | tf_op jit(solution)/shard_map/ppermute | solution.py:561
  92.6 1.4 %collective-permute-done.23.right = bf16[32,1536]{1,0:T(8,128)(2,1)S(1)} collective-permute-done((bf16[32,1536]{1,0:T(8,128)(2,1)S(1)}, bf16[32,1536]{1,0:T(8,128)(2,1)S(1)}, u32[]{:S(2)}, u32[]{:S(2)}) %collective-permute-start.23) | collective-permute-done | bytes 98336 | tf_op jit(solution)/shard_map/ppermute | solution.py:562
  94.0 0.7 fold.3
  94.7 2.0 %collective-permute-start.27 = (bf16[4,24,512]{2,1,0:T(8,128)(2,1)S(1)}, bf16[4,24,512]{2,1,0:T(8,128)(2,1)S(1)}, u32[]{:S(2)}, u32[]{:S(2)}) collective-permute-start(bf16[4,24,512]{2,1,0:T(8,128)(2,1)S(1)} %get-tuple-element.165), channel_id=1, source_target_pairs={{0,16},{16,0},{32,48},{48,32},{64,80},{80,64},{96,112},{112,96},{1... | collective-permute-start | bytes 294920 | tf_op jit(solution)/shard_map/ppermute | solution.py:725
  96.7 2.9 %backward.1 = bf16[128,1536]{1,0:T(8,128)(2,1)} custom-call(s32[10]{0:T(128)S(1)} %stack.35.where, s32[2]{0:T(128)S(1)} %copy-done.14, bf16[32,1536]{1,0:T(8,128)(2,1)S(1)} %collective-permute-done.22.left, bf16[32,1536]{1,0:T(8,128)(2,1)S(1)} %collective-permute-done.23.right, bf16[128,1536]{1,0:T(8,128)(2,1)S(1)} %grad_top.1.grad, ...), custom_call_target="tpu_custom_call" | custom-call | flops 1000 | bytes 16559999 | tf_op jit(solution)/shard_map/backward/pallas_call | solution.py:43
  99.6 0.6 last_fold.1
  100.2 7.1 %collective-permute-start.28 = (f32[4,6,512]{2,1,0:T(8,128)S(1)}, f32[4,6,512]{2,1,0:T(8,128)S(1)}, u32[]{:S(2)}, u32[]{:S(2)}) collective-permute-start(f32[4,6,512]{2,1,0:T(8,128)S(1)} %get-tuple-element.174), channel_id=1, source_target_pairs={{0,64},{16,80},{32,96},{48,112},{64,0},{80,16},{96,32},{112,48},{1... | collective-permute-start | bytes 147464 | tf_op jit(solution)/shard_map/ppermute | solution.py:544
  107.3 1.5 %collective-permute-start.29 = (f32[4,6,512]{2,1,0:T(8,128)S(1)}, f32[4,6,512]{2,1,0:T(8,128)S(1)}, u32[]{:S(2)}, u32[]{:S(2)}) collective-permute-start(f32[4,6,512]{2,1,0:T(8,128)S(1)} %get-tuple-element.175), channel_id=1, source_target_pairs={{0,32},{16,48},{32,64},{48,80},{64,96},{80,112},{96,0},{112,16},{1... | collective-permute-start | bytes 147464 | tf_op jit(solution)/shard_map/ppermute | solution.py:544
  108.8 2.6 %collective-permute-start.30 = (f32[4,6,512]{2,1,0:T(8,128)S(1)}, f32[4,6,512]{2,1,0:T(8,128)S(1)}, u32[]{:S(2)}, u32[]{:S(2)}) collective-permute-start(f32[4,6,512]{2,1,0:T(8,128)S(1)} %get-tuple-element.176), channel_id=1, source_target_pairs={{0,96},{16,112},{32,0},{48,16},{64,32},{80,48},{96,64},{112,80},{1... | collective-permute-start | bytes 147464 | tf_op jit(solution)/shard_map/ppermute | solution.py:544
  111.4 1.8 %project.1 = bf16[128,1536]{1,0:T(8,128)(2,1)} custom-call(s32[10]{0:T(128)S(1)} %stack.35.where, bf16[512,256]{1,0:T(8,128)(2,1)S(1)} %get-tuple-element.168.t0, bf16[512,256]{1,0:T(8,128)(2,1)S(1)} %collective-permute-done.12.t1, bf16[256,256]{1,0:T(8,128)(2,1)S(1)} %collective-permute-done.13.t2, bf16[256,256]{1,0:T(8,128)(2,1)S(1)} %collective-permute-done.15.t3, ...), custom_call_target="tpu_custom_call" | custom-call | flops 1000 | bytes 36000 | tf_op jit(solution)/shard_map/project/pallas_call | solution.py:43
  113.3 0.7 collective-permute-done.29.refs_2_
  113.9 0.4 collective-permute-done.30.refs_3_
  114.3 1.3 %arrange.1 = f32[6,2048]{1,0:T(8,128)} custom-call(s32[10]{0:T(128)S(1)} %stack.35.where, f32[4,6,512]{2,1,0:T(8,128)S(1)} %get-tuple-element.179.refs_0_, f32[4,6,512]{2,1,0:T(8,128)S(1)} %collective-permute-done.28.refs_1_, f32[4,6,512]{2,1,0:T(8,128)S(1)} %collective-permute-done.29.refs_2_, f32[4,6,512]{2,1,0:T(8,128)S(1)} %collective-permute-done.30.refs_3_), custom_call_target="tpu_custom_call" | custom-call | flops 1000 | bytes 3600000 | tf_op jit(solution)/shard_map/arrange/pallas_call | solution.py:43
  (64 shorter events, 0.5 us)
Async XLA Ops:
  1.6 10.7 %collective-permute-start = (bf16[32,1536]{1,0:T(8,128)(2,1)S(1)}, bf16[32,1536]{1,0:T(8,128)(2,1)S(1)}, u32[]{:S(2)}, u32[]{:S(2)}) collective-permute-start(bf16[32,1536]{1,0:T(8,128)(2,1)S(1)} %get-tuple-element.186), channel_id=1, source_target_pairs={{0,1},{1,2},{2,3},{3,4},{4,5},{5,6},{6,7},{7,8},{8,9},{9,10},{10,1... | collective-permute-start | bytes 294920 | tf_op jit(solution)/shard_map/ppermute | solution.py:561
  3.5 8.8 %collective-permute-start.1 = (bf16[32,1536]{1,0:T(8,128)(2,1)S(1)}, bf16[32,1536]{1,0:T(8,128)(2,1)S(1)}, u32[]{:S(2)}, u32[]{:S(2)}) collective-permute-start(bf16[32,1536]{1,0:T(8,128)(2,1)S(1)} %get-tuple-element.185), channel_id=1, source_target_pairs={{1,0},{2,1},{3,2},{4,3},{5,4},{6,5},{7,6},{8,7},{9,8},{10,9},{11,1... | collective-permute-start | bytes 294920 | tf_op jit(solution)/shard_map/ppermute | solution.py:562
  12.3 0.6 copy-start.16
  12.3 0.6 copy-start.17
  13.0 8.3 %copy-start.3 = (bf16[1,128,1536]{2,1,0:T(8,128)(2,1)S(1)}, bf16[1,128,1536]{2,1,0:T(8,128)(2,1)}, u32[]{:S(2)}) copy-start(bf16[1,128,1536]{2,1,0:T(8,128)(2,1)} %param.22) | copy-start | bytes 1179652
  13.0 8.3 %copy-start.13 = (s32[1,768]{1,0:T(1,128)S(1)}, s32[1,768]{1,0:T(1,128)}, u32[]{:S(2)}) copy-start(s32[1,768]{1,0:T(1,128)} %constant.50.clone.order) | copy-start | bytes 9220
  13.0 19.4 %copy-start.12 = (s32[4095]{0:T(1024)S(1)}, s32[4095]{0:T(1024)}, u32[]{:S(2)}) copy-start(s32[4095]{0:T(1024)} %param.17) | copy-start | bytes 49144
  13.0 19.4 %copy-start.15 = (f32[64,4]{0,1:T(4,128)S(1)}, f32[64,4]{0,1:T(4,128)}, u32[]{:S(2)}) copy-start(f32[64,4]{0,1:T(4,128)} %param.16) | copy-start | bytes 3076
  18.4 6.1 %collective-permute-start.2 = (bf16[128,512]{1,0:T(8,128)(2,1)}, bf16[128,512]{1,0:T(8,128)(2,1)S(1)}, u32[]{:S(2)}, u32[]{:S(2)}) collective-permute-start(bf16[128,512]{1,0:T(8,128)(2,1)} %get-tuple-element.96), channel_id=1, source_target_pairs={{0,4},{4,8},{8,12},{12,0},{1,5},{5,9},{9,13},{13,1},{2,6},{6,10},{... | collective-permute-start | bytes 393224 | tf_op jit(solution)/shard_map/ppermute | solution.py:544
  18.5 8.3 %collective-permute-start.3 = (bf16[128,512]{1,0:T(8,128)(2,1)}, bf16[128,512]{1,0:T(8,128)(2,1)S(1)}, u32[]{:S(2)}, u32[]{:S(2)}) collective-permute-start(bf16[128,512]{1,0:T(8,128)(2,1)} %get-tuple-element.97), channel_id=1, source_target_pairs={{0,8},{4,12},{8,0},{12,4},{1,9},{5,13},{9,1},{13,5},{2,10},{6,14},... | collective-permute-start | bytes 393224 | tf_op jit(solution)/shard_map/ppermute | solution.py:544
  21.3 6.6 %collective-permute-start.4 = (bf16[128,512]{1,0:T(8,128)(2,1)}, bf16[128,512]{1,0:T(8,128)(2,1)S(1)}, u32[]{:S(2)}, u32[]{:S(2)}) collective-permute-start(bf16[128,512]{1,0:T(8,128)(2,1)} %get-tuple-element.98), channel_id=1, source_target_pairs={{0,12},{4,0},{8,4},{12,8},{1,13},{5,1},{9,5},{13,9},{2,14},{6,2},{... | collective-permute-start | bytes 393224 | tf_op jit(solution)/shard_map/ppermute | solution.py:544
  21.4 1.0 copy-start.8
  22.4 17.1 %copy-start.10 = (bf16[128,512]{1,0:T(8,128)(2,1)S(1)}, bf16[128,512]{1,0:T(8,128)(2,1)}, u32[]{:S(2)}) copy-start(bf16[128,512]{1,0:T(8,128)(2,1)} %get-tuple-element.104.m0) | copy-start | bytes 393220
  28.8 9.1 %collective-permute-start.6 = (bf16[512,256]{1,0:T(8,128)(2,1)S(1)}, bf16[512,256]{1,0:T(8,128)(2,1)S(1)}, u32[]{:S(2)}, u32[]{:S(2)}) collective-permute-start(bf16[512,256]{1,0:T(8,128)(2,1)S(1)} %pad_maximum_fusion), channel_id=1, source_target_pairs={{0,2},{2,0},{1,3},{3,1},{4,6},{6,4},{5,7},{7,5},{8,10},{10,8},{9,1... | collective-permute-start | bytes 786440 | tf_op jit(solution)/shard_map/ppermute | solution.py:556
  30.4 6.2 %collective-permute-start.7 = (bf16[128,768]{1,0:T(8,128)(2,1)S(1)}, bf16[128,768]{1,0:T(8,128)(2,1)S(1)}, u32[]{:S(2)}, u32[]{:S(2)}) collective-permute-start(bf16[128,768]{1,0:T(8,128)(2,1)S(1)} %get-tuple-element.108), channel_id=1, source_target_pairs={{0,4},{4,8},{8,12},{12,0},{1,5},{5,9},{9,13},{13,1},{2,6},{6,10},{... | collective-permute-start | bytes 589832 | tf_op jit(solution)/shard_map/ppermute | solution.py:544
  31.0 6.9 %collective-permute-start.8 = (bf16[128,768]{1,0:T(8,128)(2,1)S(1)}, bf16[128,768]{1,0:T(8,128)(2,1)S(1)}, u32[]{:S(2)}, u32[]{:S(2)}) collective-permute-start(bf16[128,768]{1,0:T(8,128)(2,1)S(1)} %get-tuple-element.109), channel_id=1, source_target_pairs={{0,12},{4,0},{8,4},{12,8},{1,13},{5,1},{9,5},{13,9},{2,14},{6,2},{... | collective-permute-start | bytes 589832 | tf_op jit(solution)/shard_map/ppermute | solution.py:544
  32.4 6.6 %collective-permute-start.5 = (bf16[512,256]{1,0:T(8,128)(2,1)S(1)}, bf16[512,256]{1,0:T(8,128)(2,1)S(1)}, u32[]{:S(2)}, u32[]{:S(2)}) collective-permute-start(bf16[512,256]{1,0:T(8,128)(2,1)S(1)} %pad_maximum_fusion), channel_id=1, source_target_pairs={{0,1},{1,0},{2,3},{3,2},{4,5},{5,4},{6,7},{7,6},{8,9},{9,8},{10,11... | collective-permute-start | bytes 786440 | tf_op jit(solution)/shard_map/ppermute | solution.py:556
  34.0 17.5 %copy-start.2 = (bf16[1,128,1536]{2,1,0:T(8,128)(2,1)S(1)}, bf16[1,128,1536]{2,1,0:T(8,128)(2,1)}, u32[]{:S(2)}) copy-start(bf16[1,128,1536]{2,1,0:T(8,128)(2,1)} %param.12) | copy-start | bytes 1179652
  34.0 17.5 %copy-start.6 = (bf16[160,1536]{1,0:T(8,128)(2,1)S(1)}, bf16[160,1536]{1,0:T(8,128)(2,1)}, u32[]{:S(2)}) copy-start(bf16[160,1536]{1,0:T(8,128)(2,1)} %get-tuple-element.132.near) | copy-start | bytes 1474564
  34.0 17.5 %copy-start.9 = (f32[3,1536]{1,0:T(4,128)S(1)}, f32[3,1536]{1,0:T(4,128)}, u32[]{:S(2)}) copy-start(f32[3,1536]{1,0:T(4,128)} %gains.7) | copy-start | bytes 55300
  37.9 1.5 %collective-permute-start.9 = (bf16[512,256]{1,0:T(8,128)(2,1)S(1)}, bf16[512,256]{1,0:T(8,128)(2,1)S(1)}, u32[]{:S(2)}, u32[]{:S(2)}) collective-permute-start(bf16[512,256]{1,0:T(8,128)(2,1)S(1)} %collective-permute-done.6.kv2), channel_id=1, source_target_pairs={{0,1},{1,0},{2,3},{3,2},{4,5},{5,4},{6,7},{7,6},{8,9},{9,8},{10,11... | collective-permute-start | bytes 786440 | tf_op jit(solution)/shard_map/ppermute | solution.py:556
  37.9 8.8 %collective-permute-start.10 = (bf16[128,768]{1,0:T(8,128)(2,1)S(1)}, bf16[128,768]{1,0:T(8,128)(2,1)S(1)}, u32[]{:S(2)}, u32[]{:S(2)}) collective-permute-start(bf16[128,768]{1,0:T(8,128)(2,1)S(1)} %get-tuple-element.118), channel_id=1, source_target_pairs={{0,8},{4,12},{8,0},{12,4},{1,9},{5,13},{9,1},{13,5},{2,10},{6,14},... | collective-permute-start | bytes 589832 | tf_op jit(solution)/shard_map/ppermute | solution.py:544
  46.7 1.9 %collective-permute-start.11 = (bf16[1024,256]{1,0:T(8,128)(2,1)S(1)}, bf16[1024,256]{1,0:T(8,128)(2,1)S(1)}, u32[]{:S(2)}, u32[]{:S(2)}) collective-permute-start(bf16[1024,256]{1,0:T(8,128)(2,1)S(1)} %get-tuple-element.120), channel_id=1, source_target_pairs={{0,1},{1,0},{2,3},{3,2},{4,5},{5,4},{6,7},{7,6},{8,9},{9,8},{10,11... | collective-permute-start | bytes 1572872 | tf_op jit(solution)/shard_map/ppermute | solution.py:556
  48.7 8.4 %collective-permute-start.16 = (bf16[512,256]{1,0:T(8,128)(2,1)S(1)}, bf16[512,256]{1,0:T(8,128)(2,1)S(1)}, u32[]{:S(2)}, u32[]{:S(2)}) collective-permute-start(bf16[512,256]{1,0:T(8,128)(2,1)S(1)} %get-tuple-element.130), channel_id=1, source_target_pairs={{0,2},{2,0},{1,3},{3,1},{4,6},{6,4},{5,7},{7,5},{8,10},{10,8},{9,1... | collective-permute-start | bytes 786440 | tf_op jit(solution)/shard_map/ppermute | solution.py:556
  49.4 10.5 %collective-permute-start.12 = (bf16[512,256]{1,0:T(8,128)(2,1)S(1)}, bf16[512,256]{1,0:T(8,128)(2,1)S(1)}, u32[]{:S(2)}, u32[]{:S(2)}) collective-permute-start(bf16[512,256]{1,0:T(8,128)(2,1)S(1)} %get-tuple-element.168.t0), channel_id=1, source_target_pairs={{0,4},{4,8},{8,12},{12,0},{1,5},{5,9},{9,13},{13,1},{2,6},{6,10},{... | collective-permute-start | bytes 786440 | tf_op jit(solution)/shard_map/ppermute | solution.py:544
  49.8 12.0 %collective-permute-start.14 = (bf16[512,256]{1,0:T(8,128)(2,1)S(1)}, bf16[512,256]{1,0:T(8,128)(2,1)S(1)}, u32[]{:S(2)}, u32[]{:S(2)}) collective-permute-start(bf16[512,256]{1,0:T(8,128)(2,1)S(1)} %get-tuple-element.168.t0), channel_id=1, source_target_pairs={{0,12},{4,0},{8,4},{12,8},{1,13},{5,1},{9,5},{13,9},{2,14},{6,2},{... | collective-permute-start | bytes 786440 | tf_op jit(solution)/shard_map/ppermute | solution.py:544
  57.8 9.0 %collective-permute-start.17 = (bf16[512,256]{1,0:T(8,128)(2,1)S(1)}, bf16[512,256]{1,0:T(8,128)(2,1)S(1)}, u32[]{:S(2)}, u32[]{:S(2)}) collective-permute-start(bf16[512,256]{1,0:T(8,128)(2,1)S(1)} %second_sum.1.d0), channel_id=1, source_target_pairs={{0,4},{4,8},{8,12},{12,0},{1,5},{5,9},{9,13},{13,1},{2,6},{6,10},{... | collective-permute-start | bytes 786440 | tf_op jit(solution)/shard_map/ppermute | solution.py:544
  58.4 10.4 %collective-permute-start.19 = (bf16[512,256]{1,0:T(8,128)(2,1)S(1)}, bf16[512,256]{1,0:T(8,128)(2,1)S(1)}, u32[]{:S(2)}, u32[]{:S(2)}) collective-permute-start(bf16[512,256]{1,0:T(8,128)(2,1)S(1)} %second_sum.1.d0), channel_id=1, source_target_pairs={{0,12},{4,0},{8,4},{12,8},{1,13},{5,1},{9,5},{13,9},{2,14},{6,2},{... | collective-permute-start | bytes 786440 | tf_op jit(solution)/shard_map/ppermute | solution.py:544
  59.9 9.7 %collective-permute-start.13 = (bf16[256,256]{1,0:T(8,128)(2,1)S(1)}, bf16[256,256]{1,0:T(8,128)(2,1)S(1)}, u32[]{:S(2)}, u32[]{:S(2)}) collective-permute-start(bf16[256,256]{1,0:T(8,128)(2,1)S(1)} %slice.56), channel_id=1, source_target_pairs={{0,4},{4,8},{8,12},{12,0},{1,5},{5,9},{9,13},{13,1},{2,6},{6,10},{... | collective-permute-start | bytes 393224 | tf_op jit(solution)/shard_map/ppermute | solution.py:544
  61.8 8.1 %collective-permute-start.15 = (bf16[256,256]{1,0:T(8,128)(2,1)S(1)}, bf16[256,256]{1,0:T(8,128)(2,1)S(1)}, u32[]{:S(2)}, u32[]{:S(2)}) collective-permute-start(bf16[256,256]{1,0:T(8,128)(2,1)S(1)} %slice.57), channel_id=1, source_target_pairs={{0,12},{4,0},{8,4},{12,8},{1,13},{5,1},{9,5},{13,9},{2,14},{6,2},{... | collective-permute-start | bytes 393224 | tf_op jit(solution)/shard_map/ppermute | solution.py:544
  66.8 5.3 %collective-permute-start.18 = (bf16[256,256]{1,0:T(8,128)(2,1)S(1)}, bf16[256,256]{1,0:T(8,128)(2,1)S(1)}, u32[]{:S(2)}, u32[]{:S(2)}) collective-permute-start(bf16[256,256]{1,0:T(8,128)(2,1)S(1)} %slice.58), channel_id=1, source_target_pairs={{0,4},{4,8},{8,12},{12,0},{1,5},{5,9},{9,13},{13,1},{2,6},{6,10},{... | collective-permute-start | bytes 393224 | tf_op jit(solution)/shard_map/ppermute | solution.py:544
  68.9 6.3 %collective-permute-start.20 = (bf16[256,256]{1,0:T(8,128)(2,1)S(1)}, bf16[256,256]{1,0:T(8,128)(2,1)S(1)}, u32[]{:S(2)}, u32[]{:S(2)}) collective-permute-start(bf16[256,256]{1,0:T(8,128)(2,1)S(1)} %slice.59), channel_id=1, source_target_pairs={{0,12},{4,0},{8,4},{12,8},{1,13},{5,1},{9,5},{13,9},{2,14},{6,2},{... | collective-permute-start | bytes 393224 | tf_op jit(solution)/shard_map/ppermute | solution.py:544
  69.8 6.7 %copy-start.4 = (bf16[1536,256]{1,0:T(8,128)(2,1)S(1)}, bf16[1536,256]{1,0:T(8,128)(2,1)}, u32[]{:S(2)}) copy-start(bf16[1536,256]{1,0:T(8,128)(2,1)} %w_query.1) | copy-start | bytes 2359300
  69.8 6.8 %copy-start.5 = (bf16[1536,256]{1,0:T(8,128)(2,1)S(1)}, bf16[1536,256]{1,0:T(8,128)(2,1)}, u32[]{:S(2)}) copy-start(bf16[1536,256]{1,0:T(8,128)(2,1)} %w_key.1) | copy-start | bytes 2359300
  71.3 5.2 %copy-start.1 = (bf16[1536,768]{1,0:T(8,128)(2,1)S(1)}, bf16[1536,768]{1,0:T(8,128)(2,1)}, u32[]{:S(2)}) copy-start(bf16[1536,768]{1,0:T(8,128)(2,1)} %w_value.1) | copy-start | bytes 7077892
  71.3 5.2 %copy-start.7 = (bf16[128,1536]{1,0:T(8,128)(2,1)S(1)}, bf16[128,1536]{1,0:T(8,128)(2,1)}, u32[]{:S(2)}) copy-start(bf16[128,1536]{1,0:T(8,128)(2,1)} %get-tuple-element.173.z) | copy-start | bytes 1179652
  76.4 2.4 %collective-permute-start.21 = (bf16[4,192,512]{2,1,0:T(8,128)(2,1)S(1)}, bf16[4,192,512]{2,1,0:T(8,128)(2,1)S(1)}, u32[]{:S(2)}, u32[]{:S(2)}) collective-permute-start(bf16[4,192,512]{2,1,0:T(8,128)(2,1)S(1)} %get-tuple-element.152), channel_id=1, source_target_pairs={{0,1},{1,0},{2,3},{3,2},{4,5},{5,4},{6,7},{7,6},{8,9},{9,8},{10,11... | collective-permute-start | bytes 2359304 | tf_op jit(solution)/shard_map/ppermute | solution.py:556
  78.8 17.9 %copy-start.11 = (f32[2,3,1536]{2,0,1:T(2,128)S(1)}, f32[2,3,1536]{2,0,1:T(2,128)}, u32[]{:S(2)}) copy-start(f32[2,3,1536]{2,0,1:T(2,128)} %param.14) | copy-start | bytes 110596
  78.8 17.9 %copy-start.14 = (s32[2]{0:T(128)S(1)}, s32[2]{0:T(128)}, u32[]{:S(2)}) copy-start(s32[2]{0:T(128)} %dil.3) | copy-start | bytes 28
  79.7 14.3 %collective-permute-start.24 = (bf16[4,48,512]{2,1,0:T(8,128)(2,1)S(1)}, bf16[4,48,512]{2,1,0:T(8,128)(2,1)S(1)}, u32[]{:S(2)}, u32[]{:S(2)}) collective-permute-start(bf16[4,48,512]{2,1,0:T(8,128)(2,1)S(1)} %get-tuple-element.154), channel_id=1, source_target_pairs={{0,128},{2,130},{128,0},{130,2},{1,129},{3,131},{129,1},{131,3},{4... | collective-permute-start | bytes 589832 | tf_op jit(solution)/shard_map/ppermute | solution.py:719
  82.8 11.2 %collective-permute-start.25 = (bf16[4,48,512]{2,1,0:T(8,128)(2,1)S(1)}, bf16[4,48,512]{2,1,0:T(8,128)(2,1)S(1)}, u32[]{:S(2)}, u32[]{:S(2)}) collective-permute-start(bf16[4,48,512]{2,1,0:T(8,128)(2,1)S(1)} %get-tuple-element.155), channel_id=1, source_target_pairs={{0,2},{2,0},{128,130},{130,128},{1,3},{3,1},{129,131},{131,129},{4... | collective-permute-start | bytes 589832 | tf_op jit(solution)/shard_map/ppermute | solution.py:719
  82.8 11.2 %collective-permute-start.26 = (bf16[4,48,512]{2,1,0:T(8,128)(2,1)S(1)}, bf16[4,48,512]{2,1,0:T(8,128)(2,1)S(1)}, u32[]{:S(2)}, u32[]{:S(2)}) collective-permute-start(bf16[4,48,512]{2,1,0:T(8,128)(2,1)S(1)} %get-tuple-element.156), channel_id=1, source_target_pairs={{0,130},{2,128},{128,2},{130,0},{1,131},{3,129},{129,3},{131,1},{4... | collective-permute-start | bytes 589832 | tf_op jit(solution)/shard_map/ppermute | solution.py:719
  83.9 8.7 %collective-permute-start.22 = (bf16[32,1536]{1,0:T(8,128)(2,1)S(1)}, bf16[32,1536]{1,0:T(8,128)(2,1)S(1)}, u32[]{:S(2)}, u32[]{:S(2)}) collective-permute-start(bf16[32,1536]{1,0:T(8,128)(2,1)S(1)} %get-tuple-element.184), channel_id=1, source_target_pairs={{0,1},{1,2},{2,3},{3,4},{4,5},{5,6},{6,7},{7,8},{8,9},{9,10},{10,1... | collective-permute-start | bytes 294920 | tf_op jit(solution)/shard_map/ppermute | solution.py:561
  85.8 8.2 %collective-permute-start.23 = (bf16[32,1536]{1,0:T(8,128)(2,1)S(1)}, bf16[32,1536]{1,0:T(8,128)(2,1)S(1)}, u32[]{:S(2)}, u32[]{:S(2)}) collective-permute-start(bf16[32,1536]{1,0:T(8,128)(2,1)S(1)} %get-tuple-element.183), channel_id=1, source_target_pairs={{1,0},{2,1},{3,2},{4,3},{5,4},{6,5},{7,6},{8,7},{9,8},{10,9},{11,1... | collective-permute-start | bytes 294920 | tf_op jit(solution)/shard_map/ppermute | solution.py:562
  94.7 16.7 %copy-start = (bf16[768,1536]{1,0:T(8,128)(2,1)S(1)}, bf16[768,1536]{1,0:T(8,128)(2,1)}, u32[]{:S(2)}) copy-start(bf16[768,1536]{1,0:T(8,128)(2,1)} %w_out.1) | copy-start | bytes 7077892
  94.7 4.9 %collective-permute-start.27 = (bf16[4,24,512]{2,1,0:T(8,128)(2,1)S(1)}, bf16[4,24,512]{2,1,0:T(8,128)(2,1)S(1)}, u32[]{:S(2)}, u32[]{:S(2)}) collective-permute-start(bf16[4,24,512]{2,1,0:T(8,128)(2,1)S(1)} %get-tuple-element.165), channel_id=1, source_target_pairs={{0,16},{16,0},{32,48},{48,32},{64,80},{80,64},{96,112},{112,96},{1... | collective-permute-start | bytes 294920 | tf_op jit(solution)/shard_map/ppermute | solution.py:725
  100.2 13.1 %collective-permute-start.28 = (f32[4,6,512]{2,1,0:T(8,128)S(1)}, f32[4,6,512]{2,1,0:T(8,128)S(1)}, u32[]{:S(2)}, u32[]{:S(2)}) collective-permute-start(f32[4,6,512]{2,1,0:T(8,128)S(1)} %get-tuple-element.174), channel_id=1, source_target_pairs={{0,64},{16,80},{32,96},{48,112},{64,0},{80,16},{96,32},{112,48},{1... | collective-permute-start | bytes 147464 | tf_op jit(solution)/shard_map/ppermute | solution.py:544
  107.3 6.7 %collective-permute-start.29 = (f32[4,6,512]{2,1,0:T(8,128)S(1)}, f32[4,6,512]{2,1,0:T(8,128)S(1)}, u32[]{:S(2)}, u32[]{:S(2)}) collective-permute-start(f32[4,6,512]{2,1,0:T(8,128)S(1)} %get-tuple-element.175), channel_id=1, source_target_pairs={{0,32},{16,48},{32,64},{48,80},{64,96},{80,112},{96,0},{112,16},{1... | collective-permute-start | bytes 147464 | tf_op jit(solution)/shard_map/ppermute | solution.py:544
  108.8 5.6 %collective-permute-start.30 = (f32[4,6,512]{2,1,0:T(8,128)S(1)}, f32[4,6,512]{2,1,0:T(8,128)S(1)}, u32[]{:S(2)}, u32[]{:S(2)}) collective-permute-start(f32[4,6,512]{2,1,0:T(8,128)S(1)} %get-tuple-element.176), channel_id=1, source_target_pairs={{0,96},{16,112},{32,0},{48,16},{64,32},{80,48},{96,64},{112,80},{1... | collective-permute-start | bytes 147464 | tf_op jit(solution)/shard_map/ppermute | solution.py:544
